TPU v7x, 32 devices: a whole 2x2x4 slice. The times are simulated.
32 devices in a mesh: section: 2 (over core), ctx: 4 (over y, x), exp: 4 (over z).
Axes of the slice: x: 2, y: 2, z: 4, core: 2. Of those that a mesh axis runs over, the one named last changes fastest.
Arguments:
- inputs: bfloat16 [2, 4, 512, 768], P(None, 'exp', 'ctx'), may hold values from -6 to 6
- cotangent: bfloat16 [2, 4, 512, 768], P(None, 'exp', 'ctx'), may hold values from -6 to 6
- segments: int32 [2, 4, 512], P(None, 'exp'), may hold values from 0 to 4, as said below
- buckets: int32 [512], replicated, may hold values from 0 to 63, as said below
- routes: int32 [2, 4, 512, 2], P(None, 'exp', 'ctx'), may hold values from 0 to 7, all different within a row; in each aligned block of 128 rows (0 to 127, 128 to 255, ..., all dimensions but the last counted through in order) at most 40 rows name the same one
- gain_attn: float32 [2, 768], P('section', ('ctx', 'exp')), may hold values from 0.5 to 1.5
- w_query: float32 [2, 768, 768], P('section', ('ctx', 'exp')), may hold values from -0.21875 to 0.21875
- w_key: float32 [2, 768, 768], P('section', ('ctx', 'exp')), may hold values from -0.21875 to 0.21875
- w_value: float32 [2, 768, 768], P('section', ('ctx', 'exp')), may hold values from -0.21875 to 0.21875
- w_out: float32 [2, 768, 768], P('section', ('ctx', 'exp')), may hold values from -0.625 to 0.625
- rel_bias: float32 [2, 64, 12], P('section', ('ctx', 'exp')), may hold values from -4 to 4
- gain_moe: float32 [2, 768], P('section', ('ctx', 'exp')), may hold values from 0.5 to 1.5
- w_router: float32 [2, 768, 8], P('section', ('ctx', 'exp')), may hold values from -0.109375 to 0.109375
- w_in: float32 [2, 8, 768, 3072], P('section', 'exp', 'ctx'), may hold values from -0.21875 to 0.21875
- w_back: float32 [2, 8, 3072, 768], P('section', 'exp', 'ctx'), may hold values from -0.109375 to 0.109375
Outputs:
- activations: float32 [2, 2, 4, 512, 768], P('section', None, 'exp', 'ctx')
- grads_in: float32 [2, 2, 4, 512, 768], P('section', None, 'exp', 'ctx')
- grad_gain_attn: float32 [2, 768], P('section', ('ctx', 'exp'))
- grad_query: float32 [2, 768, 768], P('section', ('ctx', 'exp'))
- grad_key: float32 [2, 768, 768], P('section', ('ctx', 'exp'))
- grad_value: float32 [2, 768, 768], P('section', ('ctx', 'exp'))
- grad_outproj: float32 [2, 768, 768], P('section', ('ctx', 'exp'))
- grad_rel_bias: float32 [2, 64, 12], P('section', ('ctx', 'exp'))
- grad_gain_moe: float32 [2, 768], P('section', ('ctx', 'exp'))
- grad_router: float32 [2, 768, 8], P('section', ('ctx', 'exp'))
- grad_w_in: float32 [2, 8, 768, 3072], P('section', 'exp', 'ctx')
- grad_w_back: float32 [2, 8, 3072, 768], P('section', 'exp', 'ctx')
Inputs may be any that keep to these rules, and one draw needn't show every extreme that they name: `segments`: each sequence is a prompt (segment 0) of 128 to 448 positions followed by 4 continuations of near-equal length in increasing order; the last position is in segment 4; in each micro-batch one sequence has a prompt of exactly 448 positions. `buckets`: never falling in the distance; 0 at distance 0 and 63 at the largest distance. `routes`: each position names two different experts; among the 128 positions of one device in one micro-batch, at most 40 name the same expert, a bound that some block reaches.
All inputs are finite; a program needn't handle non-finite values.
Results may differ from a plain program's by a relative error of at most 0.035.
Values may be sent and summed in bfloat16 or wider, within the bound.
No kernel may reach another device: no remote copies, remote signals or barrier semaphores. Data moves between devices by JAX's collectives and lax.ppermute only.
A program may use at most 320 MiB of HBM per device.

v0:
```python
import jax
import jax.numpy as jnp
from jax import lax
from jax.sharding import PartitionSpec as P

EPS = 1e-06
NEG = -1e30


def passed_along(block, axis, distance):
    devices = range(lax.axis_size(axis))
    route = [(i - distance, i) for i in devices if i - distance in devices]
    return lax.ppermute(block, axis, route)


def bias_terms(query_pos, key_pos, query_seg, key_seg, buckets, rel_low):
    distance = query_pos[:, None] - key_pos[None, :]
    allowed = (distance >= 0) & ((key_seg[None, :] == 0) | (key_seg[None, :] == query_seg[:, None]))
    bucket_index = jnp.take(buckets, jnp.clip(distance, 0, buckets.shape[0] - 1))
    bucket_ids = jnp.arange(rel_low.shape[0], dtype=jnp.int32)
    one_hot = (bucket_index[..., None] == bucket_ids).astype(jnp.bfloat16)
    bias_grid = jnp.einsum("qkb,bh->hqk", one_hot, rel_low, preferred_element_type=jnp.float32)
    return (bias_grid, allowed, one_hot)


def norm_back(grad_out, value, inverse, gain_row):
    scaled = grad_out * gain_row
    return inverse * (
        scaled - value * inverse * inverse * jnp.mean(scaled * value, axis=-1, keepdims=True)
    )


def body(
    inputs,
    cotangent,
    segments,
    buckets,
    routes,
    gain_attn,
    w_query,
    w_key,
    w_value,
    w_out,
    rel_bias,
    gain_moe,
    w_router,
    w_in,
    w_back,
):
    low_type = jnp.bfloat16
    wide_type = jnp.float32
    section_index = lax.axis_index("section")
    is_first = section_index == 0
    ctx_rank = lax.axis_index("ctx")
    micro_count = inputs.shape[0]
    tok_rows = inputs.shape[2]
    model_width = inputs.shape[3]
    head_count = rel_bias.shape[2]
    head_dim = model_width // head_count
    exp_count = lax.axis_size("exp")
    local_exp = w_in.shape[1]
    experts = exp_count * local_exp
    capacity = 2 * tok_rows // experts * 5 // 4
    slot_count = experts * capacity
    score_scale = head_dim ** (-0.5)
    dense_low = (
        lax.all_gather(gain_attn[0].astype(low_type), ("ctx", "exp"), axis=0, tiled=True),
        lax.all_gather(w_query[0].astype(low_type), ("ctx", "exp"), axis=0, tiled=True),
        lax.all_gather(w_key[0].astype(low_type), ("ctx", "exp"), axis=0, tiled=True),
        lax.all_gather(w_value[0].astype(low_type), ("ctx", "exp"), axis=0, tiled=True),
        lax.all_gather(w_out[0].astype(low_type), ("ctx", "exp"), axis=0, tiled=True),
        lax.all_gather(rel_bias[0].astype(low_type), ("ctx", "exp"), axis=0, tiled=True),
        lax.all_gather(gain_moe[0].astype(low_type), ("ctx", "exp"), axis=0, tiled=True),
        lax.all_gather(w_router[0].astype(low_type), ("ctx", "exp"), axis=0, tiled=True),
    )
    gain_a_full = dense_low[0].astype(wide_type)
    query_full, key_full, value_full, outproj_full = (
        dense_low[1],
        dense_low[2],
        dense_low[3],
        dense_low[4],
    )
    rel_low = dense_low[5]
    gain_m_full = dense_low[6].astype(wide_type)
    router_full = dense_low[7]
    w_first, w_second = (
        lax.all_gather(w_in[0].astype(low_type), "ctx", axis=1, tiled=True),
        lax.all_gather(w_back[0].astype(low_type), "ctx", axis=1, tiled=True),
    )
    query_pos = ctx_rank * tok_rows + jnp.arange(tok_rows, dtype=jnp.int32)
    expert_ids = jnp.arange(experts, dtype=jnp.int32)
    slot_ids = jnp.arange(slot_count, dtype=jnp.int32)

    def routing(route_rows):
        flat_routes = route_rows.reshape(-1)
        member = (flat_routes[:, None] == expert_ids[None, :]).astype(jnp.int32)
        slot_rank = jnp.sum((jnp.cumsum(member, axis=0) - member) * member, axis=1)
        slot_dest = flat_routes * capacity + slot_rank
        by_slot = (slot_ids[:, None] == slot_dest[None, :]).astype(low_type)
        to_token = jnp.sum(by_slot.reshape(slot_count, tok_rows, 2), axis=2)
        return (by_slot, to_token)

    zero_rows = jnp.zeros((tok_rows, model_width), low_type)
    carried = zero_rows
    outputs = []
    saved_steps = []
    for step_index in range(micro_count + 1):
        position = jnp.clip(step_index - section_index, 0, micro_count - 1)
        if step_index > 0:
            arrived = passed_along(carried, "section", 1)
        else:
            arrived = zero_rows
        from_input = lax.dynamic_index_in_dim(inputs, position, 0, keepdims=False)[0]
        layer_input = jnp.where(is_first, from_input, arrived).astype(wide_type)
        seg_row = lax.dynamic_index_in_dim(segments, position, 0, keepdims=False)[0]
        route_rows = lax.dynamic_index_in_dim(routes, position, 0, keepdims=False)[0]
        forward_inv_attn = lax.rsqrt(
            jnp.mean(layer_input * layer_input, axis=-1, keepdims=True) + EPS
        )
        forward_normed_attn = (layer_input * forward_inv_attn * gain_a_full).astype(low_type)
        forward_queries = jnp.dot(
            forward_normed_attn, query_full, preferred_element_type=wide_type
        ).astype(low_type)
        forward_keys_local = jnp.dot(
            forward_normed_attn, key_full, preferred_element_type=wide_type
        ).astype(low_type)
        forward_values_local = jnp.dot(
            forward_normed_attn, value_full, preferred_element_type=wide_type
        ).astype(low_type)
        forward_query_seg = lax.dynamic_slice_in_dim(seg_row, ctx_rank * tok_rows, tok_rows)
        forward_query_three = forward_queries.reshape(tok_rows, head_count, head_dim)
        forward_whole_keys = (forward_keys_local, forward_values_local)
        running_max = jnp.full((head_count, tok_rows), NEG, wide_type)
        key_piece = lax.all_gather(forward_keys_local, "ctx", axis=0, tiled=True)
        value_piece = lax.all_gather(forward_values_local, "ctx", axis=0, tiled=True)
        row_count = key_piece.shape[0]
        key_pos = jnp.arange(row_count, dtype=jnp.int32)
        bias_grid, allowed, one_hot = bias_terms(
            query_pos, key_pos, forward_query_seg, seg_row, buckets, rel_low
        )
        scores = (
            jnp.einsum(
                "qhd,khd->hqk",
                forward_query_three,
                key_piece.reshape(row_count, head_count, head_dim),
                preferred_element_type=wide_type,
            )
            * score_scale
            + bias_grid
        )
        scores = jnp.where(allowed[None], scores, NEG)
        newest_max = jnp.maximum(running_max, jnp.max(scores, axis=-1))
        weights = jnp.where(allowed[None], jnp.exp(scores - newest_max[..., None]), 0.0)
        running_total = jnp.sum(weights, axis=-1)
        running_out = jnp.einsum(
            "hqk,khd->hqd",
            weights.astype(low_type),
            value_piece.reshape(row_count, head_count, head_dim),
            preferred_element_type=wide_type,
        )
        running_max, running_total, running_out = (newest_max, running_total, running_out)
        forward_log_total = running_max + jnp.log(running_total)
        forward_attn_wide = jnp.transpose(
            running_out / running_total[..., None], (1, 0, 2)
        ).reshape(tok_rows, model_width)
        forward_attn_low = forward_attn_wide.astype(low_type)
        forward_residual = layer_input + jnp.dot(
            forward_attn_low, outproj_full, preferred_element_type=wide_type
        )
        forward_inv_moe = lax.rsqrt(
            jnp.mean(forward_residual * forward_residual, axis=-1, keepdims=True) + EPS
        )
        forward_normed_moe = (forward_residual * forward_inv_moe * gain_m_full).astype(low_type)
        logits = jnp.dot(forward_normed_moe, router_full, preferred_element_type=wide_type)
        forward_gate_probs = jax.nn.softmax(
            jnp.take_along_axis(logits, route_rows, axis=1), axis=-1
        )
        forward_by_slot, forward_to_token = routing(route_rows)
        outgoing = jnp.dot(
            forward_to_token, forward_normed_moe, preferred_element_type=wide_type
        ).astype(low_type)
        forward_received = lax.all_to_all(
            outgoing.reshape(exp_count, local_exp, capacity, model_width),
            "exp",
            split_axis=0,
            concat_axis=0,
            tiled=True,
        )
        forward_hidden_pre = jnp.einsum(
            "secd,edf->secf", forward_received, w_first, preferred_element_type=wide_type
        )
        forward_activated = jax.nn.gelu(forward_hidden_pre).astype(low_type)
        produced = jnp.einsum(
            "secf,efd->secd", forward_activated, w_second, preferred_element_type=wide_type
        ).astype(low_type)
        returned = lax.all_to_all(produced, "exp", split_axis=0, concat_axis=0, tiled=True).reshape(
            slot_count, model_width
        )
        forward_picked = jnp.dot(
            forward_by_slot.T, returned, preferred_element_type=wide_type
        ).reshape(tok_rows, 2, model_width)
        result = forward_residual + jnp.sum(forward_gate_probs[..., None] * forward_picked, axis=1)
        forward_saved_state = (
            layer_input,
            forward_inv_attn,
            forward_normed_attn,
            forward_queries,
            forward_keys_local,
            forward_values_local,
            forward_whole_keys,
            forward_log_total,
            forward_attn_wide,
            forward_attn_low,
            forward_residual,
            forward_inv_moe,
            forward_normed_moe,
            forward_gate_probs,
            forward_picked,
            forward_received,
            forward_hidden_pre,
        )
        result, saved_state = (result, forward_saved_state)
        carried = result.astype(low_type)
        outputs.append(result)
        saved_steps.append(saved_state)
    activations = jnp.stack(
        [
            jnp.where(is_first, outputs[micro_at], outputs[micro_at + 1])
            for micro_at in range(micro_count)
        ]
    )

    def select_kept(early_value, later_value):
        return jnp.where(is_first, early_value, later_value)

    dense_totals = (
        jnp.zeros((model_width,), wide_type),
        jnp.zeros((model_width, model_width), wide_type),
        jnp.zeros((model_width, model_width), wide_type),
        jnp.zeros((model_width, model_width), wide_type),
        jnp.zeros((model_width, model_width), wide_type),
        jnp.zeros(rel_low.shape, wide_type),
        jnp.zeros((model_width,), wide_type),
        jnp.zeros((model_width, experts), wide_type),
    )
    expert_totals = (jnp.zeros(w_first.shape, wide_type), jnp.zeros(w_second.shape, wide_type))
    grad_carried = zero_rows
    grad_steps = []
    for step_index in range(micro_count + 1):
        micro_index = step_index - 1 + section_index
        is_valid = (micro_index >= 0) & (micro_index < micro_count)
        position = jnp.clip(micro_index, 0, micro_count - 1)
        if step_index > 0:
            arrived = passed_along(grad_carried, "section", -1)
        else:
            arrived = zero_rows
        from_cotangent = lax.dynamic_index_in_dim(cotangent, position, 0, keepdims=False)[0]
        grad_out = jnp.where(is_first, arrived, from_cotangent).astype(wide_type)
        saved_state = jax.tree.map(
            select_kept,
            saved_steps[max(step_index - 1, 0)],
            saved_steps[min(step_index + 1, micro_count)],
        )
        seg_row = lax.dynamic_index_in_dim(segments, position, 0, keepdims=False)[0]
        route_rows = lax.dynamic_index_in_dim(routes, position, 0, keepdims=False)[0]
        (
            backward_layer_input,
            inv_attn,
            normed_attn,
            queries,
            keys_local,
            values_local,
            whole_keys,
            log_total,
            attn_wide,
            attn_low,
            residual,
            inv_moe,
            normed_moe,
            gate_probs,
            picked,
            received,
            hidden_pre,
        ) = saved_state
        backward_by_slot, backward_to_token = routing(route_rows)
        grad_gates = jnp.sum(grad_out[:, None, :] * picked, axis=-1)
        grad_picked = (
            (gate_probs[..., None] * grad_out[:, None, :])
            .astype(low_type)
            .reshape(2 * tok_rows, model_width)
        )
        slot_grads = jnp.dot(
            backward_by_slot, grad_picked, preferred_element_type=wide_type
        ).astype(low_type)
        grad_produced = lax.all_to_all(
            slot_grads.reshape(exp_count, local_exp, capacity, model_width),
            "exp",
            split_axis=0,
            concat_axis=0,
            tiled=True,
        )
        grad_activated = jnp.einsum(
            "secd,efd->secf", grad_produced, w_second, preferred_element_type=wide_type
        )
        activated, gelu_back = jax.vjp(jax.nn.gelu, hidden_pre)
        grad_hidden = gelu_back(grad_activated)[0].astype(low_type)
        grad_second = jnp.einsum(
            "secf,secd->efd",
            activated.astype(low_type),
            grad_produced,
            preferred_element_type=wide_type,
        )
        grad_first = jnp.einsum(
            "secd,secf->edf", received, grad_hidden, preferred_element_type=wide_type
        )
        grad_received = jnp.einsum(
            "secf,edf->secd", grad_hidden, w_first, preferred_element_type=wide_type
        ).astype(low_type)
        grad_sent = lax.all_to_all(
            grad_received, "exp", split_axis=0, concat_axis=0, tiled=True
        ).reshape(slot_count, model_width)
        grad_normed_moe = jnp.dot(backward_to_token.T, grad_sent, preferred_element_type=wide_type)
        grad_chosen = gate_probs * (
            grad_gates - jnp.sum(gate_probs * grad_gates, axis=-1, keepdims=True)
        )
        backward_member = (route_rows[..., None] == expert_ids).astype(wide_type)
        grad_logits = jnp.sum(backward_member * grad_chosen[..., None], axis=1).astype(low_type)
        grad_normed_moe = grad_normed_moe + jnp.dot(
            grad_logits, router_full.T, preferred_element_type=wide_type
        )
        grad_router_term = jnp.dot(normed_moe.T, grad_logits, preferred_element_type=wide_type)
        grad_gain_late = jnp.sum(grad_normed_moe * residual * inv_moe, axis=0)
        grad_residual = grad_out + norm_back(grad_normed_moe, residual, inv_moe, gain_m_full)
        grad_branch = grad_residual.astype(low_type)
        grad_outproj_term = jnp.dot(attn_low.T, grad_branch, preferred_element_type=wide_type)
        grad_attn = jnp.dot(grad_branch, outproj_full.T, preferred_element_type=wide_type).astype(
            low_type
        )
        delta = jnp.transpose(
            jnp.sum(
                (grad_attn.astype(wide_type) * attn_wide).reshape(tok_rows, head_count, head_dim),
                axis=-1,
            )
        )
        grad_three = grad_attn.reshape(tok_rows, head_count, head_dim)
        query_three = queries.reshape(tok_rows, head_count, head_dim)
        query_seg = lax.dynamic_slice_in_dim(seg_row, ctx_rank * tok_rows, tok_rows)
        make_key_piece = lax.all_gather(keys_local, "ctx", axis=0, tiled=True)
        make_value_piece = lax.all_gather(values_local, "ctx", axis=0, tiled=True)
        make_row_count = make_key_piece.shape[0]
        make_key_three = make_key_piece.reshape(make_row_count, head_count, head_dim)
        make_value_three = make_value_piece.reshape(make_row_count, head_count, head_dim)
        make_key_pos = jnp.arange(make_row_count, dtype=jnp.int32)
        pair_bias_grid, pair_allowed, pair_one_hot = bias_terms(
            query_pos, make_key_pos, query_seg, seg_row, buckets, rel_low
        )
        pair_scores = (
            jnp.einsum(
                "qhd,khd->hqk", query_three, make_key_three, preferred_element_type=wide_type
            )
            * score_scale
            + pair_bias_grid
        )
        probs = jnp.where(pair_allowed[None], jnp.exp(pair_scores - log_total[..., None]), 0.0)
        grad_probs = jnp.einsum(
            "qhd,khd->hqk", grad_three, make_value_three, preferred_element_type=wide_type
        )
        grad_scores = (probs * (grad_probs - delta[..., None])).astype(low_type)
        grad_query_acc = (
            jnp.einsum(
                "hqk,khd->hqd", grad_scores, make_key_three, preferred_element_type=wide_type
            )
            * score_scale
        )
        grad_table = jnp.einsum(
            "qkb,hqk->bh", pair_one_hot, grad_scores, preferred_element_type=wide_type
        )
        grad_keys = (
            jnp.einsum("hqk,qhd->khd", grad_scores, query_three, preferred_element_type=wide_type)
            * score_scale
        )
        grad_values = jnp.einsum(
            "hqk,qhd->khd", probs.astype(low_type), grad_three, preferred_element_type=wide_type
        )
        grad_keys_all = grad_keys.reshape(make_row_count, model_width)
        grad_values_all = grad_values.reshape(make_row_count, model_width)
        back_result = (grad_query_acc, grad_table, grad_keys_all, grad_values_all)
        grad_query_acc = back_result[0]
        grad_table = back_result[1]
        grad_keys_mine = lax.psum_scatter(
            back_result[2].astype(jnp.bfloat16), "ctx", scatter_dimension=0, tiled=True
        ).astype(jnp.float32)
        grad_values_mine = lax.psum_scatter(
            back_result[3].astype(jnp.bfloat16), "ctx", scatter_dimension=0, tiled=True
        ).astype(jnp.float32)
        grad_keys_low = grad_keys_mine.astype(low_type)
        grad_values_low = grad_values_mine.astype(low_type)
        grad_query_low = (
            jnp.transpose(grad_query_acc, (1, 0, 2)).reshape(tok_rows, model_width).astype(low_type)
        )
        grad_normed_attn = (
            jnp.dot(grad_query_low, query_full.T, preferred_element_type=wide_type)
            + jnp.dot(grad_keys_low, key_full.T, preferred_element_type=wide_type)
            + jnp.dot(grad_values_low, value_full.T, preferred_element_type=wide_type)
        )
        grad_query_term = jnp.dot(normed_attn.T, grad_query_low, preferred_element_type=wide_type)
        grad_key_term = jnp.dot(normed_attn.T, grad_keys_low, preferred_element_type=wide_type)
        grad_value_term = jnp.dot(normed_attn.T, grad_values_low, preferred_element_type=wide_type)
        grad_gain_early = jnp.sum(grad_normed_attn * backward_layer_input * inv_attn, axis=0)
        grad_input = grad_residual + norm_back(
            grad_normed_attn, backward_layer_input, inv_attn, gain_a_full
        )
        dense_terms = (
            grad_gain_early,
            grad_query_term,
            grad_key_term,
            grad_value_term,
            grad_outproj_term,
            grad_table,
            grad_gain_late,
            grad_router_term,
        )
        grad_input, dense_terms, expert_terms = (grad_input, dense_terms, (grad_first, grad_second))
        grad_carried = grad_input.astype(low_type)
        grad_steps.append(grad_input)
        dense_totals = tuple(
            (
                jnp.where(is_valid, running + addend, running)
                for running, addend in zip(dense_totals, dense_terms)
            )
        )
        expert_totals = tuple(
            (
                jnp.where(is_valid, running + addend, running)
                for running, addend in zip(expert_totals, expert_terms)
            )
        )
    grads_in = jnp.stack(
        [
            jnp.where(is_first, grad_steps[micro_at + 1], grad_steps[micro_at])
            for micro_at in range(micro_count)
        ]
    )
    dense_sums = (
        lax.psum_scatter(dense_totals[0], ("ctx", "exp"), scatter_dimension=0, tiled=True),
        lax.psum_scatter(dense_totals[1], ("ctx", "exp"), scatter_dimension=0, tiled=True),
        lax.psum_scatter(dense_totals[2], ("ctx", "exp"), scatter_dimension=0, tiled=True),
        lax.psum_scatter(dense_totals[3], ("ctx", "exp"), scatter_dimension=0, tiled=True),
        lax.psum_scatter(dense_totals[4], ("ctx", "exp"), scatter_dimension=0, tiled=True),
        lax.psum_scatter(dense_totals[5], ("ctx", "exp"), scatter_dimension=0, tiled=True),
        lax.psum_scatter(dense_totals[6], ("ctx", "exp"), scatter_dimension=0, tiled=True),
        lax.psum_scatter(dense_totals[7], ("ctx", "exp"), scatter_dimension=0, tiled=True),
    )
    expert_sums = (
        lax.psum_scatter(
            expert_totals[0].astype(jnp.bfloat16), "ctx", scatter_dimension=1, tiled=True
        ).astype(jnp.float32),
        lax.psum_scatter(
            expert_totals[1].astype(jnp.bfloat16), "ctx", scatter_dimension=1, tiled=True
        ).astype(jnp.float32),
    )
    return (
        activations[None, :, None],
        grads_in[None, :, None],
        dense_sums[0][None],
        dense_sums[1][None],
        dense_sums[2][None],
        dense_sums[3][None],
        dense_sums[4][None],
        dense_sums[5][None],
        dense_sums[6][None],
        dense_sums[7][None],
        expert_sums[0][None],
        expert_sums[1][None],
    )


def solution(mesh):
    in_specs = (
        P(None, "exp", "ctx", None),
        P(None, "exp", "ctx", None),
        P(None, "exp", None),
        P(),
        P(None, "exp", "ctx", None),
        P("section", ("ctx", "exp")),
        P("section", ("ctx", "exp"), None),
        P("section", ("ctx", "exp"), None),
        P("section", ("ctx", "exp"), None),
        P("section", ("ctx", "exp"), None),
        P("section", ("ctx", "exp"), None),
        P("section", ("ctx", "exp")),
        P("section", ("ctx", "exp"), None),
        P("section", "exp", "ctx", None),
        P("section", "exp", "ctx", None),
    )
    out_specs = (
        P("section", None, "exp", "ctx", None),
        P("section", None, "exp", "ctx", None),
        P("section", ("ctx", "exp")),
        P("section", ("ctx", "exp"), None),
        P("section", ("ctx", "exp"), None),
        P("section", ("ctx", "exp"), None),
        P("section", ("ctx", "exp"), None),
        P("section", ("ctx", "exp"), None),
        P("section", ("ctx", "exp")),
        P("section", ("ctx", "exp"), None),
        P("section", "exp", "ctx", None),
        P("section", "exp", "ctx", None),
    )
    return jax.shard_map(body, mesh=mesh, in_specs=in_specs, out_specs=out_specs, check_vma=False)
```

profile of v0, /device:TPU:0, one launch (start us, length us, event | category | flops | bytes accessed | tf_op | source)
XLA Modules:
  0.0 2167.2 jit_solution(12180574242787874097)
XLA Ops:
  28.1 47.9 %all-gather.7 = bf16[1,768,8]{2,0,1:T(2,128)(2,1)S(1)} all-gather(bf16[1,48,8]{2,0,1:T(2,128)(2,1)S(1)} %copy.498), channel_id=9, replica_groups=mesh['section'=2,'ctx'=4,'exp'=4] {'ctx','exp'}, dimensions={1}, use_global_device_ids=true | all-gather | bytes 13056 | tf_op jit(solution)/shard_map/all_gather | solution.py:74
  76.5 408.2 %gather_fusion = s32[65536]{0:T(1024)S(1)} fusion(s32[512]{0:T(512)S(1)} %copy-done, s32[65536]{0:T(1024)S(1)} %broadcast_clamp_fusion), kind=kCustom, calls=%fused_computation.clone | custom fusion | bytes 786432 | tf_op jit(solution)/shard_map/jit(_take)/gather | solution.py:19
  485.2 35.7 %all-gather.3 = bf16[1,64,12]{2,0,1:T(2,128)(2,1)S(1)} all-gather(bf16[1,4,12]{2,0,1:T(2,128)(2,1)S(1)} %convert_element_type.525), channel_id=5, replica_groups=mesh['section'=2,'ctx'=4,'exp'=4] {'ctx','exp'}, dimensions={1}, use_global_device_ids=true | all-gather | bytes 1632 | tf_op jit(solution)/shard_map/all_gather | solution.py:72
  530.8 39.0 %all-reduce.6 = (bf16[768]{0:T(1024)(128)(2,1)S(1)}, bf16[768]{0:T(1024)(128)(2,1)S(1)}) all-reduce(bf16[768]{0:T(1024)(128)(2,1)S(1)} %dynamic-update-slice, bf16[768]{0:T(1024)(128)(2,1)S(1)} %dynamic-update-slice.1), channel_id=2, replica_groups=mesh['section'=2,'ctx'=4,'exp'=4] {'ctx','exp'}, use_global_device_ids=true, to_apply=%add | all-reduce | flops 1536 | bytes 6144
  581.4 10.9 all_gather.69
  597.0 11.8 all_gather.72
  626.6 12.3 all-to-all-done
  639.0 7.5 fusion.34
  646.5 7.1 fusion.219
  661.3 7.2 all-to-all-done.1
  681.3 12.8 all_gather.78
  701.2 11.5 all_gather.79
  739.6 5.6 fusion.37
  745.2 7.4 fusion.214
  760.4 8.2 all-to-all-done.3
  780.9 8.8 all-to-all-done.6
  789.6 9.2 fusion.58
  798.8 7.6 fusion.230
  813.8 7.9 all-to-all-done.7
  836.8 12.7 all_gather.80
  857.4 11.5 all_gather.81
  882.4 12.8 all_gather.82
  906.9 11.8 all_gather.83
  962.0 5.6 fusion.40
  967.5 7.6 fusion.209
  1016.9 13.0 all_gather.84
  1032.2 9.2 fusion.65
  1041.4 7.6 fusion.227
  1060.1 11.8 all_gather.85
  1125.3 26.1 %reduce-scatter.47.cloned.1.call-done = bf16[128,768]{1,0:T(8,128)(2,1)} async-done(((bf16[512,768]{1,0:T(8,128)(2,1)}), bf16[128,768]{1,0:T(8,128)(2,1)}) %reduce-scatter.47.cloned.1.call-update) | async-done | bytes 196624
  1181.9 12.8 all_gather.86
  1196.9 9.2 fusion.72
  1206.1 7.6 fusion.224
  1225.5 11.5 all_gather.87
  1251.8 11.7 fusion.121
  1268.3 11.5 fusion.122
  1281.1 19.2 fusion.1
  1302.0 9.1 fusion.129
  1311.1 9.1 fusion.127
  1320.2 18.1 fusion
  1384.1 48.8 %reduce-scatter.53.cloned.1.call-done = f32[48,8]{1,0:T(8,128)} async-done(((f32[768,8]{1,0:T(8,128)}), f32[48,8]{1,0:T(8,128)}) %reduce-scatter.53.cloned.1.call-update) | async-done | bytes 1552
  1445.2 76.7 %all-reduce.5 = (f32[768]{0:T(1024)S(1)}, f32[64,12]{0,1:T(8,128)S(1)}, f32[768]{0:T(1024)S(1)}) all-reduce(f32[768]{0:T(1024)S(1)} %add_select_fusion.14, f32[64,12]{0,1:T(8,128)} %fusion.335, f32[768]{0:T(1024)S(1)} %copy-done.149), channel_id=18, replica_groups=mesh['section'=2,'ctx'=4,'exp'=4] {'ctx','exp'}, use_global_device_ids=true, to_apply=%region_72.75.clone | all-reduce | flops 2304 | bytes 18432
  1524.9 6.4 reduce-scatter.39.cloned.1.call-done
  1535.6 94.0 %reduce-scatter.37.cloned.1.call-done = bf16[2,192,3072]{2,1,0:T(8,128)(2,1)} async-done(((bf16[2,768,3072]{2,1,0:T(8,128)(2,1)}), bf16[2,192,3072]{2,1,0:T(8,128)(2,1)}) %reduce-scatter.37.cloned.1.call-update) | async-done | bytes 2359312 | tf_op jit(solution)/shard_map/reduce_scatter | solution.py:455
  1634.0 129.4 %reduce-scatter.29.cloned.1.call-done = f32[48,768]{1,0:T(8,128)} async-done(((f32[768,768]{1,0:T(8,128)}), f32[48,768]{1,0:T(8,128)}) %reduce-scatter.29.cloned.1.call-update) | async-done | bytes 147472 | tf_op jit(solution)/shard_map/reduce_scatter | solution.py:446
  1763.3 132.0 %reduce-scatter.35.cloned.1.call-done = f32[48,768]{1,0:T(8,128)} async-done(((f32[768,768]{1,0:T(8,128)}), f32[48,768]{1,0:T(8,128)}) %reduce-scatter.35.cloned.1.call-update) | async-done | bytes 147472 | tf_op jit(solution)/shard_map/reduce_scatter | solution.py:449
  1895.3 132.8 %reduce-scatter.31.cloned.1.call-done = f32[48,768]{1,0:T(8,128)} async-done(((f32[768,768]{1,0:T(8,128)}), f32[48,768]{1,0:T(8,128)}) %reduce-scatter.31.cloned.1.call-update) | async-done | bytes 147472 | tf_op jit(solution)/shard_map/reduce_scatter | solution.py:447
  2028.2 132.1 %reduce-scatter.33.cloned.1.call-done = f32[48,768]{1,0:T(8,128)} async-done(((f32[768,768]{1,0:T(8,128)}), f32[48,768]{1,0:T(8,128)}) %reduce-scatter.33.cloned.1.call-update) | async-done | bytes 147472 | tf_op jit(solution)/shard_map/reduce_scatter | solution.py:448
  (824 shorter events, 480.3 us)
Async XLA Ops:
  7.2 569.1 %all-gather.17.cloned.1.call-start = ((), (), s32[]{:S(2)}) async-start(), calls=%async_computation.31 | async-start | bytes 1253376 | tf_op jit(solution)/shard_map/all_gather | solution.py:68
  8.8 570.1 %all-gather.19.cloned.1.call-start = ((), (), s32[]{:S(2)}) async-start(), calls=%async_computation.32 | async-start | bytes 1253376 | tf_op jit(solution)/shard_map/all_gather | solution.py:69
  10.4 584.1 %all-gather.21.cloned.1.call-start = ((), (), s32[]{:S(2)}) async-start(), calls=%async_computation.33 | async-start | bytes 1253376 | tf_op jit(solution)/shard_map/all_gather | solution.py:70
  12.1 603.8 %all-gather.23.cloned.1.call-start = ((), (), s32[]{:S(2)}) async-start(), calls=%async_computation.34 | async-start | bytes 1253376 | tf_op jit(solution)/shard_map/all_gather | solution.py:71
  13.7 625.2 %all-gather.25.cloned.1.call-start = ((), (), s32[]{:S(2)}) async-start(), calls=%async_computation.35 | async-start | bytes 11796480 | tf_op jit(solution)/shard_map/all_gather | solution.py:87
  17.9 628.5 %all-gather.27.cloned.1.call-start = ((), (), s32[]{:S(2)}) async-start(), calls=%async_computation.36 | async-start | bytes 11796480 | tf_op jit(solution)/shard_map/all_gather | solution.py:88
  24.9 600.7 %copy-start.157 = (s32[256]{0:T(256)}, s32[256]{0:T(256)S(1)}, u32[]{:S(2)}) copy-start(s32[256]{0:T(256)S(1)} %reshape_squeeze.19) | copy-start | bytes 3076
  76.2 736.6 %copy-start.104 = (bf16[1,768,8]{1,2,0:T(8,128)(2,1)}, bf16[1,768,8]{1,2,0:T(8,128)(2,1)S(1)}, u32[]{:S(2)}) copy-start(bf16[1,768,8]{1,2,0:T(8,128)(2,1)S(1)} %copy.499) | copy-start | bytes 36868
  76.2 408.6 %copy-start.172 = (s32[128]{0:T(128)}, s32[128]{0:T(128)S(1)}, u32[]{:S(2)}) copy-start(s32[128]{0:T(128)S(1)} %iota_add_fusion) | copy-start | bytes 1540
  76.5 408.6 %copy-start.194 = (f32[1,4,12]{2,1,0:T(4,128)S(1)}, f32[1,4,12]{2,1,0:T(4,128)}, u32[]{:S(2)}) copy-start(f32[1,4,12]{2,1,0:T(4,128)} %param.29) | copy-start | bytes 580
  569.8 253.5 %copy-start.107 = (f32[768]{0:T(1024)}, f32[768]{0:T(1024)S(1)}, u32[]{:S(2)}) copy-start(f32[768]{0:T(1024)S(1)} %convert_element_type.671) | copy-start | bytes 9220
  620.6 18.3 all-to-all-start
  654.3 14.1 all-to-all-start.1
  661.2 111.0 %copy-start.127 = (f32[128,2]{0,1:T(2,128)}, f32[128,2]{0,1:T(2,128)S(1)}, u32[]{:S(2)}) copy-start(f32[128,2]{0,1:T(2,128)S(1)} %get-tuple-element.138) | copy-start | bytes 3076
  661.2 111.0 %copy-start.152 = (f32[128]{0:T(128)}, f32[128]{0:T(128)S(1)}, u32[]{:S(2)}) copy-start(f32[128]{0:T(128)S(1)} %get-tuple-element.137) | copy-start | bytes 1540
  661.2 110.9 %copy-start.171 = (f32[128]{0:T(128)}, f32[128]{0:T(128)S(1)}, u32[]{:S(2)}) copy-start(f32[128]{0:T(128)S(1)} %fusion.462) | copy-start | bytes 1540
  672.7 2.3 collective-permute-start
  721.3 102.0 %copy-start.174 = (f32[128]{0:T(128)}, f32[128]{0:T(128)S(1)}, u32[]{:S(2)}) copy-start(f32[128]{0:T(128)S(1)} %get-tuple-element.196) | copy-start | bytes 1540
  723.9 15.7 all-to-all-start.2
  753.4 15.2 all-to-all-start.3
  774.7 14.9 all-to-all-start.6
  807.2 14.5 all-to-all-start.7
  811.4 169.6 %reduce-scatter.41.cloned.1.call-start = ((), (), s32[]{:S(2)}) async-start(), calls=%async_computation.37 | async-start | bytes 983040
  826.5 2.4 collective-permute-start.1
  947.1 14.9 all-to-all-start.4
  951.2 34.2 %reduce-scatter.43.cloned.1.call-start = ((), (), s32[]{:S(2)}) async-start(), calls=%async_computation.38 | async-start | bytes 983040
  976.0 22.2 %all-to-all-start.5 = ((bf16[4,2,40,768]{3,2,1,0:T(8,128)(2,1)}), bf16[4,2,40,768]{3,2,1,0:T(8,128)(2,1)}, u32[]{:S(2)}, u32[]{:S(2)}) async-start(bf16[4,2,40,768]{3,2,1,0:T(8,128)(2,1)} %copy.528), calls=%async_computation.5 | async-start | bytes 983040 | tf_op jit(solution)/shard_map/all_to_all | solution.py:196
  990.1 3.5 collective-permute-start.2
  1007.5 24.7 %all-to-all-start.8 = ((bf16[4,2,40,768]{3,2,1,0:T(8,128)(2,1)}), bf16[4,2,40,768]{3,2,1,0:T(8,128)(2,1)}, u32[]{:S(2)}, u32[]{:S(2)}) async-start(bf16[4,2,40,768]{3,2,1,0:T(8,128)(2,1)} %bitcast.724), calls=%async_computation.8 | async-start | bytes 983040 | tf_op jit(solution)/shard_map/all_to_all | solution.py:295
  1049.8 27.3 %all-to-all-start.9 = ((bf16[4,2,40,768]{3,2,1,0:T(8,128)(2,1)}), bf16[4,2,40,768]{3,2,1,0:T(8,128)(2,1)}, u32[]{:S(2)}, u32[]{:S(2)}) async-start(bf16[4,2,40,768]{3,2,1,0:T(8,128)(2,1)} %copy.549), calls=%async_computation.9 | async-start | bytes 983040 | tf_op jit(solution)/shard_map/all_to_all | solution.py:319
  1054.3 68.3 %reduce-scatter.45.cloned.1.call-start = ((), (), s32[]{:S(2)}) async-start(), calls=%async_computation.39 | async-start | bytes 983040
  1095.1 56.3 %reduce-scatter.47.cloned.1.call-start = ((), (), s32[]{:S(2)}) async-start(), calls=%async_computation.40 | async-start | bytes 983040
  1156.4 3.3 collective-permute-start.3
  1171.4 25.6 %all-to-all-start.10 = ((bf16[4,2,40,768]{3,2,1,0:T(8,128)(2,1)}), bf16[4,2,40,768]{3,2,1,0:T(8,128)(2,1)}, u32[]{:S(2)}, u32[]{:S(2)}) async-start(bf16[4,2,40,768]{3,2,1,0:T(8,128)(2,1)} %bitcast.719), calls=%async_computation.10 | async-start | bytes 983040 | tf_op jit(solution)/shard_map/all_to_all | solution.py:295
  1214.5 24.6 %all-to-all-start.11 = ((bf16[4,2,40,768]{3,2,1,0:T(8,128)(2,1)}), bf16[4,2,40,768]{3,2,1,0:T(8,128)(2,1)}, u32[]{:S(2)}, u32[]{:S(2)}) async-start(bf16[4,2,40,768]{3,2,1,0:T(8,128)(2,1)} %copy.562), calls=%async_computation.11 | async-start | bytes 983040 | tf_op jit(solution)/shard_map/all_to_all | solution.py:319
  1219.1 136.1 %reduce-scatter.49.cloned.1.call-start = ((), (), s32[]{:S(2)}) async-start(), calls=%async_computation.41 | async-start | bytes 983040
  1250.9 112.3 %reduce-scatter.51.cloned.1.call-start = ((), (), s32[]{:S(2)}) async-start(), calls=%async_computation.42 | async-start | bytes 983040
  1267.1 165.7 %reduce-scatter.53.cloned.1.call-start = ((), (), s32[]{:S(2)}) async-start(), calls=%async_computation.43 | async-start | bytes 417792
  1280.9 250.4 %reduce-scatter.39.cloned.1.call-start = ((), (), s32[]{:S(2)}) async-start(), calls=%async_computation.30 | async-start | bytes 11796480 | tf_op jit(solution)/shard_map/reduce_scatter | solution.py:458
  1300.4 329.2 %reduce-scatter.37.cloned.1.call-start = ((), (), s32[]{:S(2)}) async-start(), calls=%async_computation.29 | async-start | bytes 11796480 | tf_op jit(solution)/shard_map/reduce_scatter | solution.py:455
  1338.4 424.9 %reduce-scatter.29.cloned.1.call-start = ((), (), s32[]{:S(2)}) async-start(), calls=%async_computation.25 | async-start | bytes 2506752 | tf_op jit(solution)/shard_map/reduce_scatter | solution.py:446
  1343.5 551.8 %reduce-scatter.35.cloned.1.call-start = ((), (), s32[]{:S(2)}) async-start(), calls=%async_computation.28 | async-start | bytes 2506752 | tf_op jit(solution)/shard_map/reduce_scatter | solution.py:449
  1351.2 677.0 %reduce-scatter.31.cloned.1.call-start = ((), (), s32[]{:S(2)}) async-start(), calls=%async_computation.26 | async-start | bytes 2506752 | tf_op jit(solution)/shard_map/reduce_scatter | solution.py:447
  1359.2 801.1 %reduce-scatter.33.cloned.1.call-start = ((), (), s32[]{:S(2)}) async-start(), calls=%async_computation.27 | async-start | bytes 2506752 | tf_op jit(solution)/shard_map/reduce_scatter | solution.py:448
  1443.9 79.9 %copy-start.31 = (f32[128,768]{1,0:T(8,128)S(1)}, f32[128,768]{1,0:T(8,128)}, u32[]{:S(2)}) copy-start(f32[128,768]{1,0:T(8,128)} %copy-done.29) | copy-start | bytes 1179652
  1443.9 79.9 %copy-start.48 = (f32[128,768]{1,0:T(8,128)S(1)}, f32[128,768]{1,0:T(8,128)}, u32[]{:S(2)}) copy-start(f32[128,768]{1,0:T(8,128)} %copy-done.47) | copy-start | bytes 1179652
  1444.5 79.5 %copy-start.85 = (f32[1,128,768]{2,1,0:T(8,128)S(1)}, f32[1,128,768]{2,1,0:T(8,128)}, u32[]{:S(2)}) copy-start(f32[1,128,768]{2,1,0:T(8,128)} %get-tuple-element.107) | copy-start | bytes 1179652
  1531.4 628.9 %copy-start.1 = (s32[512]{0:T(512)S(1)}, s32[512]{0:T(512)}, u32[]{:S(2)}) copy-start(s32[512]{0:T(512)} %param.22) | copy-start | bytes 6148
  (187 other events, 1691.6 us)
Sparse Core Ops, SparseCore 0:
  11.4 59.5 all-gather.16
  74.3 55.0 all-gather.18
  132.7 55.0 all-gather.20
  190.4 55.0 all-gather.22
  247.2 95.2 all-gather.24
  344.7 96.3 all-gather.26
  932.1 24.2 reduce-scatter.40
  959.3 26.0 reduce-scatter.42
  1095.2 27.3 reduce-scatter.44
  1125.3 26.0 reduce-scatter.46
  1251.1 26.5 reduce-scatter.48
  1280.4 26.0 reduce-scatter.50
  1311.2 121.5 reduce-scatter.52
  1436.1 95.2 reduce-scatter.38
  1534.6 94.9 reduce-scatter.36
  1635.7 127.6 reduce-scatter.28
  1768.7 126.6 reduce-scatter.34
  1901.4 126.6 reduce-scatter.30
  2033.6 126.6 reduce-scatter.32
where the time goes:
time: 2180 us; the launch traced here: 2170 us
  waiting for transfers between devices  760 us (35%)
  local copies, waits for them, and re-layouts  563 us (26%)
  blocking collectives  344 us (16%)
  matrix products  335 us (15%)
  other arithmetic  86.6 us (4%)
  starting transfers between devices  59.6 us (3%)
    gather x2, local copies, waits for them, and re-layouts, bias_terms(): jnp.take(buckets, jnp.clip(distance, 0, buckets.shape[0] - 1))  408 us
    reduce_scatter x1, waiting for transfers between devices, body(): lax.psum_scatter(dense_totals[2], ('ctx', 'exp'), scatter_dimension=0, ti...  133 us
    reduce_scatter x1, waiting for transfers between devices, body(): lax.psum_scatter(dense_totals[3], ('ctx', 'exp'), scatter_dimension=0, ti...  132 us
    reduce_scatter x1, waiting for transfers between devices, body(): lax.psum_scatter(dense_totals[4], ('ctx', 'exp'), scatter_dimension=0, ti...  132 us
    reduce_scatter x1, waiting for transfers between devices, body(): lax.psum_scatter(dense_totals[1], ('ctx', 'exp'), scatter_dimension=0, ti...  129 us
    unnamed x2, blocking collectives  116 us
    reduce_scatter x1, waiting for transfers between devices, body(): lax.psum_scatter(expert_totals[0].astype(jnp.bfloat16), 'ctx', scatter_di...  94 us
    unnamed x26, waiting for transfers between devices  80.5 us
  transfers between devices with their start and end apart: 35, of which 20 were waited for; matrix products, arithmetic and copies ran while one was open for 35% of the time, Pallas kernels for 0%

commit v1 on v0

v1 whole, which is shorter than its diff:
```python
import functools

import jax
import jax.numpy as jnp
from jax import lax
from jax.experimental import pallas as pl
from jax.experimental.pallas import tpu as pltpu
from jax.sharding import PartitionSpec as P

EPS = 1e-06
NEG = -1e30
LOW = jnp.bfloat16
WIDE = jnp.float32
VMEM_BYTES = 48 * 1024 * 1024


def swapped(block):
    return lax.ppermute(block, "section", [(0, 1), (1, 0)])


def shifted(block, distance):
    size = lax.axis_size("ctx")
    route = [(i, i + distance) for i in range(size) if 0 <= i + distance < size]
    return lax.ppermute(block, "ctx", route)


def crossed(block, bits, axis="ctx"):
    return lax.ppermute(block, axis, [(i, i ^ bits) for i in range(lax.axis_size(axis))])


def tied(value, *others):
    return lax.optimization_barrier((value, *others))[0]


def place_kernel(moves, count, rank_ref, *refs):
    out_ref, sems = refs[count:]
    copies = []
    for number, (at, first, size, fixed, relation) in enumerate(moves):
        start = fixed + (rank_ref[0] ^ relation) * size
        target = out_ref.at[pl.ds(pl.multiple_of(start, 16), size)]
        copies.append(
            pltpu.make_async_copy(refs[at].at[pl.ds(first, size)], target, sems.at[number])
        )
        copies[-1].start()
    for one in copies:
        one.wait()


def placed(rank, pieces, moves, rows):
    return pl.pallas_call(
        functools.partial(place_kernel, moves, len(pieces)),
        out_shape=jax.ShapeDtypeStruct((rows, pieces[0].shape[1]), pieces[0].dtype),
        in_specs=[
            pl.BlockSpec(memory_space=pltpu.SMEM),
            *[pl.BlockSpec(memory_space=pl.ANY)] * len(pieces),
        ],
        out_specs=in_vmem(1)[0],
        scratch_shapes=[pltpu.SemaphoreType.DMA((len(moves),))],
        compiler_params=pltpu.CompilerParams(vmem_limit_bytes=VMEM_BYTES),
    )(rank.reshape(1), *pieces)


def four_by_four():
    return lax.axis_size("ctx") == 4 and lax.axis_size("exp") == 4


def exp_line(block):
    if not four_by_four():
        return [block] * 2, lax.all_gather(block, "exp", axis=0, tiled=True)
    shard = block.shape[0]
    along_exp = [block] + [crossed(block, k, "exp") for k in (1, 2, 3)]
    moves = [(k, 0, shard, 0, k) for k in range(4)]
    return along_exp, placed(lax.axis_index("exp"), along_exp, moves, 4 * shard)


def ctx_rows(line, before_relay):
    if not four_by_four():
        return lax.all_gather(line, "ctx", axis=0, tiled=True)
    from_x, from_y = crossed(line, 1), crossed(line, 2)
    along_ctx = [line, from_x, from_y, crossed(tied(from_x, *before_relay), 2)]
    size = line.shape[0]
    moves = [(k, 0, size, 0, k) for k in range(4)]
    return placed(lax.axis_index("ctx"), along_ctx, moves, 4 * size)


def plane_rows(block):
    from_x, from_y = crossed(block, 1), crossed(block, 2)
    along_ctx = [block, from_x, from_y, crossed(from_x, 2)]
    shard = block.shape[0]
    moves = [(k, 0, shard, 0, k) for k in range(4)]
    return placed(lax.axis_index("ctx"), along_ctx, moves, 4 * shard)


def all_rows(planes, shard):
    moves = [(k, at * shard, shard, at * 4 * shard, k) for k in range(4) for at in range(4)]
    return placed(lax.axis_index("exp"), planes, moves, 16 * shard)


def added(left, right):
    return left.astype(WIDE) + right.astype(WIDE)


def first_hop(parts, near, far):
    relayed = added(parts[far], crossed(parts[3], near)).astype(LOW)
    return added(parts[0], crossed(parts[near], near)), relayed


def last_hop(state, far):
    mine, relayed = state
    return mine + crossed(relayed, far).astype(WIDE)


def parts_for(blocks, axis, name):
    rank = lax.axis_index(name)
    return [lax.dynamic_index_in_dim(blocks, rank ^ k, axis, keepdims=False) for k in range(4)]


def over_exp(parts, came):
    total = parts[0].astype(WIDE)
    for one in came:
        total = total + one.astype(WIDE)
    return total


def over_ctx(parts):
    return last_hop(first_hop(parts, 2, 1), 1)


def sent_along_exp(parts):
    return [crossed(parts[k], k, "exp") for k in (1, 2, 3)]


def finished_along_ctx(parts, came):
    return over_ctx(parts_for(over_exp(parts, came).astype(LOW), 0, "ctx"))


def finished_along_exp(part):
    shard = part.shape[0] // 4
    parts = parts_for(part.astype(LOW).reshape(4, shard, part.shape[1]), 0, "exp")
    return over_exp(parts, sent_along_exp(parts))


def scattered_rows(block):
    block = lax.psum_scatter(block, "ctx", scatter_dimension=0, tiled=True)
    return lax.psum_scatter(block, "exp", scatter_dimension=0, tiled=True).astype(WIDE)


def dense_grads_kernel(ranks, normed_ref, grad_ref, attn_ref, branch_ref, small_ref, *refs):
    early_outs, late_outs, early, late = refs[:4], refs[4:8], refs[8], refs[9]
    cut, half = early.shape[1], branch_ref.shape[1]
    rest = grad_ref.shape[1] - cut
    early[...] = dot_dims(normed_ref[...], grad_ref[:, :cut], 0, 0).astype(LOW)
    late[:, :rest] = dot_dims(normed_ref[...], grad_ref[:, cut:], 0, 0).astype(LOW)
    late[:, rest : rest + half] = dot_dims(attn_ref[...], branch_ref[...], 0, 0).astype(LOW)
    late[:, rest + half :] = small_ref[...]
    shard = early.shape[0] // 16

    def rows_at(start):
        return pl.ds(pl.multiple_of(start, 16), shard)

    for k in range(4):
        at_exp = (ranks[1] ^ k) * shard
        for at in range(4):
            late_outs[k][at] = late[rows_at(at * 4 * shard + at_exp), :]
            start = (ranks[0] ^ k) * 4 * shard + at * shard
            early_outs[k][at * shard : (at + 1) * shard] = early[rows_at(start), :]


def dense_grads(normed_a, grad_qkv, attn_low, branch, small):
    width, half = normed_a.shape[1], branch.shape[1]
    shard = width // 16
    late_columns = half + half + small.shape[1]
    shapes = [(4 * shard, 2 * half)] * 4 + [(4, shard, late_columns)] * 4
    ranks = jnp.stack([lax.axis_index("ctx"), lax.axis_index("exp")]).astype(jnp.int32)
    out = pl.pallas_call(
        dense_grads_kernel,
        out_shape=[jax.ShapeDtypeStruct(one, LOW) for one in shapes],
        in_specs=[pl.BlockSpec(memory_space=pltpu.SMEM), *in_vmem(5)],
        out_specs=in_vmem(8),
        scratch_shapes=[pltpu.VMEM((width, 2 * half), LOW), pltpu.VMEM((width, late_columns), LOW)],
        compiler_params=pltpu.CompilerParams(vmem_limit_bytes=VMEM_BYTES),
    )(ranks, normed_a, grad_qkv, attn_low, branch, small)
    return out[:4], out[4:]


def in_vmem(count):
    return [pl.BlockSpec(memory_space=pltpu.VMEM)] * count


def dot_wide(left, right):
    return jnp.dot(left, right, preferred_element_type=WIDE)


def dot_dims(left, right, left_dim, right_dim):
    return lax.dot_general(
        left, right, (((left_dim,), (right_dim,)), ((), ())), preferred_element_type=WIDE
    )


def bias_kernel(rows, blocks, vec_ref, out_ref):
    for head in range(vec_ref.shape[0]):
        for at in range(blocks):
            wide = jnp.broadcast_to(vec_ref[head, at], (rows, 2 * rows))
            turned = pltpu.roll(wide, rows + 1, 1, stride=1, stride_axis=0)
            out_ref[
                head // 2, pl.ds((head % 2) * rows, rows), pl.ds(at * rows, rows)
            ] = turned[:, :rows]


def bias_blocks(vec, rows, blocks):
    heads = vec.shape[0]
    return pl.pallas_call(
        functools.partial(bias_kernel, rows, blocks),
        out_shape=jax.ShapeDtypeStruct((heads // 2, 2 * rows, blocks * rows), WIDE),
        in_specs=in_vmem(1),
        out_specs=in_vmem(1)[0],
        compiler_params=pltpu.CompilerParams(vmem_limit_bytes=VMEM_BYTES),
    )(vec)


def mask_rows(rows, at_q, key_blocks, seg_q, segk_ref):
    parts = []
    for back, at_k in enumerate(key_blocks):
        seg_k = segk_ref[at_k]
        good = (seg_k == 0) | (seg_k == seg_q)
        if back == 0:
            q_at = lax.broadcasted_iota(jnp.int32, (rows, rows), 0)
            k_at = lax.broadcasted_iota(jnp.int32, (rows, rows), 1)
            good = good & (q_at >= k_at)
        parts.append(jnp.where(good, 0.0, NEG).astype(WIDE))
    one = jnp.concatenate(parts, axis=1)
    return jnp.concatenate([one, one], axis=0)


def stacked_pair(block, half):
    lane = lax.broadcasted_iota(jnp.int32, block.shape, 1)
    zero = jnp.zeros_like(block)
    return jnp.concatenate(
        [jnp.where(lane < half, block, zero), jnp.where(lane >= half, block, zero)], axis=0
    )


def unstacked_pair(block, half):
    rows = block.shape[0] // 2
    lane = lax.broadcasted_iota(jnp.int32, (rows, block.shape[1]), 1)
    return jnp.where(lane < half, block[:rows], block[rows:])


def key_order(at_q, held, groups):
    near = [(0, at) for at in range(at_q, -1, -1)]
    return near + [(group, at) for group in range(1, groups) for at in range(held - 1, -1, -1)]


def attend_kernel(held, rows, groups, head_dim, *refs):
    q_ref, kv_refs = refs[0], refs[1 : 1 + groups]
    bias_ref, segq_ref, segk_ref, wide_ref, low_ref, log_ref = refs[1 + groups :]
    pairs = bias_ref.shape[0]
    lanes = 2 * head_dim
    width = pairs * lanes
    for at_q in range(held):
        order = key_order(at_q, held, groups)
        mask = mask_rows(rows, at_q, [g * held + at for g, at in order], segq_ref[at_q], segk_ref)
        here = pl.ds(at_q * rows, rows)
        for pair in range(pairs):
            cols = pl.ds(pair * lanes, lanes)
            vcols = pl.ds(width + pair * lanes, lanes)
            query = stacked_pair(q_ref[here, cols] * (head_dim**-0.5), head_dim)
            keys = jnp.concatenate(
                [kv_refs[g][pl.ds(at * rows, rows), cols] for g, at in order], axis=0
            )
            values = jnp.concatenate(
                [kv_refs[g][pl.ds(at * rows, rows), vcols] for g, at in order], axis=0
            )
            bias = bias_ref[pair, :, pl.ds(0, len(order) * rows)]
            scores = dot_dims(query, keys, 1, 1) + bias + mask
            top = jnp.max(scores, axis=1, keepdims=True)
            weights = jnp.exp(scores - top)
            total = jnp.sum(weights, axis=1, keepdims=True)
            out = dot_wide(weights.astype(LOW), values) / total
            log_ref[at_q * pairs + pair] = top + jnp.log(total)
            out = unstacked_pair(out, head_dim)
            wide_ref[here, cols] = out
            low_ref[here, cols] = out.astype(LOW)


def attend(query, kv_groups, bias, seg_q, seg_k, rows, head_dim):
    groups = len(kv_groups)
    held = query.shape[0] // rows
    pairs = bias.shape[0]
    return pl.pallas_call(
        functools.partial(attend_kernel, held, rows, groups, head_dim),
        out_shape=(
            jax.ShapeDtypeStruct(query.shape, WIDE),
            jax.ShapeDtypeStruct(query.shape, LOW),
            jax.ShapeDtypeStruct((held * pairs, 2 * rows, 1), WIDE),
        ),
        in_specs=in_vmem(4 + groups),
        out_specs=tuple(in_vmem(3)),
        compiler_params=pltpu.CompilerParams(vmem_limit_bytes=VMEM_BYTES),
    )(query, *kv_groups, bias, seg_q, seg_k)


def diagonal_sums(block):
    rows = block.shape[0]
    wide = jnp.concatenate([block, jnp.zeros_like(block)], axis=1)
    while rows > 8:
        rows //= 2
        wide = pltpu.roll(wide[:rows], rows, 1) + wide[rows:]
    row_at = lax.broadcasted_iota(jnp.int32, wide.shape, 0)
    for step in (4, 2, 1):
        wide = jnp.where(((7 - row_at) & step) != 0, pltpu.roll(wide, step, 1), wide)
    return jnp.sum(wide, axis=0, keepdims=True)


def attend_back_kernel(held, rows, groups, head_dim, *refs):
    q_ref, kv_refs = refs[0], refs[1 : 1 + groups]
    bias_ref, segq_ref, segk_ref, log_ref, grad_ref, wide_ref = refs[1 + groups : 7 + groups]
    dq_ref, dkv_refs = refs[7 + groups], refs[8 + groups : 8 + 2 * groups]
    diag_ref, acc_ref, dkv_acc = refs[8 + 2 * groups :]
    pairs = bias_ref.shape[0]
    lanes = 2 * head_dim
    width = pairs * lanes
    scale = head_dim**-0.5
    seen = set()

    def add_to(group, at, cols, block):
        here = pl.ds(at * rows, rows)
        if (group, at, cols.start) in seen:
            dkv_acc[group, here, cols] += block
        else:
            seen.add((group, at, cols.start))
            dkv_acc[group, here, cols] = block

    for at_q in range(held - 1, -1, -1):
        order = key_order(at_q, held, groups)
        mask = mask_rows(rows, at_q, [g * held + at for g, at in order], segq_ref[at_q], segk_ref)
        here = pl.ds(at_q * rows, rows)
        for pair in range(pairs):
            cols = pl.ds(pair * lanes, lanes)
            vcols = pl.ds(width + pair * lanes, lanes)
            query = stacked_pair(q_ref[here, cols] * scale, head_dim)
            grad = stacked_pair(grad_ref[here, cols], head_dim)
            wide = stacked_pair(wide_ref[here, cols], head_dim)
            delta = jnp.sum(grad.astype(WIDE) * wide, axis=1, keepdims=True)
            keys = jnp.concatenate(
                [kv_refs[g][pl.ds(at * rows, rows), cols] for g, at in order], axis=0
            )
            values = jnp.concatenate(
                [kv_refs[g][pl.ds(at * rows, rows), vcols] for g, at in order], axis=0
            )
            span = pl.ds(0, len(order) * rows)
            scores = dot_dims(query, keys, 1, 1) + bias_ref[pair, :, span] + mask
            probs = jnp.exp(scores - log_ref[at_q * pairs + pair])
            grad_probs = dot_dims(grad, values, 1, 1)
            grad_scores = (probs * (grad_probs - delta)).astype(LOW)
            grad_query = unstacked_pair(dot_wide(grad_scores, keys) * scale, head_dim)
            dq_ref[here, cols] = grad_query.astype(LOW)
            grad_keys = dot_dims(grad_scores, query, 0, 0)
            grad_values = dot_dims(probs.astype(LOW), grad, 0, 0)
            for back, (group, at) in enumerate(order):
                part = slice(back * rows, (back + 1) * rows)
                add_to(group, at, cols, grad_keys[part])
                add_to(group, at, vcols, grad_values[part])
            if at_q == held - 1:
                acc_ref[pair] = grad_scores.astype(WIDE)
            else:
                acc_ref[pair, :, span] += grad_scores.astype(WIDE)
    for group in range(groups):
        dkv_refs[group][...] = dkv_acc[group].astype(dkv_refs[group].dtype)
    for pair in range(pairs):
        for head in range(2):
            for at in range(held * groups):
                block = acc_ref[pair, pl.ds(head * rows, rows), pl.ds(at * rows, rows)]
                diag_ref[2 * pair + head, at] = diagonal_sums(block)


def attend_back(query, kv_groups, bias, seg_q, seg_k, log_total, grad, wide, rows, head_dim):
    groups = len(kv_groups)
    held = query.shape[0] // rows
    pairs = bias.shape[0]
    kv_shape = kv_groups[0].shape
    return pl.pallas_call(
        functools.partial(attend_back_kernel, held, rows, groups, head_dim),
        out_shape=(
            jax.ShapeDtypeStruct(query.shape, LOW),
            jax.ShapeDtypeStruct(kv_shape, WIDE),
            *[jax.ShapeDtypeStruct(kv_shape, LOW)] * (groups - 1),
            jax.ShapeDtypeStruct((2 * pairs, held * groups, 1, 2 * rows), WIDE),
        ),
        in_specs=in_vmem(7 + groups),
        out_specs=tuple(in_vmem(2 + groups)),
        scratch_shapes=[pltpu.VMEM(bias.shape, WIDE), pltpu.VMEM((groups, *kv_shape), WIDE)],
        compiler_params=pltpu.CompilerParams(vmem_limit_bytes=VMEM_BYTES),
    )(query, *kv_groups, bias, seg_q, seg_k, log_total, grad, wide)


GELU_A = 0.7978845608028654
GELU_B = 0.044715


def gelu_of(pre):
    return 0.5 * pre * (1.0 + jnp.tanh(GELU_A * (pre + GELU_B * pre * pre * pre)))


def gelu_and_slope(pre):
    square = pre * pre
    bent = jnp.tanh(GELU_A * pre * (1.0 + GELU_B * square))
    half_up = 0.5 * (1.0 + bent)
    slope = half_up + 0.5 * pre * (1.0 - bent * bent) * (
        GELU_A * (1.0 + 3.0 * GELU_B * square)
    )
    return pre * half_up, slope


def any_specs(count):
    return [pl.BlockSpec(memory_space=pl.ANY)] * count


CHUNKS = 4


class Chunks:
    def __init__(self, first_hbm, second_hbm, first, second, sems):
        hidden = second.shape[1]
        self.first_copies = [
            pltpu.make_async_copy(
                first_hbm.at[:, at * hidden : (at + 1) * hidden], first.at[at], sems.at[0, at]
            )
            for at in range(CHUNKS)
        ]
        self.second_copies = [
            pltpu.make_async_copy(
                second_hbm.at[at * hidden : (at + 1) * hidden], second.at[at], sems.at[1, at]
            )
            for at in range(CHUNKS)
        ]
        for first_copy, second_copy in zip(self.first_copies, self.second_copies):
            first_copy.start()
            second_copy.start()


def experts_forward_steps(chunks, x, first, second, total, pre_ref):
    for at in range(CHUNKS):
        chunks.first_copies[at].wait()
        pre = dot_wide(x, first[at])
        pre_ref[at] = pre
        act = gelu_of(pre).astype(LOW)
        chunks.second_copies[at].wait()
        part = dot_wide(act, second[at])
        total[...] = part if at == 0 else total[...] + part


def experts_back_steps(x, grad, pre_ref, first, second, total, gfirst, gsecond, outs, sems, chunks):
    out_first, out_second = outs
    hidden = second.shape[1]
    copies = []
    for at in range(CHUNKS):
        if chunks is not None:
            chunks.second_copies[at].wait()
            chunks.first_copies[at].wait()
        here = slice(at * hidden, (at + 1) * hidden)
        act, slope = gelu_and_slope(pre_ref[at])
        if gsecond is not None:
            gsecond[at] = dot_dims(act.astype(LOW), grad, 0, 0).astype(LOW)
            copies.append(
                pltpu.make_async_copy(gsecond.at[at], out_second.at[here], sems.at[1, at])
            )
            copies[-1].start()
        grad_act = dot_dims(grad, second[at], 1, 1)
        grad_pre = (grad_act * slope).astype(LOW)
        gfirst[at] = dot_dims(x, grad_pre, 0, 0).astype(LOW)
        copies.append(pltpu.make_async_copy(gfirst.at[at], out_first.at[:, here], sems.at[0, at]))
        copies[-1].start()
        part = dot_dims(grad_pre, first[at], 1, 1)
        total[...] = part if at == 0 else total[...] + part
    return copies


def experts_kernel(x_ref, first_hbm, second_hbm, y_ref, pre_ref, first, second, total, sems):
    chunks = Chunks(first_hbm, second_hbm, first, second, sems)
    experts_forward_steps(chunks, x_ref[...], first, second, total, pre_ref)
    y_ref[...] = total[...].astype(LOW)


def experts_second_kernel(pre_ref, grad_ref, out_ref, gsecond, sems):
    hidden = gsecond.shape[1]
    copies = []
    for at in range(CHUNKS):
        act = gelu_of(pre_ref[at]).astype(LOW)
        gsecond[at] = dot_dims(act, grad_ref[...], 0, 0).astype(LOW)
        target = out_ref.at[at * hidden : (at + 1) * hidden]
        copies.append(pltpu.make_async_copy(gsecond.at[at], target, sems.at[at]))
        copies[-1].start()
    for one in copies:
        one.wait()


def experts_back_kernel(x_ref, grad_ref, pre_ref, first_hbm, second_hbm, dx_ref, out_first, *refs):
    first, second, total, gfirst, sems, out_sems = refs
    chunks = Chunks(first_hbm, second_hbm, first, second, sems)
    copies = experts_back_steps(
        x_ref[...],
        grad_ref[...],
        pre_ref,
        first,
        second,
        total,
        gfirst,
        None,
        (out_first, None),
        out_sems,
        chunks,
    )
    dx_ref[...] = total[...].astype(LOW)
    for one in copies:
        one.wait()


def experts_both_kernel(width, x_ref, cot_ref, *refs):
    first_hbm, second_hbm, y_ref, dx_ref, out_first, out_second = refs[:6]
    first, second, total, gfirst, gsecond, pre, sems, out_sems = refs[6:]
    chunks = Chunks(first_hbm, second_hbm, first, second, sems)
    x = x_ref[:, :width]
    experts_forward_steps(chunks, x, first, second, total, pre)
    y_low = total[...].astype(LOW)
    y_ref[...] = y_low
    cot = cot_ref[...].astype(WIDE)
    grad_gate = jnp.sum(y_low.astype(WIDE) * cot, axis=1, keepdims=True)
    high = grad_gate.astype(LOW).astype(WIDE)
    lane = lax.broadcasted_iota(jnp.int32, (x.shape[0], x_ref.shape[1] - width), 1)
    both = jnp.where(lane == 0, high, jnp.where(lane == 1, grad_gate - high, 0.0))
    dx_ref[:, width:] = both.astype(LOW)
    gate = x_ref[:, width : width + 1].astype(WIDE) + x_ref[:, width + 1 : width + 2].astype(WIDE)
    grad = (gate * cot).astype(LOW)
    copies = experts_back_steps(
        x, grad, pre, first, second, total, gfirst, gsecond, (out_first, out_second), out_sems, None
    )
    dx_ref[:, :width] = total[...].astype(LOW)
    for one in copies:
        one.wait()


def expert_call(kernel, arrays, first, second, shapes, with_grads, scratch):
    width, hidden = first.shape
    rows = arrays[0].shape[0]
    weights = [
        pltpu.VMEM((CHUNKS, width, hidden // CHUNKS), LOW),
        pltpu.VMEM((CHUNKS, hidden // CHUNKS, width), LOW),
    ]
    grads = [jax.ShapeDtypeStruct(one.shape, LOW) for one in (first, second)]
    sems = [pltpu.SemaphoreType.DMA((2, CHUNKS))]
    return pl.pallas_call(
        kernel,
        out_shape=(*shapes, *(grads if with_grads else [])),
        in_specs=[*in_vmem(len(arrays)), *any_specs(2)],
        out_specs=(*in_vmem(len(shapes)), *any_specs(2 if with_grads else 0)),
        scratch_shapes=[
            *weights,
            pltpu.VMEM((rows, width), WIDE),
            *(weights if with_grads else []),
            *scratch,
            *sems,
            *(sems if with_grads else []),
        ],
        compiler_params=pltpu.CompilerParams(vmem_limit_bytes=VMEM_BYTES),
    )(*arrays, first, second)


def pre_shape(rows, first):
    return (CHUNKS, rows, first.shape[1] // CHUNKS)


def run_experts(rows_in, first, second):
    shapes = [
        jax.ShapeDtypeStruct(rows_in.shape, LOW),
        jax.ShapeDtypeStruct(pre_shape(rows_in.shape[0], first), WIDE),
    ]
    return expert_call(experts_kernel, [rows_in], first, second, shapes, False, [])


def run_experts_second(pre, grad, second):
    hidden, width = second.shape
    return pl.pallas_call(
        experts_second_kernel,
        out_shape=jax.ShapeDtypeStruct(second.shape, LOW),
        in_specs=in_vmem(2),
        out_specs=any_specs(1)[0],
        scratch_shapes=[
            pltpu.VMEM((CHUNKS, hidden // CHUNKS, width), LOW),
            pltpu.SemaphoreType.DMA((CHUNKS,)),
        ],
        compiler_params=pltpu.CompilerParams(vmem_limit_bytes=VMEM_BYTES),
    )(pre, grad)


def run_experts_back(rows_in, grad, pre, first, second):
    width, hidden = first.shape
    weights = [
        pltpu.VMEM((CHUNKS, width, hidden // CHUNKS), LOW),
        pltpu.VMEM((CHUNKS, hidden // CHUNKS, width), LOW),
    ]
    return pl.pallas_call(
        experts_back_kernel,
        out_shape=[
            jax.ShapeDtypeStruct(rows_in.shape, LOW),
            jax.ShapeDtypeStruct(first.shape, LOW),
        ],
        in_specs=[*in_vmem(3), *any_specs(2)],
        out_specs=[*in_vmem(1), *any_specs(1)],
        scratch_shapes=[
            *weights,
            pltpu.VMEM(rows_in.shape, WIDE),
            weights[0],
            pltpu.SemaphoreType.DMA((2, CHUNKS)),
            pltpu.SemaphoreType.DMA((2, CHUNKS)),
        ],
        compiler_params=pltpu.CompilerParams(vmem_limit_bytes=VMEM_BYTES),
    )(rows_in, grad, pre, first, second)


def run_experts_both(rows_in, cot, first, second):
    kernel = functools.partial(experts_both_kernel, cot.shape[1])
    shapes = [jax.ShapeDtypeStruct(cot.shape, LOW), jax.ShapeDtypeStruct(rows_in.shape, LOW)]
    scratch = [pltpu.VMEM(pre_shape(cot.shape[0], first), WIDE)]
    return expert_call(kernel, [rows_in, cot], first, second, shapes, True, scratch)


def by_core(core, zero, one):
    return jnp.where(core == 0, zero, one)


def cut_kernel(words, first_ref, second_ref, first_mine, second_mine, first_sent, second_sent):
    first_mine[...] = first_ref[words[1]].astype(LOW)
    second_mine[...] = second_ref[words[1]].astype(LOW)
    first_sent[...] = first_ref[1 - words[1]].astype(LOW)
    second_sent[...] = second_ref[1 - words[1]].astype(LOW)


def cut_experts(words, first, second):
    shapes = [first.shape[1:], second.shape[1:]] * 2
    return pl.pallas_call(
        cut_kernel,
        out_shape=[jax.ShapeDtypeStruct(one, LOW) for one in shapes],
        in_specs=[pl.BlockSpec(memory_space=pltpu.SMEM), *in_vmem(2)],
        out_specs=in_vmem(4),
        compiler_params=pltpu.CompilerParams(vmem_limit_bytes=VMEM_BYTES),
    )(words, first, second)


def choose_kernel(count, words, *refs):
    zeros, ones, outs = refs[:count], refs[count : 2 * count], refs[2 * count :]

    def copy_all(sources):
        for source, out in zip(sources, outs):
            out[...] = source[...]

    @pl.when(words[1] == 0)
    def _():
        copy_all(zeros)

    @pl.when(words[1] != 0)
    def _():
        copy_all(ones)


def chosen_by_core(words, zeros, ones):
    count = len(zeros)
    return pl.pallas_call(
        functools.partial(choose_kernel, count),
        out_shape=[jax.ShapeDtypeStruct(one.shape, one.dtype) for one in zeros],
        in_specs=[pl.BlockSpec(memory_space=pltpu.SMEM), *in_vmem(2 * count)],
        out_specs=in_vmem(count),
        compiler_params=pltpu.CompilerParams(vmem_limit_bytes=VMEM_BYTES),
    )(words, *zeros, *ones)


def join_kernel(words, *refs):
    ones, twos, came, outs = refs[:2], refs[2:4], refs[4:6], refs[6:8]
    for at in range(2):
        outs[at][1 - words[1]] = came[at][...].astype(WIDE)

    @pl.when(words[1] == 0)
    def _():
        for at in range(2):
            outs[at][0] = ones[at][...].astype(WIDE)

    @pl.when(words[1] != 0)
    def _():
        for at in range(2):
            outs[at][1] = twos[at][...].astype(WIDE)


def join_experts(words, ones, twos, came):
    return pl.pallas_call(
        join_kernel,
        out_shape=[jax.ShapeDtypeStruct((2, *one.shape), WIDE) for one in ones],
        in_specs=[pl.BlockSpec(memory_space=pltpu.SMEM), *in_vmem(6)],
        out_specs=in_vmem(2),
        compiler_params=pltpu.CompilerParams(vmem_limit_bytes=VMEM_BYTES),
    )(words, *ones, *twos, *came)


def pack_kernel(words, small_ref, *refs):
    early_mine, early_sent, late_mine, late_sent = refs[4:]
    lead = small_ref.shape[1]
    early_mine[:, :lead] = small_ref[...]
    early_sent[:, :lead] = small_ref[...]
    for at, ref in enumerate(refs[:4]):
        half = ref.shape[1] // 2
        low, high = ref[:, :half], ref[:, half:]
        mine = by_core(words[1], low, high).astype(LOW)
        sent = by_core(words[1], high, low).astype(LOW)
        if at < 3:
            cols = slice(lead + at * half, lead + (at + 1) * half)
            early_mine[:, cols] = mine
            early_sent[:, cols] = sent
        else:
            late_mine[...] = mine
            late_sent[...] = sent


def pack_dense(words, small, weights):
    shard, width = weights[0].shape
    early, late = (shard, small.shape[1] + 3 * width // 2), (shard, width // 2)
    return pl.pallas_call(
        pack_kernel,
        out_shape=[jax.ShapeDtypeStruct(one, LOW) for one in (early, early, late, late)],
        in_specs=[pl.BlockSpec(memory_space=pltpu.SMEM), *in_vmem(5)],
        out_specs=in_vmem(4),
        compiler_params=pltpu.CompilerParams(vmem_limit_bytes=VMEM_BYTES),
    )(words, small, *weights)


def unpack_kernel(words, own_ref, came_ref, *outs):
    half = outs[0].shape[1] // 2
    for at, out in enumerate(outs[:4]):
        cols = slice(at * half, (at + 1) * half)
        own, came = own_ref[:, cols], came_ref[:, cols]
        out[:, :half] = by_core(words[1], own, came)
        out[:, half:] = by_core(words[1], came, own)
    outs[4][...] = own_ref[:, 4 * half :] + came_ref[:, 4 * half :]


def unpack_dense(words, own, came, width):
    shard = own.shape[0]
    shapes = [(shard, width)] * 4 + [(shard, own.shape[1] - 2 * width)]
    return pl.pallas_call(
        unpack_kernel,
        out_shape=[jax.ShapeDtypeStruct(one, WIDE) for one in shapes],
        in_specs=[pl.BlockSpec(memory_space=pltpu.SMEM), *in_vmem(2)],
        out_specs=in_vmem(5),
        compiler_params=pltpu.CompilerParams(vmem_limit_bytes=VMEM_BYTES),
    )(words, own, came)


def norm_back(grad_out, value, inverse, gain_row):
    scaled = grad_out * gain_row
    return inverse * (
        scaled - value * inverse * inverse * jnp.mean(scaled * value, axis=-1, keepdims=True)
    )


def sums_by_token_kernel(width, *refs):
    sent_ref, hot0, hot1, *more, out_ref = refs
    lanes = out_ref.shape[1] - width
    sent = sent_ref[:, :width]
    out_ref[:, :width] = dot_dims(hot0[...] + hot1[...], sent, 0, 0)
    lane = lax.broadcasted_iota(jnp.int32, (out_ref.shape[0], lanes), 1)
    parts = []
    for hot in (hot0, hot1):
        if more:
            returned_ref, grad_ref = more
            picked = dot_dims(hot[...], returned_ref[...], 0, 0)
            parts.append(jnp.sum(grad_ref[...].astype(WIDE) * picked, axis=1, keepdims=True))
        else:
            both = dot_dims(hot[...], sent_ref[:, width:], 0, 0)
            parts.append(both[:, :1] + both[:, 1:2])
    out_ref[:, width:] = jnp.where(lane == 0, parts[0], jnp.where(lane == 1, parts[1], 0.0))


def local_call(kernel, shapes, *arrays):
    def whole(one):
        if one.ndim == 1:
            return pl.BlockSpec(memory_space=pltpu.SMEM)
        return pl.BlockSpec(one.shape, lambda step: (0,) * one.ndim)

    return pl.pallas_call(
        kernel,
        grid=(1,),
        out_shape=shapes,
        in_specs=[whole(one) for one in arrays],
        out_specs=[whole(one) for one in shapes],
        compiler_params=pltpu.CompilerParams(vmem_limit_bytes=VMEM_BYTES),
    )(*arrays)


def column_sums(block, lanes, at):
    lane = lax.broadcasted_iota(jnp.int32, (block.shape[0], lanes), 1)
    return lax.dot_general(
        block,
        jnp.where(lane == at, 1.0, 0.0).astype(WIDE),
        (((0,), (0,)), ((), ())),
        precision=lax.Precision.HIGHEST,
        preferred_element_type=WIDE,
    )


def to_attention_kernel(words, *refs):
    mine_ref, other_ref, gates_ref, routes_ref, residual_ref, normed_ref, gain_ref = refs[:7]
    small_ref, out_w, grad_ref, dh_ref, attn_ref, branch_ref, grads_ref = refs[7:]
    width, lanes = residual_ref.shape[1], small_ref.shape[1]
    sums = mine_ref[...] + other_ref[...]
    grad_gates, gates = sums[:, width : width + 2], gates_ref[...]
    grad_chosen = gates * (grad_gates - jnp.sum(gates * grad_gates, axis=1, keepdims=True))
    routes = routes_ref[...]
    column = lax.broadcasted_iota(jnp.int32, (routes.shape[0], lanes), 1) - 2
    grad_logits = jnp.where(column == routes[:, :1], grad_chosen[:, :1], 0.0) + jnp.where(
        column == routes[:, 1:], grad_chosen[:, 1:2], 0.0
    )
    grad_logits = grad_logits.astype(LOW)
    grad_normed = sums[:, :width] + dot_dims(grad_logits, small_ref[...], 1, 1)
    residual = residual_ref[...]
    inverse = lax.rsqrt(jnp.mean(residual * residual, axis=1, keepdims=True) + EPS)
    grads_ref[...] = dot_dims(normed_ref[...], grad_logits, 0, 0) + column_sums(
        grad_normed * residual * inverse, lanes, 1
    )
    grad = grad_ref[...].astype(WIDE) + norm_back(grad_normed, residual, inverse, gain_ref[...])
    dh_ref[...] = grad
    low = grad.astype(LOW)
    half = branch_ref.shape[1]
    branch_ref[...] = by_core(words[1], low[:, :half], low[:, half:])
    heads = out_w[pl.ds(pl.multiple_of(words[1] * half, 16), half), :]
    attn_ref[...] = dot_dims(low, heads, 1, 1).astype(LOW)


def from_attention_kernel(count, *refs):
    query_ref, own_ref, *more = refs
    came, (weight_ref, qkv_ref, partial_ref) = more[:count], more[count:]
    half = query_ref.shape[1]
    total = own_ref[...]
    for one in came:
        total = total + one[...].astype(WIDE)
    qkv_ref[:, :half] = query_ref[...]
    qkv_ref[:, half:] = total.astype(LOW)
    partial_ref[...] = dot_dims(qkv_ref[...], weight_ref[...], 1, 1)


def to_input_kernel(mine_ref, other_ref, dh_ref, value_ref, gain_ref, small_ref, *refs):
    grad_normed = mine_ref[...] + other_ref[...]
    value = value_ref[...].astype(WIDE)
    inverse = lax.rsqrt(jnp.mean(value * value, axis=1, keepdims=True) + EPS)
    grad = dh_ref[...] + norm_back(grad_normed, value, inverse, gain_ref[...])
    grads_ref, out_ref, *slot_refs = refs[-2:] if len(refs) == 2 else refs[3:]
    grads_ref[...] = small_ref[...] + column_sums(
        grad_normed * value * inverse, grads_ref.shape[1], 0
    )
    out_ref[...] = grad
    if slot_refs:
        gates_ref, hot0, hot1 = refs[:3]
        low = grad.astype(LOW).astype(WIDE)
        rows = dot_wide(hot0[...], (gates_ref[:, :1] * low).astype(LOW))
        rows = rows + dot_wide(hot1[...], (gates_ref[:, 1:2] * low).astype(LOW))
        slot_refs[0][...] = rows.astype(LOW)


def body(
    inputs,
    cotangent,
    segments,
    buckets,
    routes,
    gain_attn,
    w_query,
    w_key,
    w_value,
    w_out,
    rel_bias,
    gain_moe,
    w_router,
    w_in,
    w_back,
):
    core = lax.axis_index("section")
    is_first = core == 0
    ctx_rank = lax.axis_index("ctx")
    ctx_count = lax.axis_size("ctx")
    exp_count = lax.axis_size("exp")
    held, rows, width = inputs.shape[0], inputs.shape[2], inputs.shape[3]
    groups = ctx_count // held
    parity = ctx_rank % held
    is_even = parity == 0
    group_rank = ctx_rank // held
    heads = rel_bias.shape[2]
    head_dim = width // heads
    half = width // 2
    half_heads = heads // 2
    local_exp = w_in.shape[1]
    experts = exp_count * local_exp
    capacity = 2 * rows // experts * 5 // 4
    bucket_count = rel_bias.shape[1] * ctx_count * exp_count
    shard = w_query.shape[1]
    rel_cols = rel_bias.shape[1] * heads // shard
    small_used = 2 + experts + rel_cols
    small_width = -(-small_used // 128) * 128
    extra = 128
    tokens = held * rows

    def regrouped(block):
        mine = lax.dynamic_index_in_dim(block, parity, 0, keepdims=False)
        sent = lax.dynamic_index_in_dim(block, 1 - parity, 0, keepdims=False)
        came = crossed(sent, 1)
        return jnp.where(is_even, jnp.stack([mine, came]), jnp.stack([came, mine]))

    def own_order(mine, other, axis):
        return jnp.where(
            is_first,
            jnp.concatenate([mine, other], axis=axis),
            jnp.concatenate([other, mine], axis=axis),
        )

    def both_cores(mine, axis=0):
        return own_order(mine, swapped(mine), axis)

    words = jnp.stack([ctx_rank, core]).astype(jnp.int32)
    small = jnp.concatenate(
        [
            gain_attn[0].astype(LOW)[:, None],
            gain_moe[0].astype(LOW)[:, None],
            w_router[0].astype(LOW),
            rel_bias[0].astype(LOW).reshape(shard, rel_cols),
            jnp.zeros((shard, small_width - small_used), LOW),
        ],
        axis=1,
    )

    def by_section(mine, other):
        return (jnp.where(is_first, mine, other), jnp.where(is_first, other, mine))

    first_mine, second_mine, first_sent, second_sent = cut_experts(words, w_in[0], w_back[0])
    own_shards, came_shards = [first_mine, second_mine], [swapped(first_sent), swapped(second_sent)]
    shards_one = chosen_by_core(words, own_shards, came_shards)
    early_mine, early_sent, late_mine, late_sent = pack_dense(
        tied(words, first_mine), small, [w[0] for w in (w_query, w_key, w_value, w_out)]
    )
    early_shards = by_section(early_mine, swapped(early_sent))
    late_shards = by_section(late_mine, swapped(late_sent))
    _, early_line = exp_line(early_shards[0])
    shards_two = chosen_by_core(words, came_shards, own_shards)

    def gathered(shards):
        return [lax.all_gather(one, "ctx", axis=0, tiled=True) for one in shards]

    seg_row = lax.dynamic_index_in_dim(segments[:, 0], parity, 0, keepdims=False)
    seg_blocks = seg_row.reshape(groups, held, rows)
    seg_keys = []
    for back in range(groups):
        seg = lax.dynamic_index_in_dim(
            seg_blocks, jnp.maximum(group_rank - back, 0), 0, keepdims=False
        )
        seg_keys.append(jnp.where(group_rank >= back, seg, -1))
    seg_q = seg_keys[0][:, :, None]
    seg_k = jnp.concatenate(seg_keys, axis=0)[:, None, :]

    back_order = jnp.flip(jnp.concatenate([jnp.broadcast_to(buckets[:1], (rows,)), buckets]))
    span = back_order.shape[0]
    by_distance = []
    for at in range(ctx_count):
        start = span - 2 * rows - at * rows
        by_distance.append(back_order[start : start + 2 * rows])
    bucket_vec = jnp.concatenate(by_distance)
    bucket_hot = (
        bucket_vec[:, None] == jnp.arange(bucket_count, dtype=jnp.int32)[None, :]
    ).astype(LOW)

    route_rows = regrouped(routes[:, 0])
    expert_ids = jnp.arange(experts, dtype=jnp.int32)
    flat_routes = route_rows.reshape(held, 2 * rows)
    member = (flat_routes[..., None] == expert_ids).astype(jnp.int32)
    slot_rank = jnp.sum((jnp.cumsum(member, axis=1) - member) * member, axis=-1)
    block_at = jnp.arange(held, dtype=jnp.int32)[:, None]
    slot_dest = ((flat_routes * held + block_at) * capacity + slot_rank).reshape(tokens, 2)
    exp_ids = jnp.arange(exp_count, dtype=jnp.int32)[:, None, None]
    in_block = block_at[None] * capacity + jnp.arange(capacity, dtype=jnp.int32)[None, None, :]
    slots = exp_count * held * capacity
    slot_ids = ((exp_ids * local_exp + core) * held * capacity + in_block).reshape(slots, 1)
    hots = [(slot_ids == slot_dest[None, :, c]).astype(LOW) for c in range(2)]
    to_token = hots[0] + hots[1]
    route_rows = route_rows.reshape(tokens, 2)
    small_ids = jnp.arange(small_width, dtype=jnp.int32)[None, :] - 2
    chosen_hot = [(route_rows[:, c : c + 1] == small_ids).astype(WIDE) for c in range(2)]

    def early_weights(early):
        tail = early[:, :small_width]
        rel = tail[:, 2 + experts : 2 + experts + rel_cols].reshape(bucket_count, heads)
        rel_mine = lax.dynamic_slice_in_dim(rel, core * half_heads, half_heads, 1)
        vec = dot_dims(rel_mine, bucket_hot, 0, 1)
        bias = bias_blocks(vec.reshape(half_heads, ctx_count, 1, 2 * rows), rows, ctx_count)
        return dict(
            qkv=early[:, small_width:],
            gain_a=tail[:, 0].astype(WIDE),
            gain_m=tail[:, 1].astype(WIDE),
            small=tail,
            bias=bias,
        )

    def late_weights(out_half):
        out_full = both_cores(out_half, 1)
        return dict(
            out=out_full, out_mine=lax.dynamic_slice_in_dim(out_full, core * half, half, 0)
        )

    def to_experts(rows_out):
        lanes = rows_out.shape[1]
        return lax.all_to_all(
            rows_out.reshape(exp_count, held * capacity, lanes),
            "exp",
            split_axis=0,
            concat_axis=0,
            tiled=True,
        ).reshape(slots, lanes)

    def in_two(wide):
        high = wide.astype(LOW)
        low = (wide - high.astype(WIDE)).astype(LOW)
        pad = jnp.zeros((wide.shape[0], extra - 2), LOW)
        return jnp.concatenate([high, low, pad], axis=1)

    def normed(value, gain_row):
        inverse = lax.rsqrt(jnp.mean(value * value, axis=-1, keepdims=True) + EPS)
        return (value * inverse * gain_row).astype(LOW), inverse

    def attention(normed_a, weights, arrived, arrived_after):
        qkv = dot_wide(normed_a, weights["qkv"]).astype(LOW)
        query, kv = qkv[:, :half], tied(qkv[:, half:], *arrived)
        kv_groups = [kv] + [shifted(kv, held * back) for back in range(1, groups)]
        attn_wide, attn_mine, log_total = attend(
            query, kv_groups, weights["bias"], seg_q, seg_k, rows, head_dim
        )
        attn_low = both_cores(tied(attn_mine, *arrived_after), 1)
        return dict(
            normed_a=normed_a,
            query=query,
            kv_groups=kv_groups,
            attn_wide=attn_wide,
            attn_low=attn_low,
            log_total=log_total,
        )

    def forward_to_experts(value, kept, weights, with_gates, arrived):
        residual = value + dot_wide(kept["attn_low"], weights["out"])
        normed_m, inv_m = normed(residual, weights["gain_m"])
        logits = dot_wide(normed_m, weights["small"])
        chosen = [jnp.sum(logits * hot_c, axis=-1, keepdims=True) for hot_c in chosen_hot]
        gates = jax.nn.softmax(jnp.concatenate(chosen, axis=1), axis=-1)
        sent = dot_wide(to_token, normed_m).astype(LOW)
        if with_gates:
            gate_rows = dot_wide(hots[0], in_two(gates[:, :1])) + dot_wide(
                hots[1], in_two(gates[:, 1:])
            )
            sent = jnp.concatenate([sent, gate_rows.astype(LOW)], axis=1)
        received = to_experts(tied(sent, *arrived))
        return dict(
            kept,
            value=value,
            residual=residual,
            inv_m=inv_m,
            normed_m=normed_m,
            gates=gates,
            received=received,
        )

    def combined(produced, kept):
        returned = to_experts(produced)
        picked = [dot_dims(hot_c, returned, 0, 0) for hot_c in hots]
        partial = kept["gates"][:, :1] * picked[0] + kept["gates"][:, 1:] * picked[1]
        return kept["residual"] + (partial + swapped(partial)), returned

    def wide_like(*shape):
        return jax.ShapeDtypeStruct(shape, WIDE)

    def low_like(*shape):
        return jax.ShapeDtypeStruct(shape, LOW)

    def backward_from_experts(grad_out, grad_sent, returned, weights, kept, below, arrived=()):
        more = [] if returned is None else [returned, grad_out]
        (partial,) = local_call(
            functools.partial(sums_by_token_kernel, width),
            [wide_like(tokens, width + extra)],
            grad_sent,
            *hots,
            *more,
        )
        grad_residual, grad_attn, branch_mine, small_part = local_call(
            to_attention_kernel,
            [
                wide_like(tokens, width),
                low_like(tokens, half),
                low_like(tokens, half),
                wide_like(width, small_width),
            ],
            words,
            partial,
            swapped(partial),
            kept["gates"],
            route_rows,
            kept["residual"],
            kept["normed_m"],
            weights["gain_m"][None],
            weights["small"],
            weights["out"],
            grad_out,
        )
        back = attend_back(
            kept["query"],
            kept["kv_groups"],
            weights["bias"],
            seg_q,
            seg_k,
            kept["log_total"],
            grad_attn,
            kept["attn_wide"],
            rows,
            head_dim,
        )
        grad_query, diag = tied(back[0], *arrived), back[-1]
        came = [shifted(back[1 + at], -held * at) for at in range(1, groups)]
        grad_qkv, partial = local_call(
            functools.partial(from_attention_kernel, groups - 1),
            [low_like(tokens, 3 * half), wide_like(tokens, width)],
            grad_query,
            back[1],
            *came,
            weights["qkv"],
        )
        slot_inputs = [] if below is None else [below, *hots]
        small_part, grad_value, *slot_rows = local_call(
            to_input_kernel,
            [wide_like(width, small_width), wide_like(tokens, width)]
            + ([] if below is None else [low_like(slots, width)]),
            partial,
            swapped(partial),
            grad_residual,
            kept["low"],
            weights["gain_a"][None],
            small_part,
            *slot_inputs,
        )
        grad_rel = lax.dot_general(
            bucket_hot.astype(WIDE),
            diag.reshape(half_heads, -1),
            (((0,), (1,)), ((), ())),
            precision=lax.Precision.HIGHEST,
            preferred_element_type=WIDE,
        )
        grad_rel = own_order(grad_rel, jnp.zeros_like(grad_rel), 1)
        rel_columns = jnp.pad(
            grad_rel.reshape(width, rel_cols),
            ((0, 0), (2 + experts, small_width - small_used)),
        )
        small_grads = (0.5 * small_part + rel_columns).astype(LOW)
        grads_of = (kept["normed_a"], grad_qkv, kept["attn_low"], branch_mine, small_grads)
        return grad_value, grads_of, grad_qkv, grad_attn, slot_rows

    def whole_dense_grads(normed_a, grad_qkv, attn_low, branch, small):
        qkv_w, out_w = dot_dims(normed_a, grad_qkv, 0, 0), dot_dims(attn_low, branch, 0, 0)
        return scattered_rows(
            jnp.concatenate([qkv_w.astype(LOW), out_w.astype(LOW), small], axis=1)
        )

    def summed_shards(grads):
        return [
            lax.psum_scatter(one, "ctx", scatter_dimension=0, tiled=True) for one in grads
        ]

    relayed = four_by_four()
    both = jnp.concatenate([early_shards[1], late_shards[1]], axis=1)
    if relayed:
        plane = plane_rows(both)
        planes = [plane] + sent_along_exp([plane] * 4)
        both = all_rows(planes, shard)
        early_line = tied(early_line, plane)
    else:
        planes = [both] * 4
        both = lax.all_gather(both, ("ctx", "exp"), axis=0, tiled=True)
    _, late_line = exp_line(tied(late_shards[0], early_line))
    early_one = tied(ctx_rows(early_line, []), late_line)
    dense_one = early_weights(early_one)
    value_low = regrouped(inputs[:, 0]).reshape(tokens, width)
    value = value_low.astype(WIDE)
    normed_a, inv_a = normed(value, dense_one["gain_a"])
    cot = regrouped(cotangent[:, 0]).reshape(tokens, width)
    experts_one = gathered(shards_one)
    kept_one = attention(normed_a, dense_one, [planes[1]], [planes[2]])
    kv_came = kept_one["kv_groups"][-1]
    dense_one = dict(dense_one, **late_weights(ctx_rows(late_line, [kv_came])))
    kept_one = forward_to_experts(value, kept_one, dense_one, False, [])
    kept_one["low"] = value_low
    experts_two = gathered([tied(one, kept_one["received"]) for one in shards_two])
    produced, pre_one = run_experts(kept_one["received"], *experts_one)
    out_one, returned_one = combined(tied(produced, planes[3]), kept_one)

    dense_two = dict(
        early_weights(both[:, : small_width + 3 * half]),
        **late_weights(both[:, small_width + 3 * half :]),
    )
    value_low = out_one.astype(LOW)
    value = value_low.astype(WIDE)
    normed_a, inv_a = normed(value, dense_two["gain_a"])
    kept_two = attention(normed_a, dense_two, [], [])
    cot_rows = to_experts(tied(dot_wide(to_token, cot).astype(LOW), out_one))
    kept_two = forward_to_experts(value, kept_two, dense_two, True, [cot_rows])
    kept_two["low"] = value_low
    produced, grad_rows, *grads_two = run_experts_both(
        kept_two["received"], cot_rows, *experts_two
    )
    grad_sent = to_experts(grad_rows)
    sums_two = summed_shards(grads_two)
    grad_two, grads_of_two, _, grad_attn, (slot_rows,) = backward_from_experts(
        cot, grad_sent, None, dense_two, kept_two, kept_one["gates"]
    )
    out_two, _ = combined(tied(produced, grad_attn), kept_two)

    grad_out = grad_two.astype(LOW)
    grad_rows = to_experts(slot_rows)
    if relayed:
        early_parts, late_parts = dense_grads(*grads_of_two)
        grad_rows = tied(grad_rows, *late_parts, *early_parts)
        early_hop = first_hop(early_parts, 2, 1)
    grad_rows, out_two = lax.optimization_barrier((grad_rows, out_two))
    second_grads = run_experts_second(pre_one, grad_rows, experts_one[1])
    sums_one = summed_shards([second_grads])
    grad_rows, first_grads = run_experts_back(
        kept_one["received"], grad_rows, tied(pre_one, second_grads), *experts_one
    )
    sums_one = summed_shards([first_grads]) + sums_one
    activations = regrouped(jnp.where(is_first, out_one, out_two).reshape(held, rows, width))
    grad_sent = to_experts(grad_rows)
    late_two, early_two = [], []
    if relayed:
        grad_sent, early_hop = lax.optimization_barrier((grad_sent, early_hop))
        late_two = sent_along_exp([tied(one, grad_sent) for one in late_parts])
        early_two = [finished_along_exp(last_hop(early_hop, 1))]
    grad_one, grads_of_one, grad_qkv, _, _ = backward_from_experts(
        grad_out, grad_sent, returned_one, dense_one, kept_one, None, [*late_two, *early_two]
    )
    came = [swapped(one) for one in chosen_by_core(words, sums_two, sums_one)]
    if relayed:
        late_parts_two = late_parts
        early_parts, late_parts = dense_grads(*grads_of_one)
        late_two = [tied(one, late_parts[0]) for one in late_two]
        late_one = sent_along_exp(late_parts)
        early_one = over_ctx(early_parts)
        dense_sum_one = jnp.concatenate(
            [finished_along_exp(early_one), finished_along_ctx(late_parts, late_one)], axis=1
        )
        dense_sum_two = jnp.concatenate(
            [early_two[0], finished_along_ctx(late_parts_two, late_two)], axis=1
        )
    else:
        dense_sum_two = whole_dense_grads(*grads_of_two)
        dense_sum_one = whole_dense_grads(*grads_of_one)

    grads_in = regrouped(jnp.where(is_first, grad_one, grad_two).reshape(held, rows, width))
    dense_own = jnp.where(is_first, dense_sum_one, dense_sum_two)
    dense_came = swapped(jnp.where(is_first, dense_sum_two, dense_sum_one))
    dense_own, *came = lax.optimization_barrier((dense_own, *came))
    query_out, key_out, value_out, outproj_out, tail = unpack_dense(
        words, dense_own, dense_came, width
    )
    rel_out = tail[:, 2 + experts : 2 + experts + rel_cols].reshape(rel_bias.shape)
    first_out, second_out = join_experts(words, sums_one, sums_two, came)
    out_shape = (1, held, 1, rows, width)
    return (
        activations.reshape(out_shape),
        grads_in.reshape(out_shape),
        tail[:, 0][None],
        query_out[None],
        key_out[None],
        value_out[None],
        outproj_out[None],
        rel_out,
        tail[:, 1][None],
        tail[:, 2 : 2 + experts][None],
        first_out[None],
        second_out[None],
    )


def solution(mesh):
    rows_spec = P("section", ("ctx", "exp"), None)
    gain_spec = P("section", ("ctx", "exp"))
    expert_spec = P("section", "exp", "ctx", None)
    token_spec = P(None, "exp", "ctx", None)
    state_spec = P("section", None, "exp", "ctx", None)
    in_specs = (
        token_spec,
        token_spec,
        P(None, "exp", None),
        P(),
        token_spec,
        gain_spec,
        *[rows_spec] * 5,
        gain_spec,
        rows_spec,
        *[expert_spec] * 2,
    )
    out_specs = (
        *[state_spec] * 2,
        gain_spec,
        *[rows_spec] * 5,
        gain_spec,
        rows_spec,
        *[expert_spec] * 2,
    )
    return jax.shard_map(body, mesh=mesh, in_specs=in_specs, out_specs=out_specs, check_vma=False)
```

time: 2180 us -> 640 us (0.29)
  waiting for transfers between devices: 760 us -> 215 us
  local copies, waits for them, and re-layouts: 563 us -> 95.7 us
  blocking collectives: 344 us -> 0 us
  matrix products: 335 us -> 19.6 us
  Pallas kernels: 0 us -> 108 us
  starting transfers between devices: 59.6 us -> 133 us
  other arithmetic: 86.6 us -> 40.8 us
    reduce_scatter x6 -> x4, waiting for transfers between devices: 627 us -> 0.01 us  [summed_shards(): lax.psum_scatter(one, 'ctx', scatter_dimension=0, tiled=True)]
    gather x17 -> x0, local copies, waits for them, and re-layouts: 418 us -> none  [the longest x2 408 us: bias_terms(): jnp.take(buckets, jnp.clip(distance, 0, buckets.shape[0] - 1))]
    dot_general x100 -> x19, matrix products: 335 us -> 19.6 us  [the longest x11 11.7 us: dot_wide(): return jnp.dot(left, right, preferred_element_type=WIDE)]
    all_gather x14 -> x0, blocking collectives: 228 us -> none  [the longest x1 47.9 us: body(): lax.all_gather(w_router[0].astype(low_type), ('ctx', 'exp'), axis=0, tile...]
    ppermute x4 -> x68, waiting for transfers between devices: 3.64 us -> 163 us  [the longest x47 137 us: crossed(): lax.ppermute(block, axis, [(i, i ^ bits) for i in range(lax.axis_size(axi...]
    unnamed x2 -> x0, blocking collectives: 116 us -> none
    pallas_call x0 -> x33, Pallas kernels: none -> 108 us  [the longest x2 25 us: expert_call(): pl.pallas_call(kernel, out_shape=(*shapes, *(grads if with_grads else [])...]
    unnamed x26 -> x8, waiting for transfers between devices: 80.5 us -> 1.98 us
  transfers between devices with their start and end apart: 35 -> 84, of which waited for: 20 -> 37; matrix products, arithmetic and copies ran while one was open for 35% -> 14% of each run, Pallas kernels for 0% -> 12%
where the time goes in v1:
time: 640 us; the launch traced here: 629 us
  waiting for transfers between devices  215 us (34%)
  starting transfers between devices  133 us (21%)
  Pallas kernels  108 us (17%)
  local copies, waits for them, and re-layouts  95.7 us (15%)
  other arithmetic  40.8 us (6%)
  matrix products  19.6 us (3%)
  between operations  16.8 us (3%)
    ppermute x47, waiting for transfers between devices, crossed(): lax.ppermute(block, axis, [(i, i ^ bits) for i in range(lax.axis_size(axi...  137 us
    ppermute x47, starting transfers between devices, crossed(): lax.ppermute(block, axis, [(i, i ^ bits) for i in range(lax.axis_size(axi...  66.6 us
    unnamed x390, local copies, waits for them, and re-layouts  65.9 us
    all_to_all x8, starting transfers between devices, to_experts(): lax.all_to_all(rows_out.reshape(exp_count, held * capacity, lanes), 'exp'...  44.5 us
    all_to_all x8, waiting for transfers between devices, to_experts(): lax.all_to_all(rows_out.reshape(exp_count, held * capacity, lanes), 'exp'...  33.3 us
    pallas_call x2, Pallas kernels, expert_call(): pl.pallas_call(kernel, out_shape=(*shapes, *(grads if with_grads else [])...  25 us
    ppermute x4, waiting for transfers between devices, shifted(): return lax.ppermute(block, 'ctx', route)  20.7 us
    pallas_call x8, Pallas kernels, local_call(): pl.pallas_call(kernel, grid=(1,), out_shape=shapes, in_specs=[whole(one)...  17.1 us
  transfers between devices with their start and end apart: 84, of which 37 were waited for; matrix products, arithmetic and copies ran while one was open for 14% of the time, Pallas kernels for 12%

profile of v1, /device:TPU:0, one launch (start us, length us, event | category | flops | bytes accessed | tf_op | source)
XLA Modules:
  0.0 628.7 jit_solution(118949215760229309)
XLA Ops:
  7.3 4.2 shard_map.238
  28.1 3.6 collective-permute-start.4
  36.5 5.6 collective-permute-done.3.refs_2_
  43.3 5.6 collective-permute-done.8.refs_3_
  52.1 9.1 %collective-permute-done.9.refs_1_ = bf16[192,1280]{1,0:T(8,128)(2,1)S(1)} collective-permute-done((bf16[192,1280]{1,0:T(8,128)(2,1)S(1)}, bf16[192,1280]{1,0:T(8,128)(2,1)S(1)}, u32[]{:S(2)}, u32[]{:S(2)}) %collective-permute-start.9) | collective-permute-done | bytes 491552 | tf_op jit(solution)/shard_map/ppermute | solution.py:28
  66.7 3.5 collective-permute-start.14
  76.9 11.1 %collective-permute-done.11.refs_3_ = bf16[192,1280]{1,0:T(8,128)(2,1)S(1)} collective-permute-done((bf16[192,1280]{1,0:T(8,128)(2,1)S(1)}, bf16[192,1280]{1,0:T(8,128)(2,1)S(1)}, u32[]{:S(2)}, u32[]{:S(2)}) %collective-permute-start.11) | collective-permute-done | bytes 491552 | tf_op jit(solution)/shard_map/ppermute | solution.py:28
  98.6 3.9 collective-permute-start.16
  121.4 4.7 collective-permute-done.21.refs_3_
  131.3 3.1 shard_map.245
  141.1 4.1 all-to-all-start
  151.6 8.3 %all-to-all-done = bf16[4,80,768]{2,1,0:T(8,128)(2,1)} async-done(((bf16[4,80,768]{2,1,0:T(8,128)(2,1)}), bf16[4,80,768]{2,1,0:T(8,128)(2,1)}, u32[]{:S(2)}, u32[]{:S(2)}) %all-to-all-start) | async-done | bytes 491552 | tf_op jit(solution)/shard_map/all_to_all | solution.py:1014
  163.1 7.5 %shard_map.248 = (bf16[320,768]{1,0:T(8,128)(2,1)S(1)}, f32[4,320,768]{2,1,0:T(8,128)S(1)}) custom-call(bf16[320,768]{1,0:T(8,128)(2,1)} %bitcast.33.x_ref, bf16[768,3072]{1,0:T(8,128)(2,1)} %all-gather.5.cloned.1.call-done.first_hbm, bf16[3072,768]{1,0:T(8,128)(2,1)} %all-gather.7.cloned.1.call-done.second_hbm), custom_call_target="tpu_custom_call" | custom-call | tf_op jit(solution)/shard_map/pallas_call | solution.py:552
  173.3 4.7 collective-permute-done.26.refs_3_
  178.1 12.6 %all-to-all-start.1 = ((bf16[4,80,768]{2,1,0:T(8,128)(2,1)}), bf16[4,80,768]{2,1,0:T(8,128)(2,1)S(1)}, u32[]{:S(2)}, u32[]{:S(2)}) async-start(bf16[4,80,768]{2,1,0:T(8,128)(2,1)} %bitcast.177), calls=%async_computation.1 | async-start | bytes 983040 | tf_op jit(solution)/shard_map/all_to_all | solution.py:1014
  193.3 10.0 %all-to-all-done.1 = bf16[4,80,768]{2,1,0:T(8,128)(2,1)S(1)} async-done(((bf16[4,80,768]{2,1,0:T(8,128)(2,1)}), bf16[4,80,768]{2,1,0:T(8,128)(2,1)S(1)}, u32[]{:S(2)}, u32[]{:S(2)}) %all-to-all-start.1) | async-done | bytes 491552 | tf_op jit(solution)/shard_map/all_to_all | solution.py:1014
  205.9 3.2 shard_map.249
  213.0 3.2 collective-permute-start.28
  222.0 5.9 collective-permute-done.28.refs_2_
  228.9 3.8 shard_map.251
  236.8 4.8 all-to-all-start.2
  256.8 5.1 all-to-all-start.3
  261.9 8.5 %reduce-scatter.5.cloned.1.call-start = ((), (), s32[]{:S(2)}) async-start(), calls=%async_computation.16 | async-start | bytes 5898240 | tf_op jit(solution)/shard_map/reduce_scatter | solution.py:1172
  270.4 16.3 %all-gather.9.cloned.1.call-done.refs_0_ = bf16[768,3072]{1,0:T(8,128)(2,1)} async-done(((bf16[192,3072]{1,0:T(8,128)(2,1)}), bf16[768,3072]{1,0:T(8,128)(2,1)}) %all-gather.9.cloned.1.call-update) | async-done | bytes 4718608 | tf_op jit(solution)/shard_map/all_gather | solution.py:951
  286.8 17.5 %shard_map.253 = (bf16[320,768]{1,0:T(8,128)(2,1)S(1)}, bf16[320,896]{1,0:T(8,128)(2,1)S(1)}, bf16[768,3072]{1,0:T(8,128)(2,1)}, bf16[3072,768]{1,0:T(8,128)(2,1)}) custom-call(bf16[320,896]{1,0:T(8,128)(2,1)} %bitcast.45.x_ref, bf16[320,768]{1,0:T(8,128)(2,1)} %bitcast.43.cot_ref, bf16[768,3072]{1,0:T(8,128)(2,1)} %all-gather.9.cloned.1.call-done.refs_0_, ...), custom_call_target="tpu_custom_call" | custom-call | tf_op jit(solution)/shard_map/pallas_call | solution.py:552
  306.6 4.6 all-to-all-start.4
  312.6 14.2 %all-to-all-done.4 = bf16[4,80,896]{2,1,0:T(8,128)(2,1)} async-done(((bf16[4,80,896]{2,1,0:T(8,128)(2,1)}), bf16[4,80,896]{2,1,0:T(8,128)(2,1)}, u32[]{:S(2)}, u32[]{:S(2)}) %all-to-all-start.4) | async-done | bytes 573472 | tf_op jit(solution)/shard_map/all_to_all | solution.py:1014
  333.3 3.2 shard_map.255
  339.5 4.1 all-to-all-start.6
  348.7 5.1 shard_map.256
  355.3 14.7 %collective-permute-done.33.refs_2_ = bf16[256,768]{1,0:T(8,128)(2,1)S(1)} collective-permute-done((bf16[256,768]{1,0:T(8,128)(2,1)S(1)}, bf16[256,768]{1,0:T(8,128)(2,1)S(1)}, u32[]{:S(2)}, u32[]{:S(2)}) %collective-permute-start.33) | collective-permute-done | bytes 393248 | tf_op jit(solution)/shard_map/ppermute | solution.py:24
  384.3 4.7 all-to-all-start.5
  405.1 4.0 shard_map.260
  412.0 12.4 %shard_map.261 = (bf16[320,768]{1,0:T(8,128)(2,1)}, bf16[768,3072]{1,0:T(8,128)(2,1)}) custom-call(bf16[320,768]{1,0:T(8,128)(2,1)} %bitcast.33.x_ref, bf16[320,768]{1,0:T(8,128)(2,1)S(1)} %bitcast.168, f32[4,320,768]{2,1,0:T(8,128)S(1)} %copy-done.4, bf16[768,3072]{1,0:T(8,128)(2,1)} %all-gather.5.cloned.1.call-done.first_hbm, ...), custom_call_target="tpu_custom_call" | custom-call | tf_op jit(solution)/shard_map/pallas_call | solution.py:602
  425.3 4.3 all-to-all-start.7
  436.2 4.8 collective-permute-done.37
  447.5 14.8 %collective-permute-done.43 = bf16[192,768]{1,0:T(8,128)(2,1)} collective-permute-done((bf16[192,768]{1,0:T(8,128)(2,1)}, bf16[192,768]{1,0:T(8,128)(2,1)}, u32[]{:S(2)}, u32[]{:S(2)}) %collective-permute-start.43) | collective-permute-done | bytes 294944 | tf_op jit(solution)/shard_map/ppermute | solution.py:28
  468.0 3.6 shard_map.263
  474.1 5.3 shard_map.264
  491.4 30.5 %collective-permute-done.45 = bf16[48,768]{1,0:T(8,128)(2,1)S(1)} collective-permute-done((bf16[48,768]{1,0:T(8,128)(2,1)}, bf16[48,768]{1,0:T(8,128)(2,1)S(1)}, u32[]{:S(2)}, u32[]{:S(2)}) %collective-permute-start.45) | collective-permute-done | bytes 73760 | tf_op jit(solution)/shard_map/ppermute | solution.py:28
  539.5 3.0 collective-permute-start.57
  545.4 8.2 %collective-permute-done.51 = bf16[192,768]{1,0:T(8,128)(2,1)S(1)} collective-permute-done((bf16[192,768]{1,0:T(8,128)(2,1)S(1)}, bf16[192,768]{1,0:T(8,128)(2,1)S(1)}, u32[]{:S(2)}, u32[]{:S(2)}) %collective-permute-start.51) | collective-permute-done | bytes 294944 | tf_op jit(solution)/shard_map/ppermute | solution.py:28
  557.4 8.8 %collective-permute-done.57 = bf16[4,48,896]{2,1,0:T(8,128)(2,1)S(1)} collective-permute-done((bf16[4,48,896]{2,1,0:T(8,128)(2,1)S(1)}, bf16[4,48,896]{2,1,0:T(8,128)(2,1)S(1)}, u32[]{:S(2)}, u32[]{:S(2)}) %collective-permute-start.57) | collective-permute-done | bytes 344096 | tf_op jit(solution)/shard_map/ppermute | solution.py:28
  579.1 6.0 collective-permute-start.53
  588.2 4.0 collective-permute-done.55
  594.6 5.1 collective-permute-done.36
  600.6 6.0 collective-permute-done.49
  616.0 5.6 shard_map.270
  (716 shorter events, 264.5 us)
Async XLA Ops:
  7.2 155.8 %all-gather.5.cloned.1.call-start = ((), (), s32[]{:S(2)}) async-start(), calls=%async_computation.12 | async-start | bytes 5898240 | tf_op jit(solution)/shard_map/all_gather | solution.py:951
  20.3 142.8 %all-gather.7.cloned.1.call-start = ((), (), s32[]{:S(2)}) async-start(), calls=%async_computation.13 | async-start | bytes 5898240 | tf_op jit(solution)/shard_map/all_gather | solution.py:951
  34.0 14.9 %collective-permute-start.8 = (bf16[48,1664]{1,0:T(8,128)(2,1)S(1)}, bf16[48,1664]{1,0:T(8,128)(2,1)S(1)}, u32[]{:S(2)}, u32[]{:S(2)}) collective-permute-start(bf16[48,1664]{1,0:T(8,128)(2,1)S(1)} %collective-permute-done.6.refs_1_), channel_id=1, source_target_pairs={{0,8},{4,12},{8,0},{12,4},{1,9},{5,13},{9,1},{13,5},{2,10},{6,14},... | collective-permute-start | bytes 479240 | tf_op jit(solution)/shard_map/ppermute | solution.py:28
  36.1 28.4 %collective-permute-start.23 = (s32[128,2]{0,1:T(2,128)S(1)}, s32[128,2]{0,1:T(2,128)S(1)}, u32[]{:S(2)}, u32[]{:S(2)}) collective-permute-start(s32[128,2]{0,1:T(2,128)S(1)} %get-tuple-element.333), channel_id=1, source_target_pairs={{0,4},{4,0},{8,12},{12,8},{1,5},{5,1},{9,13},{13,9},{2,6},{6,2},{1... | collective-permute-start | bytes 3080 | tf_op jit(solution)/shard_map/ppermute | solution.py:28
  42.1 22.7 %collective-permute-start = (bf16[128,768]{1,0:T(8,128)(2,1)}, bf16[128,768]{1,0:T(8,128)(2,1)S(1)}, u32[]{:S(2)}, u32[]{:S(2)}) collective-permute-start(bf16[128,768]{1,0:T(8,128)(2,1)} %get-tuple-element.310), channel_id=1, source_target_pairs={{0,4},{4,0},{8,12},{12,8},{1,5},{5,1},{9,13},{13,9},{2,6},{6,2},{1... | collective-permute-start | bytes 589832 | tf_op jit(solution)/shard_map/ppermute | solution.py:28
  50.0 26.1 %collective-permute-start.10 = (bf16[192,1280]{1,0:T(8,128)(2,1)S(1)}, bf16[192,1280]{1,0:T(8,128)(2,1)S(1)}, u32[]{:S(2)}, u32[]{:S(2)}) collective-permute-start(bf16[192,1280]{1,0:T(8,128)(2,1)S(1)} %shard_map.240.refs_0_), channel_id=1, source_target_pairs={{0,8},{4,12},{8,0},{12,4},{1,9},{5,13},{9,1},{13,5},{2,10},{6,14},... | collective-permute-start | bytes 1474568 | tf_op jit(solution)/shard_map/ppermute | solution.py:28
  61.2 26.8 %collective-permute-start.11 = (bf16[192,1280]{1,0:T(8,128)(2,1)S(1)}, bf16[192,1280]{1,0:T(8,128)(2,1)S(1)}, u32[]{:S(2)}, u32[]{:S(2)}) collective-permute-start(bf16[192,1280]{1,0:T(8,128)(2,1)S(1)} %collective-permute-done.9.refs_1_), channel_id=1, source_target_pairs={{0,8},{4,12},{8,0},{12,4},{1,9},{5,13},{9,1},{13,5},{2,10},{6,14},... | collective-permute-start | bytes 1474568 | tf_op jit(solution)/shard_map/ppermute | solution.py:28
  72.7 24.3 %collective-permute-start.15 = (bf16[192,1664]{1,0:T(8,128)(2,1)S(1)}, bf16[192,1664]{1,0:T(8,128)(2,1)S(1)}, u32[]{:S(2)}, u32[]{:S(2)}) collective-permute-start(bf16[192,1664]{1,0:T(8,128)(2,1)S(1)} %shard_map.241.refs_0_), channel_id=1, source_target_pairs={{0,1},{1,0},{2,3},{3,2},{4,5},{5,4},{6,7},{7,6},{8,9},{9,8},{10,11... | collective-permute-start | bytes 1916936 | tf_op jit(solution)/shard_map/ppermute | solution.py:28
  98.6 14.6 %collective-permute-start.16 = (bf16[256,768]{1,0:T(8,128)(2,1)S(1)}, bf16[256,768]{1,0:T(8,128)(2,1)}, u32[]{:S(2)}, u32[]{:S(2)}) collective-permute-start(bf16[256,768]{1,0:T(8,128)(2,1)S(1)} %slice.167.refs_1_), channel_id=1, source_target_pairs={{0,8},{4,12},{1,9},{5,13},{2,10},{6,14},{3,11},{7,15},{16,24},{20,... | collective-permute-start | bytes 1179656 | tf_op jit(solution)/shard_map/ppermute | solution.py:24
  105.3 29.1 %collective-permute-start.17 = (bf16[192,1664]{1,0:T(8,128)(2,1)S(1)}, bf16[192,1664]{1,0:T(8,128)(2,1)}, u32[]{:S(2)}, u32[]{:S(2)}) collective-permute-start(bf16[192,1664]{1,0:T(8,128)(2,1)S(1)} %shard_map.241.refs_0_), channel_id=1, source_target_pairs={{0,2},{1,3},{2,0},{3,1},{4,6},{5,7},{6,4},{7,5},{8,10},{9,11},{10,... | collective-permute-start | bytes 1916936 | tf_op jit(solution)/shard_map/ppermute | solution.py:28
  141.1 18.8 %all-to-all-start = ((bf16[4,80,768]{2,1,0:T(8,128)(2,1)}), bf16[4,80,768]{2,1,0:T(8,128)(2,1)}, u32[]{:S(2)}, u32[]{:S(2)}) async-start(bf16[4,80,768]{2,1,0:T(8,128)(2,1)} %bitcast.192), calls=%async_computation | async-start | bytes 983040 | tf_op jit(solution)/shard_map/all_to_all | solution.py:1014
  145.3 125.2 %all-gather.11.cloned.1.call-start = ((), (), s32[]{:S(2)}) async-start(), calls=%async_computation.15 | async-start | bytes 5898240 | tf_op jit(solution)/shard_map/all_gather | solution.py:951
  159.9 18.1 %collective-permute-start.26 = (bf16[192,1664]{1,0:T(8,128)(2,1)}, bf16[192,1664]{1,0:T(8,128)(2,1)}, u32[]{:S(2)}, u32[]{:S(2)}) collective-permute-start(bf16[192,1664]{1,0:T(8,128)(2,1)} %copy-done.69), channel_id=1, source_target_pairs={{0,3},{1,2},{2,1},{3,0},{4,7},{5,6},{6,5},{7,4},{8,11},{9,10},{10,... | collective-permute-start | bytes 1916936 | tf_op jit(solution)/shard_map/ppermute | solution.py:28
  178.1 25.2 %all-to-all-start.1 = ((bf16[4,80,768]{2,1,0:T(8,128)(2,1)}), bf16[4,80,768]{2,1,0:T(8,128)(2,1)S(1)}, u32[]{:S(2)}, u32[]{:S(2)}) async-start(bf16[4,80,768]{2,1,0:T(8,128)(2,1)} %bitcast.177), calls=%async_computation.1 | async-start | bytes 983040 | tf_op jit(solution)/shard_map/all_to_all | solution.py:1014
  190.7 96.1 %all-gather.9.cloned.1.call-start = ((), (), s32[]{:S(2)}) async-start(), calls=%async_computation.14 | async-start | bytes 5898240 | tf_op jit(solution)/shard_map/all_gather | solution.py:951
  213.0 15.0 %collective-permute-start.28 = (bf16[256,768]{1,0:T(8,128)(2,1)}, bf16[256,768]{1,0:T(8,128)(2,1)}, u32[]{:S(2)}, u32[]{:S(2)}) collective-permute-start(bf16[256,768]{1,0:T(8,128)(2,1)} %slice.179.refs_1_), channel_id=1, source_target_pairs={{0,8},{4,12},{1,9},{5,13},{2,10},{6,14},{3,11},{7,15},{16,24},{20,... | collective-permute-start | bytes 1179656 | tf_op jit(solution)/shard_map/ppermute | solution.py:24
  218.0 15.9 %collective-permute-start.30 = (bf16[768,384]{1,0:T(8,128)(2,1)}, bf16[768,384]{1,0:T(8,128)(2,1)}, u32[]{:S(2)}, u32[]{:S(2)}) collective-permute-start(bf16[768,384]{1,0:T(8,128)(2,1)} %slice.181), channel_id=1, source_target_pairs={{0,16},{16,0},{1,17},{17,1},{2,18},{18,2},{3,19},{19,3},{4,20},{20... | collective-permute-start | bytes 1769480 | tf_op jit(solution)/shard_map/ppermute | solution.py:18
  236.8 20.0 %all-to-all-start.2 = ((bf16[4,80,768]{2,1,0:T(8,128)(2,1)}), bf16[4,80,768]{2,1,0:T(8,128)(2,1)}, u32[]{:S(2)}, u32[]{:S(2)}) async-start(bf16[4,80,768]{2,1,0:T(8,128)(2,1)} %bitcast.191), calls=%async_computation.2 | async-start | bytes 983040 | tf_op jit(solution)/shard_map/all_to_all | solution.py:1014
  256.8 30.0 %all-to-all-start.3 = ((bf16[4,80,896]{2,1,0:T(8,128)(2,1)}), bf16[4,80,896]{2,1,0:T(8,128)(2,1)}, u32[]{:S(2)}, u32[]{:S(2)}) async-start(bf16[4,80,896]{2,1,0:T(8,128)(2,1)} %bitcast.190), calls=%async_computation.3 | async-start | bytes 1146880 | tf_op jit(solution)/shard_map/all_to_all | solution.py:1014
  261.9 311.2 %reduce-scatter.5.cloned.1.call-start = ((), (), s32[]{:S(2)}) async-start(), calls=%async_computation.16 | async-start | bytes 5898240 | tf_op jit(solution)/shard_map/reduce_scatter | solution.py:1172
  306.0 267.1 %reduce-scatter.7.cloned.1.call-start = ((), (), s32[]{:S(2)}) async-start(), calls=%async_computation.17 | async-start | bytes 5898240 | tf_op jit(solution)/shard_map/reduce_scatter | solution.py:1172
  306.6 20.3 %all-to-all-start.4 = ((bf16[4,80,896]{2,1,0:T(8,128)(2,1)}), bf16[4,80,896]{2,1,0:T(8,128)(2,1)}, u32[]{:S(2)}, u32[]{:S(2)}) async-start(bf16[4,80,896]{2,1,0:T(8,128)(2,1)} %bitcast.174), calls=%async_computation.4 | async-start | bytes 1146880 | tf_op jit(solution)/shard_map/all_to_all | solution.py:1014
  339.5 32.9 %all-to-all-start.6 = ((bf16[4,80,768]{2,1,0:T(8,128)(2,1)}), bf16[4,80,768]{2,1,0:T(8,128)(2,1)}, u32[]{:S(2)}, u32[]{:S(2)}) async-start(bf16[4,80,768]{2,1,0:T(8,128)(2,1)} %bitcast.175), calls=%async_computation.6 | async-start | bytes 983040 | tf_op jit(solution)/shard_map/all_to_all | solution.py:1014
  353.8 16.2 %collective-permute-start.33 = (bf16[256,768]{1,0:T(8,128)(2,1)S(1)}, bf16[256,768]{1,0:T(8,128)(2,1)S(1)}, u32[]{:S(2)}, u32[]{:S(2)}) collective-permute-start(bf16[256,768]{1,0:T(8,128)(2,1)S(1)} %get-tuple-element.151), channel_id=1, source_target_pairs={{8,0},{12,4},{9,1},{13,5},{10,2},{14,6},{11,3},{15,7},{24,16},{28,... | collective-permute-start | bytes 1179656 | tf_op jit(solution)/shard_map/ppermute | solution.py:24
  376.6 23.2 %collective-permute-start.35 = (f32[256,768]{1,0:T(8,128)}, f32[256,768]{1,0:T(8,128)}, u32[]{:S(2)}, u32[]{:S(2)}) collective-permute-start(f32[256,768]{1,0:T(8,128)} %fusion), channel_id=1, source_target_pairs={{0,16},{16,0},{1,17},{17,1},{2,18},{18,2},{3,19},{19,3},{4,20},{20... | collective-permute-start | bytes 2359304 | tf_op jit(solution)/shard_map/ppermute | solution.py:18
  384.3 18.7 %all-to-all-start.5 = ((bf16[4,80,768]{2,1,0:T(8,128)(2,1)}), bf16[4,80,768]{2,1,0:T(8,128)(2,1)S(1)}, u32[]{:S(2)}, u32[]{:S(2)}) async-start(bf16[4,80,768]{2,1,0:T(8,128)(2,1)} %bitcast.176), calls=%async_computation.5 | async-start | bytes 983040 | tf_op jit(solution)/shard_map/all_to_all | solution.py:1014
  389.0 184.0 %reduce-scatter.9.cloned.1.call-start = ((), (), s32[]{:S(2)}) async-start(), calls=%async_computation.18 | async-start | bytes 5898240 | tf_op jit(solution)/shard_map/reduce_scatter | solution.py:1172
  424.4 148.6 %reduce-scatter.11.cloned.1.call-start = ((), (), s32[]{:S(2)}) async-start(), calls=%async_computation.19 | async-start | bytes 5898240 | tf_op jit(solution)/shard_map/reduce_scatter | solution.py:1172
  425.3 17.5 %all-to-all-start.7 = ((bf16[4,80,768]{2,1,0:T(8,128)(2,1)}), bf16[4,80,768]{2,1,0:T(8,128)(2,1)}, u32[]{:S(2)}, u32[]{:S(2)}) async-start(bf16[4,80,768]{2,1,0:T(8,128)(2,1)} %bitcast.56), calls=%async_computation.7 | async-start | bytes 983040 | tf_op jit(solution)/shard_map/all_to_all | solution.py:1014
  445.8 22.1 %collective-permute-start.39 = (f32[256,896]{1,0:T(8,128)S(1)}, f32[256,896]{1,0:T(8,128)}, u32[]{:S(2)}, u32[]{:S(2)}) collective-permute-start(f32[256,896]{1,0:T(8,128)S(1)} %shard_map.262.refs_0_), channel_id=1, source_target_pairs={{0,16},{16,0},{1,17},{17,1},{2,18},{18,2},{3,19},{19,3},{4,20},{20... | collective-permute-start | bytes 2752520 | tf_op jit(solution)/shard_map/ppermute | solution.py:18
  445.9 16.4 %collective-permute-start.43 = (bf16[192,768]{1,0:T(8,128)(2,1)}, bf16[192,768]{1,0:T(8,128)(2,1)}, u32[]{:S(2)}, u32[]{:S(2)}) collective-permute-start(bf16[192,768]{1,0:T(8,128)(2,1)} %add_convert_fusion.5), channel_id=1, source_target_pairs={{0,4},{4,0},{8,12},{12,8},{1,5},{5,1},{9,13},{13,9},{2,6},{6,2},{1... | collective-permute-start | bytes 884744 | tf_op jit(solution)/shard_map/ppermute | solution.py:28
  464.2 23.3 %collective-permute-start.44 = (bf16[48,768]{1,0:T(8,128)(2,1)S(1)}, bf16[48,768]{1,0:T(8,128)(2,1)}, u32[]{:S(2)}, u32[]{:S(2)}) collective-permute-start(bf16[48,768]{1,0:T(8,128)(2,1)S(1)} %get-tuple-element.319), channel_id=1, source_target_pairs={{0,1},{1,0},{2,3},{3,2},{4,5},{5,4},{6,7},{7,6},{8,9},{9,8},{10,11... | collective-permute-start | bytes 221192 | tf_op jit(solution)/shard_map/ppermute | solution.py:28
  481.5 41.5 %collective-permute-start.47 = (bf16[256,768]{1,0:T(8,128)(2,1)}, bf16[256,768]{1,0:T(8,128)(2,1)S(1)}, u32[]{:S(2)}, u32[]{:S(2)}) collective-permute-start(bf16[256,768]{1,0:T(8,128)(2,1)} %get-tuple-element.189), channel_id=1, source_target_pairs={{8,0},{12,4},{9,1},{13,5},{10,2},{14,6},{11,3},{15,7},{24,16},{28,... | collective-permute-start | bytes 1179656 | tf_op jit(solution)/shard_map/ppermute | solution.py:24
  485.5 37.4 %collective-permute-start.40 = (bf16[4,48,896]{2,1,0:T(8,128)(2,1)}, bf16[4,48,896]{2,1,0:T(8,128)(2,1)S(1)}, u32[]{:S(2)}, u32[]{:S(2)}) collective-permute-start(bf16[4,48,896]{2,1,0:T(8,128)(2,1)} %get-tuple-element.182), channel_id=1, source_target_pairs={{0,1},{1,0},{2,3},{3,2},{4,5},{5,4},{6,7},{7,6},{8,9},{9,8},{10,11... | collective-permute-start | bytes 1032200 | tf_op jit(solution)/shard_map/ppermute | solution.py:28
  486.0 37.0 %collective-permute-start.41 = (bf16[4,48,896]{2,1,0:T(8,128)(2,1)}, bf16[4,48,896]{2,1,0:T(8,128)(2,1)S(1)}, u32[]{:S(2)}, u32[]{:S(2)}) collective-permute-start(bf16[4,48,896]{2,1,0:T(8,128)(2,1)} %get-tuple-element.183), channel_id=1, source_target_pairs={{0,2},{1,3},{2,0},{3,1},{4,6},{5,7},{6,4},{7,5},{8,10},{9,11},{10,... | collective-permute-start | bytes 1032200 | tf_op jit(solution)/shard_map/ppermute | solution.py:28
  487.5 35.5 %collective-permute-start.42 = (bf16[4,48,896]{2,1,0:T(8,128)(2,1)}, bf16[4,48,896]{2,1,0:T(8,128)(2,1)}, u32[]{:S(2)}, u32[]{:S(2)}) collective-permute-start(bf16[4,48,896]{2,1,0:T(8,128)(2,1)} %get-tuple-element.184), channel_id=1, source_target_pairs={{0,3},{1,2},{2,1},{3,0},{4,7},{5,6},{6,5},{7,4},{8,11},{9,10},{10,... | collective-permute-start | bytes 1032200 | tf_op jit(solution)/shard_map/ppermute | solution.py:28
  490.2 31.8 %collective-permute-start.45 = (bf16[48,768]{1,0:T(8,128)(2,1)}, bf16[48,768]{1,0:T(8,128)(2,1)S(1)}, u32[]{:S(2)}, u32[]{:S(2)}) collective-permute-start(bf16[48,768]{1,0:T(8,128)(2,1)} %get-tuple-element.321), channel_id=1, source_target_pairs={{0,2},{1,3},{2,0},{3,1},{4,6},{5,7},{6,4},{7,5},{8,10},{9,11},{10,... | collective-permute-start | bytes 221192 | tf_op jit(solution)/shard_map/ppermute | solution.py:28
  535.1 32.7 %collective-permute-start.62 = (bf16[48,896]{1,0:T(8,128)(2,1)S(1)}, bf16[48,896]{1,0:T(8,128)(2,1)S(1)}, u32[]{:S(2)}, u32[]{:S(2)}) collective-permute-start(bf16[48,896]{1,0:T(8,128)(2,1)S(1)} %get-tuple-element.314), channel_id=1, source_target_pairs={{0,8},{4,12},{8,0},{12,4},{1,9},{5,13},{9,1},{13,5},{2,10},{6,14},... | collective-permute-start | bytes 258056 | tf_op jit(solution)/shard_map/ppermute | solution.py:28
  537.5 16.1 %collective-permute-start.51 = (bf16[192,768]{1,0:T(8,128)(2,1)S(1)}, bf16[192,768]{1,0:T(8,128)(2,1)S(1)}, u32[]{:S(2)}, u32[]{:S(2)}) collective-permute-start(bf16[192,768]{1,0:T(8,128)(2,1)S(1)} %get-tuple-element.201), channel_id=1, source_target_pairs={{0,8},{4,12},{8,0},{12,4},{1,9},{5,13},{9,1},{13,5},{2,10},{6,14},... | collective-permute-start | bytes 884744 | tf_op jit(solution)/shard_map/ppermute | solution.py:28
  539.5 16.7 %collective-permute-start.56 = (bf16[4,48,896]{2,1,0:T(8,128)(2,1)S(1)}, bf16[4,48,896]{2,1,0:T(8,128)(2,1)S(1)}, u32[]{:S(2)}, u32[]{:S(2)}) collective-permute-start(bf16[4,48,896]{2,1,0:T(8,128)(2,1)S(1)} %get-tuple-element.203), channel_id=1, source_target_pairs={{0,1},{1,0},{2,3},{3,2},{4,5},{5,4},{6,7},{7,6},{8,9},{9,8},{10,11... | collective-permute-start | bytes 1032200 | tf_op jit(solution)/shard_map/ppermute | solution.py:28
  539.5 26.7 %collective-permute-start.57 = (bf16[4,48,896]{2,1,0:T(8,128)(2,1)S(1)}, bf16[4,48,896]{2,1,0:T(8,128)(2,1)S(1)}, u32[]{:S(2)}, u32[]{:S(2)}) collective-permute-start(bf16[4,48,896]{2,1,0:T(8,128)(2,1)S(1)} %get-tuple-element.204), channel_id=1, source_target_pairs={{0,2},{1,3},{2,0},{3,1},{4,6},{5,7},{6,4},{7,5},{8,10},{9,11},{10,... | collective-permute-start | bytes 1032200 | tf_op jit(solution)/shard_map/ppermute | solution.py:28
  543.5 23.9 %collective-permute-start.58 = (bf16[4,48,896]{2,1,0:T(8,128)(2,1)S(1)}, bf16[4,48,896]{2,1,0:T(8,128)(2,1)S(1)}, u32[]{:S(2)}, u32[]{:S(2)}) collective-permute-start(bf16[4,48,896]{2,1,0:T(8,128)(2,1)S(1)} %get-tuple-element.205), channel_id=1, source_target_pairs={{0,3},{1,2},{2,1},{3,0},{4,7},{5,6},{6,5},{7,4},{8,11},{9,10},{10,... | collective-permute-start | bytes 1032200 | tf_op jit(solution)/shard_map/ppermute | solution.py:28
  553.6 24.8 %collective-permute-start.50 = (bf16[192,768]{1,0:T(8,128)(2,1)S(1)}, bf16[192,768]{1,0:T(8,128)(2,1)S(1)}, u32[]{:S(2)}, u32[]{:S(2)}) collective-permute-start(bf16[192,768]{1,0:T(8,128)(2,1)S(1)} %get-tuple-element.199), channel_id=1, source_target_pairs={{0,8},{4,12},{8,0},{12,4},{1,9},{5,13},{9,1},{13,5},{2,10},{6,14},... | collective-permute-start | bytes 884744 | tf_op jit(solution)/shard_map/ppermute | solution.py:28
  567.8 17.2 %collective-permute-start.59 = (bf16[48,896]{1,0:T(8,128)(2,1)S(1)}, bf16[48,896]{1,0:T(8,128)(2,1)S(1)}, u32[]{:S(2)}, u32[]{:S(2)}) collective-permute-start(bf16[48,896]{1,0:T(8,128)(2,1)S(1)} %get-tuple-element.312), channel_id=1, source_target_pairs={{0,8},{4,12},{8,0},{12,4},{1,9},{5,13},{9,1},{13,5},{2,10},{6,14},... | collective-permute-start | bytes 258056 | tf_op jit(solution)/shard_map/ppermute | solution.py:28
  572.3 15.1 %collective-permute-start.61 = (bf16[48,896]{1,0:T(8,128)(2,1)S(1)}, bf16[48,896]{1,0:T(8,128)(2,1)S(1)}, u32[]{:S(2)}, u32[]{:S(2)}) collective-permute-start(bf16[48,896]{1,0:T(8,128)(2,1)S(1)} %fusion.27), channel_id=1, source_target_pairs={{0,4},{4,0},{8,12},{12,8},{1,5},{5,1},{9,13},{13,9},{2,6},{6,2},{1... | collective-permute-start | bytes 258056 | tf_op jit(solution)/shard_map/ppermute | solution.py:28
  578.3 29.2 %collective-permute-start.65 = (bf16[192,3072]{1,0:T(8,128)(2,1)S(1)}, bf16[192,3072]{1,0:T(8,128)(2,1)S(1)}, u32[]{:S(2)}, u32[]{:S(2)}) collective-permute-start(bf16[192,3072]{1,0:T(8,128)(2,1)S(1)} %get-tuple-element.212), channel_id=1, source_target_pairs={{0,16},{16,0},{1,17},{17,1},{2,18},{18,2},{3,19},{19,3},{4,20},{20... | collective-permute-start | bytes 3538952 | tf_op jit(solution)/shard_map/ppermute | solution.py:18
  578.4 30.2 %collective-permute-start.66 = (bf16[768,768]{1,0:T(8,128)(2,1)S(1)}, bf16[768,768]{1,0:T(8,128)(2,1)S(1)}, u32[]{:S(2)}, u32[]{:S(2)}) collective-permute-start(bf16[768,768]{1,0:T(8,128)(2,1)S(1)} %get-tuple-element.213), channel_id=1, source_target_pairs={{0,16},{16,0},{1,17},{17,1},{2,18},{18,2},{3,19},{19,3},{4,20},{20... | collective-permute-start | bytes 3538952 | tf_op jit(solution)/shard_map/ppermute | solution.py:18
  592.1 14.5 %collective-permute-start.49 = (f32[128,768]{1,0:T(8,128)}, f32[128,768]{1,0:T(8,128)S(1)}, u32[]{:S(2)}, u32[]{:S(2)}) collective-permute-start(f32[128,768]{1,0:T(8,128)} %get-tuple-element.303), channel_id=1, source_target_pairs={{0,4},{4,0},{8,12},{12,8},{1,5},{5,1},{9,13},{13,9},{2,6},{6,2},{1... | collective-permute-start | bytes 1179656 | tf_op jit(solution)/shard_map/ppermute | solution.py:28
  (229 other events, 1749.1 us)
Sparse Core Ops, SparseCore 0:
  20.4 79.8 all-gather.4
  102.2 60.9 all-gather.6
  164.9 61.1 all-gather.10
  228.4 58.3 all-gather.8
  306.1 60.0 reduce-scatter.4
  369.6 56.8 reduce-scatter.6
  429.5 68.5 reduce-scatter.8
  501.1 66.8 reduce-scatter.10

commit v2 on v1

--- a/solution.py
+++ b/solution.py
@@ -1235,13 +1235,12 @@
     sums_one = summed_shards([first_grads]) + sums_one
     activations = regrouped(jnp.where(is_first, out_one, out_two).reshape(held, rows, width))
     grad_sent = to_experts(grad_rows)
-    late_two, early_two = [], []
+    late_two = []
     if relayed:
         grad_sent, early_hop = lax.optimization_barrier((grad_sent, early_hop))
         late_two = sent_along_exp([tied(one, grad_sent) for one in late_parts])
-        early_two = [finished_along_exp(last_hop(early_hop, 1))]
     grad_one, grads_of_one, grad_qkv, _, _ = backward_from_experts(
-        grad_out, grad_sent, returned_one, dense_one, kept_one, None, [*late_two, *early_two]
+        grad_out, grad_sent, returned_one, dense_one, kept_one, None, late_two
     )
     came = [swapped(one) for one in chosen_by_core(words, sums_two, sums_one)]
     if relayed:
@@ -1250,11 +1249,13 @@
         late_two = [tied(one, late_parts[0]) for one in late_two]
         late_one = sent_along_exp(late_parts)
         early_one = over_ctx(early_parts)
+        early_hop = [tied(one, late_one[0]) for one in early_hop]
+        early_two = finished_along_exp(last_hop(early_hop, 1))
         dense_sum_one = jnp.concatenate(
             [finished_along_exp(early_one), finished_along_ctx(late_parts, late_one)], axis=1
         )
         dense_sum_two = jnp.concatenate(
-            [early_two[0], finished_along_ctx(late_parts_two, late_two)], axis=1
+            [early_two, finished_along_ctx(late_parts_two, late_two)], axis=1
         )
     else:
         dense_sum_two = whole_dense_grads(*grads_of_two)

time: 640 us -> 639 us (level)
    reduce_scatter x4, waiting for transfers between devices: 0.01 us -> 10.4 us  [summed_shards(): lax.psum_scatter(one, 'ctx', scatter_dimension=0, tiled=True)]
    ppermute x47, waiting for transfers between devices: 137 us -> 127 us  [crossed(): lax.ppermute(block, axis, [(i, i ^ bits) for i in range(lax.axis_size(axi...]
    unnamed x390 -> x386, local copies, waits for them, and re-layouts: 65.9 us -> 70.3 us
  transfers between devices with their start and end apart: 84 -> 84, of which waited for: 37 -> 40; matrix products, arithmetic and copies ran while one was open for 14% -> 13% of each run, Pallas kernels for 12% -> 12%
where the time goes in v2:
time: 639 us; the launch traced here: 628 us
  waiting for transfers between devices  215 us (34%)
  starting transfers between devices  137 us (21%)
  Pallas kernels  105 us (16%)
  local copies, waits for them, and re-layouts  96.6 us (15%)
  other arithmetic  37.7 us (6%)
  matrix products  20.1 us (3%)
  between operations  16.6 us (3%)
    ppermute x47, waiting for transfers between devices, crossed(): lax.ppermute(block, axis, [(i, i ^ bits) for i in range(lax.axis_size(axi...  127 us
    unnamed x386, local copies, waits for them, and re-layouts  70.3 us
    ppermute x47, starting transfers between devices, crossed(): lax.ppermute(block, axis, [(i, i ^ bits) for i in range(lax.axis_size(axi...  70.3 us
    all_to_all x8, starting transfers between devices, to_experts(): lax.all_to_all(rows_out.reshape(exp_count, held * capacity, lanes), 'exp'...  44.3 us
    all_to_all x8, waiting for transfers between devices, to_experts(): lax.all_to_all(rows_out.reshape(exp_count, held * capacity, lanes), 'exp'...  31 us
    pallas_call x2, Pallas kernels, expert_call(): pl.pallas_call(kernel, out_shape=(*shapes, *(grads if with_grads else [])...  24 us
    ppermute x4, waiting for transfers between devices, shifted(): return lax.ppermute(block, 'ctx', route)  20.7 us
    all_gather x4, waiting for transfers between devices, gathered(): return [lax.all_gather(one, 'ctx', axis=0, tiled=True) for one in shards]  16.8 us
  transfers between devices with their start and end apart: 84, of which 40 were waited for; matrix products, arithmetic and copies ran while one was open for 13% of the time, Pallas kernels for 12%

profile of v2, /device:TPU:0, one launch (start us, length us, event | category | flops | bytes accessed | tf_op | source)
XLA Modules:
  0.0 628.0 jit_solution(6207368798103896956)
XLA Ops:
  7.3 4.2 shard_map.238
  28.1 3.6 collective-permute-start.4
  36.5 5.6 collective-permute-done.3.refs_2_
  43.3 5.6 collective-permute-done.8.refs_3_
  52.1 9.1 %collective-permute-done.9.refs_1_ = bf16[192,1280]{1,0:T(8,128)(2,1)S(1)} collective-permute-done((bf16[192,1280]{1,0:T(8,128)(2,1)S(1)}, bf16[192,1280]{1,0:T(8,128)(2,1)S(1)}, u32[]{:S(2)}, u32[]{:S(2)}) %collective-permute-start.9) | collective-permute-done | bytes 491552 | tf_op jit(solution)/shard_map/ppermute | solution.py:28
  66.0 3.5 collective-permute-start.14
  76.1 11.8 %collective-permute-done.11.refs_3_ = bf16[192,1280]{1,0:T(8,128)(2,1)S(1)} collective-permute-done((bf16[192,1280]{1,0:T(8,128)(2,1)S(1)}, bf16[192,1280]{1,0:T(8,128)(2,1)S(1)}, u32[]{:S(2)}, u32[]{:S(2)}) %collective-permute-start.11) | collective-permute-done | bytes 491552 | tf_op jit(solution)/shard_map/ppermute | solution.py:28
  98.6 4.0 collective-permute-start.16
  121.5 4.7 collective-permute-done.21.refs_3_
  142.0 3.5 all-to-all-start
  153.1 6.9 %all-to-all-done = bf16[4,80,768]{2,1,0:T(8,128)(2,1)S(1)} async-done(((bf16[4,80,768]{2,1,0:T(8,128)(2,1)}), bf16[4,80,768]{2,1,0:T(8,128)(2,1)S(1)}, u32[]{:S(2)}, u32[]{:S(2)}) %all-to-all-start) | async-done | bytes 491552 | tf_op jit(solution)/shard_map/all_to_all | solution.py:1014
  163.0 6.5 %shard_map.248 = (bf16[320,768]{1,0:T(8,128)(2,1)S(1)}, f32[4,320,768]{2,1,0:T(8,128)S(1)}) custom-call(bf16[320,768]{1,0:T(8,128)(2,1)S(1)} %bitcast.167, bf16[768,3072]{1,0:T(8,128)(2,1)} %all-gather.5.cloned.1.call-done.first_hbm, bf16[3072,768]{1,0:T(8,128)(2,1)} %all-gather.7.cloned.1.call-done.second_hbm), custom_call_target="tpu_custom_call" | custom-call | tf_op jit(solution)/shard_map/pallas_call | solution.py:552
  172.2 6.0 collective-permute-done.26.refs_3_
  178.2 12.7 %all-to-all-start.1 = ((bf16[4,80,768]{2,1,0:T(8,128)(2,1)}), bf16[4,80,768]{2,1,0:T(8,128)(2,1)S(1)}, u32[]{:S(2)}, u32[]{:S(2)}) async-start(bf16[4,80,768]{2,1,0:T(8,128)(2,1)} %bitcast.179), calls=%async_computation.1 | async-start | bytes 983040 | tf_op jit(solution)/shard_map/all_to_all | solution.py:1014
  193.6 9.9 %all-to-all-done.1 = bf16[4,80,768]{2,1,0:T(8,128)(2,1)S(1)} async-done(((bf16[4,80,768]{2,1,0:T(8,128)(2,1)}), bf16[4,80,768]{2,1,0:T(8,128)(2,1)S(1)}, u32[]{:S(2)}, u32[]{:S(2)}) %all-to-all-start.1) | async-done | bytes 491552 | tf_op jit(solution)/shard_map/all_to_all | solution.py:1014
  206.1 3.2 shard_map.249
  213.1 3.2 collective-permute-start.28
  222.2 5.7 collective-permute-done.28.refs_2_
  228.9 3.8 shard_map.251
  236.8 4.8 all-to-all-start.2
  256.9 5.1 all-to-all-start.3
  262.0 8.5 %reduce-scatter.5.cloned.1.call-start = ((), (), s32[]{:S(2)}) async-start(), calls=%async_computation.16 | async-start | bytes 5898240 | tf_op jit(solution)/shard_map/reduce_scatter | solution.py:1172
  270.5 16.1 %all-gather.9.cloned.1.call-done.refs_0_ = bf16[768,3072]{1,0:T(8,128)(2,1)} async-done(((bf16[192,3072]{1,0:T(8,128)(2,1)}), bf16[768,3072]{1,0:T(8,128)(2,1)}) %all-gather.9.cloned.1.call-update) | async-done | bytes 4718608 | tf_op jit(solution)/shard_map/all_gather | solution.py:951
  286.6 17.5 %shard_map.253 = (bf16[320,768]{1,0:T(8,128)(2,1)S(1)}, bf16[320,896]{1,0:T(8,128)(2,1)S(1)}, bf16[768,3072]{1,0:T(8,128)(2,1)}, bf16[3072,768]{1,0:T(8,128)(2,1)}) custom-call(bf16[320,896]{1,0:T(8,128)(2,1)} %bitcast.45.x_ref, bf16[320,768]{1,0:T(8,128)(2,1)} %bitcast.43.cot_ref, bf16[768,3072]{1,0:T(8,128)(2,1)} %all-gather.9.cloned.1.call-done.refs_0_, ...), custom_call_target="tpu_custom_call" | custom-call | tf_op jit(solution)/shard_map/pallas_call | solution.py:552
  306.4 4.6 all-to-all-start.4
  312.5 14.1 %all-to-all-done.4 = bf16[4,80,896]{2,1,0:T(8,128)(2,1)} async-done(((bf16[4,80,896]{2,1,0:T(8,128)(2,1)}), bf16[4,80,896]{2,1,0:T(8,128)(2,1)}, u32[]{:S(2)}, u32[]{:S(2)}) %all-to-all-start.4) | async-done | bytes 573472 | tf_op jit(solution)/shard_map/all_to_all | solution.py:1014
  333.1 3.1 shard_map.255
  339.2 4.1 all-to-all-start.6
  348.4 5.1 shard_map.256
  354.9 14.9 %collective-permute-done.33.refs_2_ = bf16[256,768]{1,0:T(8,128)(2,1)S(1)} collective-permute-done((bf16[256,768]{1,0:T(8,128)(2,1)S(1)}, bf16[256,768]{1,0:T(8,128)(2,1)S(1)}, u32[]{:S(2)}, u32[]{:S(2)}) %collective-permute-start.33) | collective-permute-done | bytes 393248 | tf_op jit(solution)/shard_map/ppermute | solution.py:24
  384.5 4.6 all-to-all-start.5
  407.6 3.9 shard_map.260
  413.7 11.3 %shard_map.261 = (bf16[320,768]{1,0:T(8,128)(2,1)}, bf16[768,3072]{1,0:T(8,128)(2,1)}) custom-call(bf16[320,768]{1,0:T(8,128)(2,1)S(1)} %bitcast.168, bf16[320,768]{1,0:T(8,128)(2,1)S(1)} %bitcast.170, f32[4,320,768]{2,1,0:T(8,128)S(1)} %copy-done.4, bf16[768,3072]{1,0:T(8,128)(2,1)} %all-gather.5.cloned.1.call-done.first_hbm, ...), custom_call_target="tpu_custom_call" | custom-call | tf_op jit(solution)/shard_map/pallas_call | solution.py:602
  426.4 4.9 all-to-all-start.7
  438.0 7.1 %collective-permute-done.37 = bf16[192,768]{1,0:T(8,128)(2,1)S(1)} collective-permute-done((bf16[192,768]{1,0:T(8,128)(2,1)}, bf16[192,768]{1,0:T(8,128)(2,1)S(1)}, u32[]{:S(2)}, u32[]{:S(2)}) %collective-permute-start.37) | collective-permute-done | bytes 294944 | tf_op jit(solution)/shard_map/ppermute | solution.py:28
  454.5 3.5 shard_map.263
  460.4 5.0 shard_map.264
  471.5 12.4 %collective-permute-done.40 = bf16[4,48,896]{2,1,0:T(8,128)(2,1)S(1)} collective-permute-done((bf16[4,48,896]{2,1,0:T(8,128)(2,1)S(1)}, bf16[4,48,896]{2,1,0:T(8,128)(2,1)S(1)}, u32[]{:S(2)}, u32[]{:S(2)}) %collective-permute-start.40) | collective-permute-done | bytes 344096 | tf_op jit(solution)/shard_map/ppermute | solution.py:28
  483.9 11.6 %collective-permute-done.41 = bf16[4,48,896]{2,1,0:T(8,128)(2,1)S(1)} collective-permute-done((bf16[4,48,896]{2,1,0:T(8,128)(2,1)S(1)}, bf16[4,48,896]{2,1,0:T(8,128)(2,1)S(1)}, u32[]{:S(2)}, u32[]{:S(2)}) %collective-permute-start.41) | collective-permute-done | bytes 344096 | tf_op jit(solution)/shard_map/ppermute | solution.py:28
  508.2 5.9 collective-permute-start.52
  519.4 7.4 %collective-permute-done.52 = bf16[4,48,896]{2,1,0:T(8,128)(2,1)S(1)} collective-permute-done((bf16[4,48,896]{2,1,0:T(8,128)(2,1)S(1)}, bf16[4,48,896]{2,1,0:T(8,128)(2,1)S(1)}, u32[]{:S(2)}, u32[]{:S(2)}) %collective-permute-start.52) | collective-permute-done | bytes 344096 | tf_op jit(solution)/shard_map/ppermute | solution.py:28
  528.3 12.4 %collective-permute-done.53 = bf16[4,48,896]{2,1,0:T(8,128)(2,1)S(1)} collective-permute-done((bf16[4,48,896]{2,1,0:T(8,128)(2,1)S(1)}, bf16[4,48,896]{2,1,0:T(8,128)(2,1)S(1)}, u32[]{:S(2)}, u32[]{:S(2)}) %collective-permute-start.53) | collective-permute-done | bytes 344096 | tf_op jit(solution)/shard_map/ppermute | solution.py:28
  552.6 6.9 %collective-permute-done.57 = bf16[48,896]{1,0:T(8,128)(2,1)S(1)} collective-permute-done((bf16[48,896]{1,0:T(8,128)(2,1)S(1)}, bf16[48,896]{1,0:T(8,128)(2,1)S(1)}, u32[]{:S(2)}, u32[]{:S(2)}) %collective-permute-start.57) | collective-permute-done | bytes 86048 | tf_op jit(solution)/shard_map/ppermute | solution.py:28
  565.0 10.3 %reduce-scatter.11.cloned.1.call-done.refs_3_.refs_1_ = bf16[768,768]{1,0:T(8,128)(2,1)} async-done(((bf16[3072,768]{1,0:T(8,128)(2,1)}), bf16[768,768]{1,0:T(8,128)(2,1)}) %reduce-scatter.11.cloned.1.call-update) | async-done | bytes 1179664 | tf_op jit(solution)/shard_map/reduce_scatter | solution.py:1172
  588.4 3.1 collective-permute-done.61
  594.1 4.9 collective-permute-done.36
  600.0 6.0 collective-permute-done.45
  615.3 5.6 shard_map.270
  (712 shorter events, 272.8 us)
Async XLA Ops:
  7.2 155.1 %all-gather.5.cloned.1.call-start = ((), (), s32[]{:S(2)}) async-start(), calls=%async_computation.12 | async-start | bytes 5898240 | tf_op jit(solution)/shard_map/all_gather | solution.py:951
  20.3 142.7 %all-gather.7.cloned.1.call-start = ((), (), s32[]{:S(2)}) async-start(), calls=%async_computation.13 | async-start | bytes 5898240 | tf_op jit(solution)/shard_map/all_gather | solution.py:951
  34.0 14.9 %collective-permute-start.8 = (bf16[48,1664]{1,0:T(8,128)(2,1)S(1)}, bf16[48,1664]{1,0:T(8,128)(2,1)S(1)}, u32[]{:S(2)}, u32[]{:S(2)}) collective-permute-start(bf16[48,1664]{1,0:T(8,128)(2,1)S(1)} %collective-permute-done.6.refs_1_), channel_id=1, source_target_pairs={{0,8},{4,12},{8,0},{12,4},{1,9},{5,13},{9,1},{13,5},{2,10},{6,14},... | collective-permute-start | bytes 479240 | tf_op jit(solution)/shard_map/ppermute | solution.py:28
  36.1 28.3 %collective-permute-start.23 = (s32[128,2]{0,1:T(2,128)S(1)}, s32[128,2]{0,1:T(2,128)S(1)}, u32[]{:S(2)}, u32[]{:S(2)}) collective-permute-start(s32[128,2]{0,1:T(2,128)S(1)} %get-tuple-element.337), channel_id=1, source_target_pairs={{0,4},{4,0},{8,12},{12,8},{1,5},{5,1},{9,13},{13,9},{2,6},{6,2},{1... | collective-permute-start | bytes 3080 | tf_op jit(solution)/shard_map/ppermute | solution.py:28
  42.1 22.6 %collective-permute-start = (bf16[128,768]{1,0:T(8,128)(2,1)}, bf16[128,768]{1,0:T(8,128)(2,1)}, u32[]{:S(2)}, u32[]{:S(2)}) collective-permute-start(bf16[128,768]{1,0:T(8,128)(2,1)} %get-tuple-element.314), channel_id=1, source_target_pairs={{0,4},{4,0},{8,12},{12,8},{1,5},{5,1},{9,13},{13,9},{2,6},{6,2},{1... | collective-permute-start | bytes 589832 | tf_op jit(solution)/shard_map/ppermute | solution.py:28
  50.0 25.3 %collective-permute-start.10 = (bf16[192,1280]{1,0:T(8,128)(2,1)S(1)}, bf16[192,1280]{1,0:T(8,128)(2,1)S(1)}, u32[]{:S(2)}, u32[]{:S(2)}) collective-permute-start(bf16[192,1280]{1,0:T(8,128)(2,1)S(1)} %shard_map.240.refs_0_), channel_id=1, source_target_pairs={{0,8},{4,12},{8,0},{12,4},{1,9},{5,13},{9,1},{13,5},{2,10},{6,14},... | collective-permute-start | bytes 1474568 | tf_op jit(solution)/shard_map/ppermute | solution.py:28
  61.2 26.8 %collective-permute-start.11 = (bf16[192,1280]{1,0:T(8,128)(2,1)S(1)}, bf16[192,1280]{1,0:T(8,128)(2,1)S(1)}, u32[]{:S(2)}, u32[]{:S(2)}) collective-permute-start(bf16[192,1280]{1,0:T(8,128)(2,1)S(1)} %collective-permute-done.9.refs_1_), channel_id=1, source_target_pairs={{0,8},{4,12},{8,0},{12,4},{1,9},{5,13},{9,1},{13,5},{2,10},{6,14},... | collective-permute-start | bytes 1474568 | tf_op jit(solution)/shard_map/ppermute | solution.py:28
  71.9 25.1 %collective-permute-start.15 = (bf16[192,1664]{1,0:T(8,128)(2,1)S(1)}, bf16[192,1664]{1,0:T(8,128)(2,1)S(1)}, u32[]{:S(2)}, u32[]{:S(2)}) collective-permute-start(bf16[192,1664]{1,0:T(8,128)(2,1)S(1)} %shard_map.241.refs_0_), channel_id=1, source_target_pairs={{0,1},{1,0},{2,3},{3,2},{4,5},{5,4},{6,7},{7,6},{8,9},{9,8},{10,11... | collective-permute-start | bytes 1916936 | tf_op jit(solution)/shard_map/ppermute | solution.py:28
  98.6 14.7 %collective-permute-start.16 = (bf16[256,768]{1,0:T(8,128)(2,1)S(1)}, bf16[256,768]{1,0:T(8,128)(2,1)}, u32[]{:S(2)}, u32[]{:S(2)}) collective-permute-start(bf16[256,768]{1,0:T(8,128)(2,1)S(1)} %slice.167.refs_1_), channel_id=1, source_target_pairs={{0,8},{4,12},{1,9},{5,13},{2,10},{6,14},{3,11},{7,15},{16,24},{20,... | collective-permute-start | bytes 1179656 | tf_op jit(solution)/shard_map/ppermute | solution.py:24
  105.4 29.0 %collective-permute-start.17 = (bf16[192,1664]{1,0:T(8,128)(2,1)S(1)}, bf16[192,1664]{1,0:T(8,128)(2,1)}, u32[]{:S(2)}, u32[]{:S(2)}) collective-permute-start(bf16[192,1664]{1,0:T(8,128)(2,1)S(1)} %shard_map.241.refs_0_), channel_id=1, source_target_pairs={{0,2},{1,3},{2,0},{3,1},{4,6},{5,7},{6,4},{7,5},{8,10},{9,11},{10,... | collective-permute-start | bytes 1916936 | tf_op jit(solution)/shard_map/ppermute | solution.py:28
  142.0 18.0 %all-to-all-start = ((bf16[4,80,768]{2,1,0:T(8,128)(2,1)}), bf16[4,80,768]{2,1,0:T(8,128)(2,1)S(1)}, u32[]{:S(2)}, u32[]{:S(2)}) async-start(bf16[4,80,768]{2,1,0:T(8,128)(2,1)} %bitcast.194), calls=%async_computation | async-start | bytes 983040 | tf_op jit(solution)/shard_map/all_to_all | solution.py:1014
  145.4 125.1 %all-gather.11.cloned.1.call-start = ((), (), s32[]{:S(2)}) async-start(), calls=%async_computation.15 | async-start | bytes 5898240 | tf_op jit(solution)/shard_map/all_gather | solution.py:951
  160.0 18.1 %collective-permute-start.26 = (bf16[192,1664]{1,0:T(8,128)(2,1)}, bf16[192,1664]{1,0:T(8,128)(2,1)}, u32[]{:S(2)}, u32[]{:S(2)}) collective-permute-start(bf16[192,1664]{1,0:T(8,128)(2,1)} %copy-done.67), channel_id=1, source_target_pairs={{0,3},{1,2},{2,1},{3,0},{4,7},{5,6},{6,5},{7,4},{8,11},{9,10},{10,... | collective-permute-start | bytes 1916936 | tf_op jit(solution)/shard_map/ppermute | solution.py:28
  178.2 25.3 %all-to-all-start.1 = ((bf16[4,80,768]{2,1,0:T(8,128)(2,1)}), bf16[4,80,768]{2,1,0:T(8,128)(2,1)S(1)}, u32[]{:S(2)}, u32[]{:S(2)}) async-start(bf16[4,80,768]{2,1,0:T(8,128)(2,1)} %bitcast.179), calls=%async_computation.1 | async-start | bytes 983040 | tf_op jit(solution)/shard_map/all_to_all | solution.py:1014
  190.9 95.7 %all-gather.9.cloned.1.call-start = ((), (), s32[]{:S(2)}) async-start(), calls=%async_computation.14 | async-start | bytes 5898240 | tf_op jit(solution)/shard_map/all_gather | solution.py:951
  213.1 14.8 %collective-permute-start.28 = (bf16[256,768]{1,0:T(8,128)(2,1)}, bf16[256,768]{1,0:T(8,128)(2,1)}, u32[]{:S(2)}, u32[]{:S(2)}) collective-permute-start(bf16[256,768]{1,0:T(8,128)(2,1)} %slice.179.refs_1_), channel_id=1, source_target_pairs={{0,8},{4,12},{1,9},{5,13},{2,10},{6,14},{3,11},{7,15},{16,24},{20,... | collective-permute-start | bytes 1179656 | tf_op jit(solution)/shard_map/ppermute | solution.py:24
  218.2 15.6 %collective-permute-start.30 = (bf16[768,384]{1,0:T(8,128)(2,1)}, bf16[768,384]{1,0:T(8,128)(2,1)}, u32[]{:S(2)}, u32[]{:S(2)}) collective-permute-start(bf16[768,384]{1,0:T(8,128)(2,1)} %slice.181), channel_id=1, source_target_pairs={{0,16},{16,0},{1,17},{17,1},{2,18},{18,2},{3,19},{19,3},{4,20},{20... | collective-permute-start | bytes 1769480 | tf_op jit(solution)/shard_map/ppermute | solution.py:18
  236.8 20.1 %all-to-all-start.2 = ((bf16[4,80,768]{2,1,0:T(8,128)(2,1)}), bf16[4,80,768]{2,1,0:T(8,128)(2,1)}, u32[]{:S(2)}, u32[]{:S(2)}) async-start(bf16[4,80,768]{2,1,0:T(8,128)(2,1)} %bitcast.193), calls=%async_computation.2 | async-start | bytes 983040 | tf_op jit(solution)/shard_map/all_to_all | solution.py:1014
  256.9 29.7 %all-to-all-start.3 = ((bf16[4,80,896]{2,1,0:T(8,128)(2,1)}), bf16[4,80,896]{2,1,0:T(8,128)(2,1)}, u32[]{:S(2)}, u32[]{:S(2)}) async-start(bf16[4,80,896]{2,1,0:T(8,128)(2,1)} %bitcast.192), calls=%async_computation.3 | async-start | bytes 1146880 | tf_op jit(solution)/shard_map/all_to_all | solution.py:1014
  262.0 303.0 %reduce-scatter.5.cloned.1.call-start = ((), (), s32[]{:S(2)}) async-start(), calls=%async_computation.16 | async-start | bytes 5898240 | tf_op jit(solution)/shard_map/reduce_scatter | solution.py:1172
  305.8 259.2 %reduce-scatter.7.cloned.1.call-start = ((), (), s32[]{:S(2)}) async-start(), calls=%async_computation.17 | async-start | bytes 5898240 | tf_op jit(solution)/shard_map/reduce_scatter | solution.py:1172
  306.4 20.3 %all-to-all-start.4 = ((bf16[4,80,896]{2,1,0:T(8,128)(2,1)}), bf16[4,80,896]{2,1,0:T(8,128)(2,1)}, u32[]{:S(2)}, u32[]{:S(2)}) async-start(bf16[4,80,896]{2,1,0:T(8,128)(2,1)} %bitcast.176), calls=%async_computation.4 | async-start | bytes 1146880 | tf_op jit(solution)/shard_map/all_to_all | solution.py:1014
  339.2 33.1 %all-to-all-start.6 = ((bf16[4,80,768]{2,1,0:T(8,128)(2,1)}), bf16[4,80,768]{2,1,0:T(8,128)(2,1)}, u32[]{:S(2)}, u32[]{:S(2)}) async-start(bf16[4,80,768]{2,1,0:T(8,128)(2,1)} %bitcast.177), calls=%async_computation.6 | async-start | bytes 983040 | tf_op jit(solution)/shard_map/all_to_all | solution.py:1014
  353.5 16.4 %collective-permute-start.33 = (bf16[256,768]{1,0:T(8,128)(2,1)S(1)}, bf16[256,768]{1,0:T(8,128)(2,1)S(1)}, u32[]{:S(2)}, u32[]{:S(2)}) collective-permute-start(bf16[256,768]{1,0:T(8,128)(2,1)S(1)} %get-tuple-element.153), channel_id=1, source_target_pairs={{8,0},{12,4},{9,1},{13,5},{10,2},{14,6},{11,3},{15,7},{24,16},{28,... | collective-permute-start | bytes 1179656 | tf_op jit(solution)/shard_map/ppermute | solution.py:24
  376.4 26.7 %collective-permute-start.35 = (f32[256,768]{1,0:T(8,128)}, f32[256,768]{1,0:T(8,128)}, u32[]{:S(2)}, u32[]{:S(2)}) collective-permute-start(f32[256,768]{1,0:T(8,128)} %fusion), channel_id=1, source_target_pairs={{0,16},{16,0},{1,17},{17,1},{2,18},{18,2},{3,19},{19,3},{4,20},{20... | collective-permute-start | bytes 2359304 | tf_op jit(solution)/shard_map/ppermute | solution.py:18
  384.5 20.9 %all-to-all-start.5 = ((bf16[4,80,768]{2,1,0:T(8,128)(2,1)}), bf16[4,80,768]{2,1,0:T(8,128)(2,1)S(1)}, u32[]{:S(2)}, u32[]{:S(2)}) async-start(bf16[4,80,768]{2,1,0:T(8,128)(2,1)} %bitcast.178), calls=%async_computation.5 | async-start | bytes 983040 | tf_op jit(solution)/shard_map/all_to_all | solution.py:1014
  389.1 175.9 %reduce-scatter.9.cloned.1.call-start = ((), (), s32[]{:S(2)}) async-start(), calls=%async_computation.18 | async-start | bytes 5898240 | tf_op jit(solution)/shard_map/reduce_scatter | solution.py:1172
  425.0 150.3 %reduce-scatter.11.cloned.1.call-start = ((), (), s32[]{:S(2)}) async-start(), calls=%async_computation.19 | async-start | bytes 5898240 | tf_op jit(solution)/shard_map/reduce_scatter | solution.py:1172
  426.4 20.7 %all-to-all-start.7 = ((bf16[4,80,768]{2,1,0:T(8,128)(2,1)}), bf16[4,80,768]{2,1,0:T(8,128)(2,1)}, u32[]{:S(2)}, u32[]{:S(2)}) async-start(bf16[4,80,768]{2,1,0:T(8,128)(2,1)} %bitcast.56), calls=%async_computation.7 | async-start | bytes 983040 | tf_op jit(solution)/shard_map/all_to_all | solution.py:1014
  431.2 13.8 %collective-permute-start.37 = (bf16[192,768]{1,0:T(8,128)(2,1)}, bf16[192,768]{1,0:T(8,128)(2,1)S(1)}, u32[]{:S(2)}, u32[]{:S(2)}) collective-permute-start(bf16[192,768]{1,0:T(8,128)(2,1)} %get-tuple-element.168), channel_id=1, source_target_pairs={{0,8},{4,12},{8,0},{12,4},{1,9},{5,13},{9,1},{13,5},{2,10},{6,14},... | collective-permute-start | bytes 884744 | tf_op jit(solution)/shard_map/ppermute | solution.py:28
  465.4 30.1 %collective-permute-start.43 = (bf16[256,768]{1,0:T(8,128)(2,1)S(1)}, bf16[256,768]{1,0:T(8,128)(2,1)S(1)}, u32[]{:S(2)}, u32[]{:S(2)}) collective-permute-start(bf16[256,768]{1,0:T(8,128)(2,1)S(1)} %get-tuple-element.189), channel_id=1, source_target_pairs={{8,0},{12,4},{9,1},{13,5},{10,2},{14,6},{11,3},{15,7},{24,16},{28,... | collective-permute-start | bytes 1179656 | tf_op jit(solution)/shard_map/ppermute | solution.py:24
  466.9 17.0 %collective-permute-start.40 = (bf16[4,48,896]{2,1,0:T(8,128)(2,1)S(1)}, bf16[4,48,896]{2,1,0:T(8,128)(2,1)S(1)}, u32[]{:S(2)}, u32[]{:S(2)}) collective-permute-start(bf16[4,48,896]{2,1,0:T(8,128)(2,1)S(1)} %copy-done.138), channel_id=1, source_target_pairs={{0,1},{1,0},{2,3},{3,2},{4,5},{5,4},{6,7},{7,6},{8,9},{9,8},{10,11... | collective-permute-start | bytes 1032200 | tf_op jit(solution)/shard_map/ppermute | solution.py:28
  468.8 26.6 %collective-permute-start.41 = (bf16[4,48,896]{2,1,0:T(8,128)(2,1)S(1)}, bf16[4,48,896]{2,1,0:T(8,128)(2,1)S(1)}, u32[]{:S(2)}, u32[]{:S(2)}) collective-permute-start(bf16[4,48,896]{2,1,0:T(8,128)(2,1)S(1)} %copy-done.136), channel_id=1, source_target_pairs={{0,2},{1,3},{2,0},{3,1},{4,6},{5,7},{6,4},{7,5},{8,10},{9,11},{10,... | collective-permute-start | bytes 1032200 | tf_op jit(solution)/shard_map/ppermute | solution.py:28
  471.2 24.2 %collective-permute-start.42 = (bf16[4,48,896]{2,1,0:T(8,128)(2,1)S(1)}, bf16[4,48,896]{2,1,0:T(8,128)(2,1)S(1)}, u32[]{:S(2)}, u32[]{:S(2)}) collective-permute-start(bf16[4,48,896]{2,1,0:T(8,128)(2,1)S(1)} %copy-done.134), channel_id=1, source_target_pairs={{0,3},{1,2},{2,1},{3,0},{4,7},{5,6},{6,5},{7,4},{8,11},{9,10},{10,... | collective-permute-start | bytes 1032200 | tf_op jit(solution)/shard_map/ppermute | solution.py:28
  505.5 43.8 %collective-permute-start.62 = (bf16[48,896]{1,0:T(8,128)(2,1)S(1)}, bf16[48,896]{1,0:T(8,128)(2,1)S(1)}, u32[]{:S(2)}, u32[]{:S(2)}) collective-permute-start(bf16[48,896]{1,0:T(8,128)(2,1)S(1)} %get-tuple-element.318), channel_id=1, source_target_pairs={{0,8},{4,12},{8,0},{12,4},{1,9},{5,13},{9,1},{13,5},{2,10},{6,14},... | collective-permute-start | bytes 258056 | tf_op jit(solution)/shard_map/ppermute | solution.py:28
  508.2 18.6 %collective-permute-start.52 = (bf16[4,48,896]{2,1,0:T(8,128)(2,1)S(1)}, bf16[4,48,896]{2,1,0:T(8,128)(2,1)S(1)}, u32[]{:S(2)}, u32[]{:S(2)}) collective-permute-start(bf16[4,48,896]{2,1,0:T(8,128)(2,1)S(1)} %get-tuple-element.203), channel_id=1, source_target_pairs={{0,1},{1,0},{2,3},{3,2},{4,5},{5,4},{6,7},{7,6},{8,9},{9,8},{10,11... | collective-permute-start | bytes 1032200 | tf_op jit(solution)/shard_map/ppermute | solution.py:28
  514.1 26.6 %collective-permute-start.53 = (bf16[4,48,896]{2,1,0:T(8,128)(2,1)S(1)}, bf16[4,48,896]{2,1,0:T(8,128)(2,1)S(1)}, u32[]{:S(2)}, u32[]{:S(2)}) collective-permute-start(bf16[4,48,896]{2,1,0:T(8,128)(2,1)S(1)} %get-tuple-element.204), channel_id=1, source_target_pairs={{0,2},{1,3},{2,0},{3,1},{4,6},{5,7},{6,4},{7,5},{8,10},{9,11},{10,... | collective-permute-start | bytes 1032200 | tf_op jit(solution)/shard_map/ppermute | solution.py:28
  515.0 27.5 %collective-permute-start.54 = (bf16[4,48,896]{2,1,0:T(8,128)(2,1)S(1)}, bf16[4,48,896]{2,1,0:T(8,128)(2,1)S(1)}, u32[]{:S(2)}, u32[]{:S(2)}) collective-permute-start(bf16[4,48,896]{2,1,0:T(8,128)(2,1)S(1)} %get-tuple-element.205), channel_id=1, source_target_pairs={{0,3},{1,2},{2,1},{3,0},{4,7},{5,6},{6,5},{7,4},{8,11},{9,10},{10,... | collective-permute-start | bytes 1032200 | tf_op jit(solution)/shard_map/ppermute | solution.py:28
  517.4 42.1 %collective-permute-start.46 = (bf16[192,768]{1,0:T(8,128)(2,1)S(1)}, bf16[192,768]{1,0:T(8,128)(2,1)S(1)}, u32[]{:S(2)}, u32[]{:S(2)}) collective-permute-start(bf16[192,768]{1,0:T(8,128)(2,1)S(1)} %get-tuple-element.199), channel_id=1, source_target_pairs={{0,8},{4,12},{8,0},{12,4},{1,9},{5,13},{9,1},{13,5},{2,10},{6,14},... | collective-permute-start | bytes 884744 | tf_op jit(solution)/shard_map/ppermute | solution.py:28
  526.8 19.3 %collective-permute-start.47 = (bf16[192,768]{1,0:T(8,128)(2,1)S(1)}, bf16[192,768]{1,0:T(8,128)(2,1)S(1)}, u32[]{:S(2)}, u32[]{:S(2)}) collective-permute-start(bf16[192,768]{1,0:T(8,128)(2,1)S(1)} %get-tuple-element.201), channel_id=1, source_target_pairs={{0,8},{4,12},{8,0},{12,4},{1,9},{5,13},{9,1},{13,5},{2,10},{6,14},... | collective-permute-start | bytes 884744 | tf_op jit(solution)/shard_map/ppermute | solution.py:28
  550.3 30.5 %collective-permute-start.58 = (bf16[192,768]{1,0:T(8,128)(2,1)S(1)}, bf16[192,768]{1,0:T(8,128)(2,1)S(1)}, u32[]{:S(2)}, u32[]{:S(2)}) collective-permute-start(bf16[192,768]{1,0:T(8,128)(2,1)S(1)} %copy-done.159), channel_id=1, source_target_pairs={{0,4},{4,0},{8,12},{12,8},{1,5},{5,1},{9,13},{13,9},{2,6},{6,2},{1... | collective-permute-start | bytes 884744 | tf_op jit(solution)/shard_map/ppermute | solution.py:28
  559.7 21.7 %collective-permute-start.49 = (bf16[48,768]{1,0:T(8,128)(2,1)S(1)}, bf16[48,768]{1,0:T(8,128)(2,1)S(1)}, u32[]{:S(2)}, u32[]{:S(2)}) collective-permute-start(bf16[48,768]{1,0:T(8,128)(2,1)S(1)} %get-tuple-element.320), channel_id=1, source_target_pairs={{0,1},{1,0},{2,3},{3,2},{4,5},{5,4},{6,7},{7,6},{8,9},{9,8},{10,11... | collective-permute-start | bytes 221192 | tf_op jit(solution)/shard_map/ppermute | solution.py:28
  562.6 21.8 %collective-permute-start.51 = (bf16[48,768]{1,0:T(8,128)(2,1)S(1)}, bf16[48,768]{1,0:T(8,128)(2,1)S(1)}, u32[]{:S(2)}, u32[]{:S(2)}) collective-permute-start(bf16[48,768]{1,0:T(8,128)(2,1)S(1)} %get-tuple-element.321), channel_id=1, source_target_pairs={{0,3},{1,2},{2,1},{3,0},{4,7},{5,6},{6,5},{7,4},{8,11},{9,10},{10,... | collective-permute-start | bytes 221192 | tf_op jit(solution)/shard_map/ppermute | solution.py:28
  565.0 21.9 %collective-permute-start.50 = (bf16[48,768]{1,0:T(8,128)(2,1)S(1)}, bf16[48,768]{1,0:T(8,128)(2,1)S(1)}, u32[]{:S(2)}, u32[]{:S(2)}) collective-permute-start(bf16[48,768]{1,0:T(8,128)(2,1)S(1)} %get-tuple-element.322), channel_id=1, source_target_pairs={{0,2},{1,3},{2,0},{3,1},{4,6},{5,7},{6,4},{7,5},{8,10},{9,11},{10,... | collective-permute-start | bytes 221192 | tf_op jit(solution)/shard_map/ppermute | solution.py:28
  580.7 26.2 %collective-permute-start.65 = (bf16[192,3072]{1,0:T(8,128)(2,1)S(1)}, bf16[192,3072]{1,0:T(8,128)(2,1)S(1)}, u32[]{:S(2)}, u32[]{:S(2)}) collective-permute-start(bf16[192,3072]{1,0:T(8,128)(2,1)S(1)} %get-tuple-element.216), channel_id=1, source_target_pairs={{0,16},{16,0},{1,17},{17,1},{2,18},{18,2},{3,19},{19,3},{4,20},{20... | collective-permute-start | bytes 3538952 | tf_op jit(solution)/shard_map/ppermute | solution.py:18
  580.8 27.1 %collective-permute-start.66 = (bf16[768,768]{1,0:T(8,128)(2,1)S(1)}, bf16[768,768]{1,0:T(8,128)(2,1)S(1)}, u32[]{:S(2)}, u32[]{:S(2)}) collective-permute-start(bf16[768,768]{1,0:T(8,128)(2,1)S(1)} %get-tuple-element.217), channel_id=1, source_target_pairs={{0,16},{16,0},{1,17},{17,1},{2,18},{18,2},{3,19},{19,3},{4,20},{20... | collective-permute-start | bytes 3538952 | tf_op jit(solution)/shard_map/ppermute | solution.py:18
  591.5 14.5 %collective-permute-start.45 = (f32[128,768]{1,0:T(8,128)}, f32[128,768]{1,0:T(8,128)S(1)}, u32[]{:S(2)}, u32[]{:S(2)}) collective-permute-start(f32[128,768]{1,0:T(8,128)} %get-tuple-element.307), channel_id=1, source_target_pairs={{0,4},{4,0},{8,12},{12,8},{1,5},{5,1},{9,13},{13,9},{2,6},{6,2},{1... | collective-permute-start | bytes 1179656 | tf_op jit(solution)/shard_map/ppermute | solution.py:28
  594.0 13.9 %collective-permute-start.67 = (f32[48,1664]{1,0:T(8,128)S(1)}, f32[48,1664]{1,0:T(8,128)S(1)}, u32[]{:S(2)}, u32[]{:S(2)}) collective-permute-start(f32[48,1664]{1,0:T(8,128)S(1)} %get-tuple-element.310), channel_id=1, source_target_pairs={{0,16},{16,0},{1,17},{17,1},{2,18},{18,2},{3,19},{19,3},{4,20},{20... | collective-permute-start | bytes 958472 | tf_op jit(solution)/shard_map/ppermute | solution.py:18
  (227 other events, 1477.9 us)
Sparse Core Ops, SparseCore 0:
  20.4 79.8 all-gather.4
  102.1 60.7 all-gather.6
  164.8 61.2 all-gather.10
  228.4 58.1 all-gather.8
  306.0 60.3 reduce-scatter.4
  369.7 56.8 reduce-scatter.6
  429.6 62.9 reduce-scatter.8
  495.5 79.7 reduce-scatter.10

commit v3 on v2

--- a/solution.py
+++ b/solution.py
@@ -908,7 +908,9 @@
     def regrouped(block):
         mine = lax.dynamic_index_in_dim(block, parity, 0, keepdims=False)
         sent = lax.dynamic_index_in_dim(block, 1 - parity, 0, keepdims=False)
-        came = crossed(sent, 1)
+        if block.dtype == WIDE:
+            sent = sent.astype(LOW)
+        came = crossed(sent, 1).astype(block.dtype)
         return jnp.where(is_even, jnp.stack([mine, came]), jnp.stack([came, mine]))
 
     def own_order(mine, other, axis):

time: 639 us -> 625 us (0.978)
  waiting for transfers between devices: 215 us -> 199 us
    reduce_scatter x4, waiting for transfers between devices: 10.4 us -> 0.08 us  [summed_shards(): lax.psum_scatter(one, 'ctx', scatter_dimension=0, tiled=True)]
    unnamed x386 -> x390, local copies, waits for them, and re-layouts: 70.3 us -> 70.6 us
  transfers between devices with their start and end apart: 84 -> 84, of which waited for: 40 -> 37; matrix products, arithmetic and copies ran while one was open for 13% -> 13% of each run, Pallas kernels for 12% -> 12%
where the time goes in v3:
time: 625 us; the launch traced here: 614 us
  waiting for transfers between devices  199 us (32%)
  starting transfers between devices  138 us (22%)
  Pallas kernels  105 us (17%)
  local copies, waits for them, and re-layouts  96 us (15%)
  other arithmetic  38.4 us (6%)
  matrix products  20.1 us (3%)
  between operations  16.7 us (3%)
    ppermute x47, waiting for transfers between devices, crossed(): lax.ppermute(block, axis, [(i, i ^ bits) for i in range(lax.axis_size(axi...  122 us
    ppermute x47, starting transfers between devices, crossed(): lax.ppermute(block, axis, [(i, i ^ bits) for i in range(lax.axis_size(axi...  71.3 us
    unnamed x390, local copies, waits for them, and re-layouts  70.6 us
    all_to_all x8, starting transfers between devices, to_experts(): lax.all_to_all(rows_out.reshape(exp_count, held * capacity, lanes), 'exp'...  44.4 us
    all_to_all x8, waiting for transfers between devices, to_experts(): lax.all_to_all(rows_out.reshape(exp_count, held * capacity, lanes), 'exp'...  31 us
    pallas_call x2, Pallas kernels, expert_call(): pl.pallas_call(kernel, out_shape=(*shapes, *(grads if with_grads else [])...  24 us
    ppermute x4, waiting for transfers between devices, shifted(): return lax.ppermute(block, 'ctx', route)  20.6 us
    all_gather x4, waiting for transfers between devices, gathered(): return [lax.all_gather(one, 'ctx', axis=0, tiled=True) for one in shards]  16.7 us
  transfers between devices with their start and end apart: 84, of which 37 were waited for; matrix products, arithmetic and copies ran while one was open for 13% of the time, Pallas kernels for 12%

profile of v3, /device:TPU:0, one launch (start us, length us, event | category | flops | bytes accessed | tf_op | source)
XLA Modules:
  0.0 613.6 jit_solution(13203130591512164206)
XLA Ops:
  7.3 4.2 shard_map.238
  28.1 3.6 collective-permute-start.4
  36.5 5.6 collective-permute-done.3.refs_2_
  43.3 5.6 collective-permute-done.8.refs_3_
  52.1 9.1 %collective-permute-done.9.refs_1_ = bf16[192,1280]{1,0:T(8,128)(2,1)S(1)} collective-permute-done((bf16[192,1280]{1,0:T(8,128)(2,1)S(1)}, bf16[192,1280]{1,0:T(8,128)(2,1)S(1)}, u32[]{:S(2)}, u32[]{:S(2)}) %collective-permute-start.9) | collective-permute-done | bytes 491552 | tf_op jit(solution)/shard_map/ppermute | solution.py:28
  66.1 3.5 collective-permute-start.14
  76.2 11.7 %collective-permute-done.11.refs_3_ = bf16[192,1280]{1,0:T(8,128)(2,1)S(1)} collective-permute-done((bf16[192,1280]{1,0:T(8,128)(2,1)S(1)}, bf16[192,1280]{1,0:T(8,128)(2,1)S(1)}, u32[]{:S(2)}, u32[]{:S(2)}) %collective-permute-start.11) | collective-permute-done | bytes 491552 | tf_op jit(solution)/shard_map/ppermute | solution.py:28
  98.6 4.0 collective-permute-start.16
  121.5 4.7 collective-permute-done.21.refs_3_
  131.4 3.0 shard_map.245
  142.0 3.5 all-to-all-start
  153.1 6.9 %all-to-all-done = bf16[4,80,768]{2,1,0:T(8,128)(2,1)S(1)} async-done(((bf16[4,80,768]{2,1,0:T(8,128)(2,1)}), bf16[4,80,768]{2,1,0:T(8,128)(2,1)S(1)}, u32[]{:S(2)}, u32[]{:S(2)}) %all-to-all-start) | async-done | bytes 491552 | tf_op jit(solution)/shard_map/all_to_all | solution.py:1016
  163.0 6.5 %shard_map.248 = (bf16[320,768]{1,0:T(8,128)(2,1)S(1)}, f32[4,320,768]{2,1,0:T(8,128)S(1)}) custom-call(bf16[320,768]{1,0:T(8,128)(2,1)S(1)} %bitcast.171, bf16[768,3072]{1,0:T(8,128)(2,1)} %all-gather.5.cloned.1.call-done.first_hbm, bf16[3072,768]{1,0:T(8,128)(2,1)} %all-gather.7.cloned.1.call-done.second_hbm), custom_call_target="tpu_custom_call" | custom-call | tf_op jit(solution)/shard_map/pallas_call | solution.py:552
  172.2 6.0 collective-permute-done.26.refs_3_
  178.2 12.7 %all-to-all-start.1 = ((bf16[4,80,768]{2,1,0:T(8,128)(2,1)}), bf16[4,80,768]{2,1,0:T(8,128)(2,1)S(1)}, u32[]{:S(2)}, u32[]{:S(2)}) async-start(bf16[4,80,768]{2,1,0:T(8,128)(2,1)} %bitcast.183), calls=%async_computation.1 | async-start | bytes 983040 | tf_op jit(solution)/shard_map/all_to_all | solution.py:1016
  193.7 9.9 %all-to-all-done.1 = bf16[4,80,768]{2,1,0:T(8,128)(2,1)S(1)} async-done(((bf16[4,80,768]{2,1,0:T(8,128)(2,1)}), bf16[4,80,768]{2,1,0:T(8,128)(2,1)S(1)}, u32[]{:S(2)}, u32[]{:S(2)}) %all-to-all-start.1) | async-done | bytes 491552 | tf_op jit(solution)/shard_map/all_to_all | solution.py:1016
  206.2 3.2 shard_map.249
  213.2 3.3 collective-permute-start.28
  222.3 5.7 collective-permute-done.28.refs_2_
  228.9 3.8 shard_map.251
  236.8 4.8 all-to-all-start.2
  256.9 5.1 all-to-all-start.3
  262.0 8.5 %reduce-scatter.5.cloned.1.call-start = ((), (), s32[]{:S(2)}) async-start(), calls=%async_computation.16 | async-start | bytes 5898240 | tf_op jit(solution)/shard_map/reduce_scatter | solution.py:1174
  270.5 16.1 %all-gather.9.cloned.1.call-done.refs_0_ = bf16[768,3072]{1,0:T(8,128)(2,1)} async-done(((bf16[192,3072]{1,0:T(8,128)(2,1)}), bf16[768,3072]{1,0:T(8,128)(2,1)}) %all-gather.9.cloned.1.call-update) | async-done | bytes 4718608 | tf_op jit(solution)/shard_map/all_gather | solution.py:953
  286.6 17.5 %shard_map.253 = (bf16[320,768]{1,0:T(8,128)(2,1)S(1)}, bf16[320,896]{1,0:T(8,128)(2,1)S(1)}, bf16[768,3072]{1,0:T(8,128)(2,1)}, bf16[3072,768]{1,0:T(8,128)(2,1)}) custom-call(bf16[320,896]{1,0:T(8,128)(2,1)} %bitcast.45.x_ref, bf16[320,768]{1,0:T(8,128)(2,1)} %bitcast.43.cot_ref, bf16[768,3072]{1,0:T(8,128)(2,1)} %all-gather.9.cloned.1.call-done.refs_0_, ...), custom_call_target="tpu_custom_call" | custom-call | tf_op jit(solution)/shard_map/pallas_call | solution.py:552
  306.4 4.6 all-to-all-start.4
  312.5 14.2 %all-to-all-done.4 = bf16[4,80,896]{2,1,0:T(8,128)(2,1)} async-done(((bf16[4,80,896]{2,1,0:T(8,128)(2,1)}), bf16[4,80,896]{2,1,0:T(8,128)(2,1)}, u32[]{:S(2)}, u32[]{:S(2)}) %all-to-all-start.4) | async-done | bytes 573472 | tf_op jit(solution)/shard_map/all_to_all | solution.py:1016
  333.1 3.1 shard_map.255
  339.2 4.1 all-to-all-start.6
  348.4 5.1 shard_map.256
  354.9 14.9 %collective-permute-done.33.refs_2_ = bf16[256,768]{1,0:T(8,128)(2,1)S(1)} collective-permute-done((bf16[256,768]{1,0:T(8,128)(2,1)S(1)}, bf16[256,768]{1,0:T(8,128)(2,1)S(1)}, u32[]{:S(2)}, u32[]{:S(2)}) %collective-permute-start.33) | collective-permute-done | bytes 393248 | tf_op jit(solution)/shard_map/ppermute | solution.py:24
  384.5 4.6 all-to-all-start.5
  407.6 4.0 shard_map.260
  413.7 11.3 %shard_map.261 = (bf16[320,768]{1,0:T(8,128)(2,1)}, bf16[768,3072]{1,0:T(8,128)(2,1)}) custom-call(bf16[320,768]{1,0:T(8,128)(2,1)S(1)} %bitcast.172, bf16[320,768]{1,0:T(8,128)(2,1)S(1)} %bitcast.174, f32[4,320,768]{2,1,0:T(8,128)S(1)} %copy-done.4, bf16[768,3072]{1,0:T(8,128)(2,1)} %all-gather.5.cloned.1.call-done.first_hbm, ...), custom_call_target="tpu_custom_call" | custom-call | tf_op jit(solution)/shard_map/pallas_call | solution.py:602
  426.3 4.9 all-to-all-start.7
  437.9 7.0 %collective-permute-done.37 = bf16[192,768]{1,0:T(8,128)(2,1)S(1)} collective-permute-done((bf16[192,768]{1,0:T(8,128)(2,1)}, bf16[192,768]{1,0:T(8,128)(2,1)S(1)}, u32[]{:S(2)}, u32[]{:S(2)}) %collective-permute-start.37) | collective-permute-done | bytes 294944 | tf_op jit(solution)/shard_map/ppermute | solution.py:28
  454.4 3.5 shard_map.263
  460.3 5.0 shard_map.264
  471.7 12.3 %collective-permute-done.40 = bf16[4,48,896]{2,1,0:T(8,128)(2,1)S(1)} collective-permute-done((bf16[4,48,896]{2,1,0:T(8,128)(2,1)S(1)}, bf16[4,48,896]{2,1,0:T(8,128)(2,1)S(1)}, u32[]{:S(2)}, u32[]{:S(2)}) %collective-permute-start.40) | collective-permute-done | bytes 344096 | tf_op jit(solution)/shard_map/ppermute | solution.py:28
  484.0 11.6 %collective-permute-done.41 = bf16[4,48,896]{2,1,0:T(8,128)(2,1)S(1)} collective-permute-done((bf16[4,48,896]{2,1,0:T(8,128)(2,1)S(1)}, bf16[4,48,896]{2,1,0:T(8,128)(2,1)S(1)}, u32[]{:S(2)}, u32[]{:S(2)}) %collective-permute-start.41) | collective-permute-done | bytes 344096 | tf_op jit(solution)/shard_map/ppermute | solution.py:28
  499.5 7.4 %collective-permute-done.36 = bf16[128,768]{1,0:T(8,128)(2,1)} collective-permute-done((bf16[128,768]{1,0:T(8,128)(2,1)}, bf16[128,768]{1,0:T(8,128)(2,1)}, u32[]{:S(2)}, u32[]{:S(2)}) %collective-permute-start.36) | collective-permute-done | bytes 196640 | tf_op jit(solution)/shard_map/ppermute | solution.py:28
  514.3 4.1 collective-permute-start.62
  518.5 7.7 %collective-permute-start.52 = (bf16[4,48,896]{2,1,0:T(8,128)(2,1)S(1)}, bf16[4,48,896]{2,1,0:T(8,128)(2,1)S(1)}, u32[]{:S(2)}, u32[]{:S(2)}) collective-permute-start(bf16[4,48,896]{2,1,0:T(8,128)(2,1)S(1)} %get-tuple-element.203), channel_id=1, source_target_pairs={{0,1},{1,0},{2,3},{3,2},{4,5},{5,4},{6,7},{7,6},{8,9},{9,8},{10,11... | collective-permute-start | bytes 1032200 | tf_op jit(solution)/shard_map/ppermute | solution.py:28
  532.5 7.5 %collective-permute-done.52 = bf16[4,48,896]{2,1,0:T(8,128)(2,1)S(1)} collective-permute-done((bf16[4,48,896]{2,1,0:T(8,128)(2,1)S(1)}, bf16[4,48,896]{2,1,0:T(8,128)(2,1)S(1)}, u32[]{:S(2)}, u32[]{:S(2)}) %collective-permute-start.52) | collective-permute-done | bytes 344096 | tf_op jit(solution)/shard_map/ppermute | solution.py:28
  541.5 11.3 %collective-permute-done.53 = bf16[4,48,896]{2,1,0:T(8,128)(2,1)S(1)} collective-permute-done((bf16[4,48,896]{2,1,0:T(8,128)(2,1)S(1)}, bf16[4,48,896]{2,1,0:T(8,128)(2,1)S(1)}, u32[]{:S(2)}, u32[]{:S(2)}) %collective-permute-start.53) | collective-permute-done | bytes 344096 | tf_op jit(solution)/shard_map/ppermute | solution.py:28
  557.2 4.5 collective-permute-done.56
  566.2 3.0 collective-permute-done.57
  600.8 5.6 shard_map.270
  (719 shorter events, 267.2 us)
Async XLA Ops:
  7.2 155.2 %all-gather.5.cloned.1.call-start = ((), (), s32[]{:S(2)}) async-start(), calls=%async_computation.12 | async-start | bytes 5898240 | tf_op jit(solution)/shard_map/all_gather | solution.py:953
  20.3 142.7 %all-gather.7.cloned.1.call-start = ((), (), s32[]{:S(2)}) async-start(), calls=%async_computation.13 | async-start | bytes 5898240 | tf_op jit(solution)/shard_map/all_gather | solution.py:953
  34.0 14.9 %collective-permute-start.8 = (bf16[48,1664]{1,0:T(8,128)(2,1)S(1)}, bf16[48,1664]{1,0:T(8,128)(2,1)S(1)}, u32[]{:S(2)}, u32[]{:S(2)}) collective-permute-start(bf16[48,1664]{1,0:T(8,128)(2,1)S(1)} %collective-permute-done.6.refs_1_), channel_id=1, source_target_pairs={{0,8},{4,12},{8,0},{12,4},{1,9},{5,13},{9,1},{13,5},{2,10},{6,14},... | collective-permute-start | bytes 479240 | tf_op jit(solution)/shard_map/ppermute | solution.py:28
  36.1 28.4 %collective-permute-start.23 = (s32[128,2]{0,1:T(2,128)S(1)}, s32[128,2]{0,1:T(2,128)S(1)}, u32[]{:S(2)}, u32[]{:S(2)}) collective-permute-start(s32[128,2]{0,1:T(2,128)S(1)} %get-tuple-element.333), channel_id=1, source_target_pairs={{0,4},{4,0},{8,12},{12,8},{1,5},{5,1},{9,13},{13,9},{2,6},{6,2},{1... | collective-permute-start | bytes 3080 | tf_op jit(solution)/shard_map/ppermute | solution.py:28
  42.1 22.7 %collective-permute-start = (bf16[128,768]{1,0:T(8,128)(2,1)}, bf16[128,768]{1,0:T(8,128)(2,1)}, u32[]{:S(2)}, u32[]{:S(2)}) collective-permute-start(bf16[128,768]{1,0:T(8,128)(2,1)} %get-tuple-element.310), channel_id=1, source_target_pairs={{0,4},{4,0},{8,12},{12,8},{1,5},{5,1},{9,13},{13,9},{2,6},{6,2},{1... | collective-permute-start | bytes 589832 | tf_op jit(solution)/shard_map/ppermute | solution.py:28
  50.0 25.4 %collective-permute-start.10 = (bf16[192,1280]{1,0:T(8,128)(2,1)S(1)}, bf16[192,1280]{1,0:T(8,128)(2,1)S(1)}, u32[]{:S(2)}, u32[]{:S(2)}) collective-permute-start(bf16[192,1280]{1,0:T(8,128)(2,1)S(1)} %shard_map.240.refs_0_), channel_id=1, source_target_pairs={{0,8},{4,12},{8,0},{12,4},{1,9},{5,13},{9,1},{13,5},{2,10},{6,14},... | collective-permute-start | bytes 1474568 | tf_op jit(solution)/shard_map/ppermute | solution.py:28
  61.2 26.8 %collective-permute-start.11 = (bf16[192,1280]{1,0:T(8,128)(2,1)S(1)}, bf16[192,1280]{1,0:T(8,128)(2,1)S(1)}, u32[]{:S(2)}, u32[]{:S(2)}) collective-permute-start(bf16[192,1280]{1,0:T(8,128)(2,1)S(1)} %collective-permute-done.9.refs_1_), channel_id=1, source_target_pairs={{0,8},{4,12},{8,0},{12,4},{1,9},{5,13},{9,1},{13,5},{2,10},{6,14},... | collective-permute-start | bytes 1474568 | tf_op jit(solution)/shard_map/ppermute | solution.py:28
  72.0 25.0 %collective-permute-start.15 = (bf16[192,1664]{1,0:T(8,128)(2,1)S(1)}, bf16[192,1664]{1,0:T(8,128)(2,1)S(1)}, u32[]{:S(2)}, u32[]{:S(2)}) collective-permute-start(bf16[192,1664]{1,0:T(8,128)(2,1)S(1)} %shard_map.241.refs_0_), channel_id=1, source_target_pairs={{0,1},{1,0},{2,3},{3,2},{4,5},{5,4},{6,7},{7,6},{8,9},{9,8},{10,11... | collective-permute-start | bytes 1916936 | tf_op jit(solution)/shard_map/ppermute | solution.py:28
  98.6 14.8 %collective-permute-start.16 = (bf16[256,768]{1,0:T(8,128)(2,1)S(1)}, bf16[256,768]{1,0:T(8,128)(2,1)}, u32[]{:S(2)}, u32[]{:S(2)}) collective-permute-start(bf16[256,768]{1,0:T(8,128)(2,1)S(1)} %slice.167.refs_1_), channel_id=1, source_target_pairs={{0,8},{4,12},{1,9},{5,13},{2,10},{6,14},{3,11},{7,15},{16,24},{20,... | collective-permute-start | bytes 1179656 | tf_op jit(solution)/shard_map/ppermute | solution.py:24
  105.4 29.0 %collective-permute-start.17 = (bf16[192,1664]{1,0:T(8,128)(2,1)S(1)}, bf16[192,1664]{1,0:T(8,128)(2,1)}, u32[]{:S(2)}, u32[]{:S(2)}) collective-permute-start(bf16[192,1664]{1,0:T(8,128)(2,1)S(1)} %shard_map.241.refs_0_), channel_id=1, source_target_pairs={{0,2},{1,3},{2,0},{3,1},{4,6},{5,7},{6,4},{7,5},{8,10},{9,11},{10,... | collective-permute-start | bytes 1916936 | tf_op jit(solution)/shard_map/ppermute | solution.py:28
  113.3 12.9 %collective-permute-start.21 = (bf16[192,384]{1,0:T(8,128)(2,1)}, bf16[192,384]{1,0:T(8,128)(2,1)}, u32[]{:S(2)}, u32[]{:S(2)}) collective-permute-start(bf16[192,384]{1,0:T(8,128)(2,1)} %collective-permute-done.19.refs_1_), channel_id=1, source_target_pairs={{0,8},{4,12},{8,0},{12,4},{1,9},{5,13},{9,1},{13,5},{2,10},{6,14},... | collective-permute-start | bytes 442376 | tf_op jit(solution)/shard_map/ppermute | solution.py:28
  142.0 18.0 %all-to-all-start = ((bf16[4,80,768]{2,1,0:T(8,128)(2,1)}), bf16[4,80,768]{2,1,0:T(8,128)(2,1)S(1)}, u32[]{:S(2)}, u32[]{:S(2)}) async-start(bf16[4,80,768]{2,1,0:T(8,128)(2,1)} %bitcast.200), calls=%async_computation | async-start | bytes 983040 | tf_op jit(solution)/shard_map/all_to_all | solution.py:1016
  145.5 125.0 %all-gather.11.cloned.1.call-start = ((), (), s32[]{:S(2)}) async-start(), calls=%async_computation.15 | async-start | bytes 5898240 | tf_op jit(solution)/shard_map/all_gather | solution.py:953
  160.1 18.1 %collective-permute-start.26 = (bf16[192,1664]{1,0:T(8,128)(2,1)}, bf16[192,1664]{1,0:T(8,128)(2,1)}, u32[]{:S(2)}, u32[]{:S(2)}) collective-permute-start(bf16[192,1664]{1,0:T(8,128)(2,1)} %copy-done.67), channel_id=1, source_target_pairs={{0,3},{1,2},{2,1},{3,0},{4,7},{5,6},{6,5},{7,4},{8,11},{9,10},{10,... | collective-permute-start | bytes 1916936 | tf_op jit(solution)/shard_map/ppermute | solution.py:28
  178.2 25.3 %all-to-all-start.1 = ((bf16[4,80,768]{2,1,0:T(8,128)(2,1)}), bf16[4,80,768]{2,1,0:T(8,128)(2,1)S(1)}, u32[]{:S(2)}, u32[]{:S(2)}) async-start(bf16[4,80,768]{2,1,0:T(8,128)(2,1)} %bitcast.183), calls=%async_computation.1 | async-start | bytes 983040 | tf_op jit(solution)/shard_map/all_to_all | solution.py:1016
  190.9 95.6 %all-gather.9.cloned.1.call-start = ((), (), s32[]{:S(2)}) async-start(), calls=%async_computation.14 | async-start | bytes 5898240 | tf_op jit(solution)/shard_map/all_gather | solution.py:953
  204.7 11.8 %collective-permute-start.31 = (bf16[128,768]{1,0:T(8,128)(2,1)S(1)}, bf16[128,768]{1,0:T(8,128)(2,1)S(1)}, u32[]{:S(2)}, u32[]{:S(2)}) collective-permute-start(bf16[128,768]{1,0:T(8,128)(2,1)S(1)} %get-tuple-element.309), channel_id=1, source_target_pairs={{0,4},{4,0},{8,12},{12,8},{1,5},{5,1},{9,13},{13,9},{2,6},{6,2},{1... | collective-permute-start | bytes 589832 | tf_op jit(solution)/shard_map/ppermute | solution.py:28
  213.2 14.7 %collective-permute-start.28 = (bf16[256,768]{1,0:T(8,128)(2,1)}, bf16[256,768]{1,0:T(8,128)(2,1)}, u32[]{:S(2)}, u32[]{:S(2)}) collective-permute-start(bf16[256,768]{1,0:T(8,128)(2,1)} %slice.179.refs_1_), channel_id=1, source_target_pairs={{0,8},{4,12},{1,9},{5,13},{2,10},{6,14},{3,11},{7,15},{16,24},{20,... | collective-permute-start | bytes 1179656 | tf_op jit(solution)/shard_map/ppermute | solution.py:24
  218.3 15.6 %collective-permute-start.30 = (bf16[768,384]{1,0:T(8,128)(2,1)}, bf16[768,384]{1,0:T(8,128)(2,1)}, u32[]{:S(2)}, u32[]{:S(2)}) collective-permute-start(bf16[768,384]{1,0:T(8,128)(2,1)} %slice.181), channel_id=1, source_target_pairs={{0,16},{16,0},{1,17},{17,1},{2,18},{18,2},{3,19},{19,3},{4,20},{20... | collective-permute-start | bytes 1769480 | tf_op jit(solution)/shard_map/ppermute | solution.py:18
  236.8 20.1 %all-to-all-start.2 = ((bf16[4,80,768]{2,1,0:T(8,128)(2,1)}), bf16[4,80,768]{2,1,0:T(8,128)(2,1)}, u32[]{:S(2)}, u32[]{:S(2)}) async-start(bf16[4,80,768]{2,1,0:T(8,128)(2,1)} %bitcast.199), calls=%async_computation.2 | async-start | bytes 983040 | tf_op jit(solution)/shard_map/all_to_all | solution.py:1016
  256.9 29.7 %all-to-all-start.3 = ((bf16[4,80,896]{2,1,0:T(8,128)(2,1)}), bf16[4,80,896]{2,1,0:T(8,128)(2,1)}, u32[]{:S(2)}, u32[]{:S(2)}) async-start(bf16[4,80,896]{2,1,0:T(8,128)(2,1)} %bitcast.198), calls=%async_computation.3 | async-start | bytes 1146880 | tf_op jit(solution)/shard_map/all_to_all | solution.py:1016
  262.0 311.5 %reduce-scatter.5.cloned.1.call-start = ((), (), s32[]{:S(2)}) async-start(), calls=%async_computation.16 | async-start | bytes 5898240 | tf_op jit(solution)/shard_map/reduce_scatter | solution.py:1174
  305.8 267.7 %reduce-scatter.7.cloned.1.call-start = ((), (), s32[]{:S(2)}) async-start(), calls=%async_computation.17 | async-start | bytes 5898240 | tf_op jit(solution)/shard_map/reduce_scatter | solution.py:1174
  306.4 20.3 %all-to-all-start.4 = ((bf16[4,80,896]{2,1,0:T(8,128)(2,1)}), bf16[4,80,896]{2,1,0:T(8,128)(2,1)}, u32[]{:S(2)}, u32[]{:S(2)}) async-start(bf16[4,80,896]{2,1,0:T(8,128)(2,1)} %bitcast.180), calls=%async_computation.4 | async-start | bytes 1146880 | tf_op jit(solution)/shard_map/all_to_all | solution.py:1016
  339.2 33.1 %all-to-all-start.6 = ((bf16[4,80,768]{2,1,0:T(8,128)(2,1)}), bf16[4,80,768]{2,1,0:T(8,128)(2,1)}, u32[]{:S(2)}, u32[]{:S(2)}) async-start(bf16[4,80,768]{2,1,0:T(8,128)(2,1)} %bitcast.181), calls=%async_computation.6 | async-start | bytes 983040 | tf_op jit(solution)/shard_map/all_to_all | solution.py:1016
  353.5 16.4 %collective-permute-start.33 = (bf16[256,768]{1,0:T(8,128)(2,1)S(1)}, bf16[256,768]{1,0:T(8,128)(2,1)S(1)}, u32[]{:S(2)}, u32[]{:S(2)}) collective-permute-start(bf16[256,768]{1,0:T(8,128)(2,1)S(1)} %get-tuple-element.153), channel_id=1, source_target_pairs={{8,0},{12,4},{9,1},{13,5},{10,2},{14,6},{11,3},{15,7},{24,16},{28,... | collective-permute-start | bytes 1179656 | tf_op jit(solution)/shard_map/ppermute | solution.py:24
  376.4 26.7 %collective-permute-start.35 = (f32[256,768]{1,0:T(8,128)}, f32[256,768]{1,0:T(8,128)}, u32[]{:S(2)}, u32[]{:S(2)}) collective-permute-start(f32[256,768]{1,0:T(8,128)} %fusion), channel_id=1, source_target_pairs={{0,16},{16,0},{1,17},{17,1},{2,18},{18,2},{3,19},{19,3},{4,20},{20... | collective-permute-start | bytes 2359304 | tf_op jit(solution)/shard_map/ppermute | solution.py:18
  384.5 20.9 %all-to-all-start.5 = ((bf16[4,80,768]{2,1,0:T(8,128)(2,1)}), bf16[4,80,768]{2,1,0:T(8,128)(2,1)S(1)}, u32[]{:S(2)}, u32[]{:S(2)}) async-start(bf16[4,80,768]{2,1,0:T(8,128)(2,1)} %bitcast.182), calls=%async_computation.5 | async-start | bytes 983040 | tf_op jit(solution)/shard_map/all_to_all | solution.py:1016
  389.1 184.4 %reduce-scatter.9.cloned.1.call-start = ((), (), s32[]{:S(2)}) async-start(), calls=%async_computation.18 | async-start | bytes 5898240 | tf_op jit(solution)/shard_map/reduce_scatter | solution.py:1174
  425.0 148.6 %reduce-scatter.11.cloned.1.call-start = ((), (), s32[]{:S(2)}) async-start(), calls=%async_computation.19 | async-start | bytes 5898240 | tf_op jit(solution)/shard_map/reduce_scatter | solution.py:1174
  426.3 20.6 %all-to-all-start.7 = ((bf16[4,80,768]{2,1,0:T(8,128)(2,1)}), bf16[4,80,768]{2,1,0:T(8,128)(2,1)}, u32[]{:S(2)}, u32[]{:S(2)}) async-start(bf16[4,80,768]{2,1,0:T(8,128)(2,1)} %bitcast.57), calls=%async_computation.7 | async-start | bytes 983040 | tf_op jit(solution)/shard_map/all_to_all | solution.py:1016
  431.2 13.7 %collective-permute-start.37 = (bf16[192,768]{1,0:T(8,128)(2,1)}, bf16[192,768]{1,0:T(8,128)(2,1)S(1)}, u32[]{:S(2)}, u32[]{:S(2)}) collective-permute-start(bf16[192,768]{1,0:T(8,128)(2,1)} %get-tuple-element.168), channel_id=1, source_target_pairs={{0,8},{4,12},{8,0},{12,4},{1,9},{5,13},{9,1},{13,5},{2,10},{6,14},... | collective-permute-start | bytes 884744 | tf_op jit(solution)/shard_map/ppermute | solution.py:28
  465.3 30.4 %collective-permute-start.43 = (bf16[256,768]{1,0:T(8,128)(2,1)S(1)}, bf16[256,768]{1,0:T(8,128)(2,1)S(1)}, u32[]{:S(2)}, u32[]{:S(2)}) collective-permute-start(bf16[256,768]{1,0:T(8,128)(2,1)S(1)} %get-tuple-element.189), channel_id=1, source_target_pairs={{8,0},{12,4},{9,1},{13,5},{10,2},{14,6},{11,3},{15,7},{24,16},{28,... | collective-permute-start | bytes 1179656 | tf_op jit(solution)/shard_map/ppermute | solution.py:24
  466.9 17.1 %collective-permute-start.40 = (bf16[4,48,896]{2,1,0:T(8,128)(2,1)S(1)}, bf16[4,48,896]{2,1,0:T(8,128)(2,1)S(1)}, u32[]{:S(2)}, u32[]{:S(2)}) collective-permute-start(bf16[4,48,896]{2,1,0:T(8,128)(2,1)S(1)} %copy-done.138), channel_id=1, source_target_pairs={{0,1},{1,0},{2,3},{3,2},{4,5},{5,4},{6,7},{7,6},{8,9},{9,8},{10,11... | collective-permute-start | bytes 1032200 | tf_op jit(solution)/shard_map/ppermute | solution.py:28
  469.0 26.6 %collective-permute-start.41 = (bf16[4,48,896]{2,1,0:T(8,128)(2,1)S(1)}, bf16[4,48,896]{2,1,0:T(8,128)(2,1)S(1)}, u32[]{:S(2)}, u32[]{:S(2)}) collective-permute-start(bf16[4,48,896]{2,1,0:T(8,128)(2,1)S(1)} %copy-done.136), channel_id=1, source_target_pairs={{0,2},{1,3},{2,0},{3,1},{4,6},{5,7},{6,4},{7,5},{8,10},{9,11},{10,... | collective-permute-start | bytes 1032200 | tf_op jit(solution)/shard_map/ppermute | solution.py:28
  471.3 24.3 %collective-permute-start.42 = (bf16[4,48,896]{2,1,0:T(8,128)(2,1)S(1)}, bf16[4,48,896]{2,1,0:T(8,128)(2,1)S(1)}, u32[]{:S(2)}, u32[]{:S(2)}) collective-permute-start(bf16[4,48,896]{2,1,0:T(8,128)(2,1)S(1)} %copy-done.134), channel_id=1, source_target_pairs={{0,3},{1,2},{2,1},{3,0},{4,7},{5,6},{6,5},{7,4},{8,11},{9,10},{10,... | collective-permute-start | bytes 1032200 | tf_op jit(solution)/shard_map/ppermute | solution.py:28
  497.1 13.0 %collective-permute-start.44 = (f32[256,768]{1,0:T(8,128)S(1)}, f32[256,768]{1,0:T(8,128)S(1)}, u32[]{:S(2)}, u32[]{:S(2)}) collective-permute-start(f32[256,768]{1,0:T(8,128)S(1)} %get-tuple-element.190.mine_ref), channel_id=1, source_target_pairs={{0,16},{16,0},{1,17},{17,1},{2,18},{18,2},{3,19},{19,3},{4,20},{20... | collective-permute-start | bytes 2359304 | tf_op jit(solution)/shard_map/ppermute | solution.py:18
  514.3 49.3 %collective-permute-start.62 = (bf16[48,896]{1,0:T(8,128)(2,1)S(1)}, bf16[48,896]{1,0:T(8,128)(2,1)S(1)}, u32[]{:S(2)}, u32[]{:S(2)}) collective-permute-start(bf16[48,896]{1,0:T(8,128)(2,1)S(1)} %get-tuple-element.314), channel_id=1, source_target_pairs={{0,8},{4,12},{8,0},{12,4},{1,9},{5,13},{9,1},{13,5},{2,10},{6,14},... | collective-permute-start | bytes 258056 | tf_op jit(solution)/shard_map/ppermute | solution.py:28
  518.4 12.1 %collective-permute-start.63 = (bf16[48,896]{1,0:T(8,128)(2,1)S(1)}, bf16[48,896]{1,0:T(8,128)(2,1)S(1)}, u32[]{:S(2)}, u32[]{:S(2)}) collective-permute-start(bf16[48,896]{1,0:T(8,128)(2,1)S(1)} %get-tuple-element.315), channel_id=1, source_target_pairs={{0,8},{4,12},{8,0},{12,4},{1,9},{5,13},{9,1},{13,5},{2,10},{6,14},... | collective-permute-start | bytes 258056 | tf_op jit(solution)/shard_map/ppermute | solution.py:28
  518.5 21.5 %collective-permute-start.52 = (bf16[4,48,896]{2,1,0:T(8,128)(2,1)S(1)}, bf16[4,48,896]{2,1,0:T(8,128)(2,1)S(1)}, u32[]{:S(2)}, u32[]{:S(2)}) collective-permute-start(bf16[4,48,896]{2,1,0:T(8,128)(2,1)S(1)} %get-tuple-element.203), channel_id=1, source_target_pairs={{0,1},{1,0},{2,3},{3,2},{4,5},{5,4},{6,7},{7,6},{8,9},{9,8},{10,11... | collective-permute-start | bytes 1032200 | tf_op jit(solution)/shard_map/ppermute | solution.py:28
  526.2 26.6 %collective-permute-start.53 = (bf16[4,48,896]{2,1,0:T(8,128)(2,1)S(1)}, bf16[4,48,896]{2,1,0:T(8,128)(2,1)S(1)}, u32[]{:S(2)}, u32[]{:S(2)}) collective-permute-start(bf16[4,48,896]{2,1,0:T(8,128)(2,1)S(1)} %get-tuple-element.204), channel_id=1, source_target_pairs={{0,2},{1,3},{2,0},{3,1},{4,6},{5,7},{6,4},{7,5},{8,10},{9,11},{10,... | collective-permute-start | bytes 1032200 | tf_op jit(solution)/shard_map/ppermute | solution.py:28
  527.0 27.4 %collective-permute-start.54 = (bf16[4,48,896]{2,1,0:T(8,128)(2,1)S(1)}, bf16[4,48,896]{2,1,0:T(8,128)(2,1)S(1)}, u32[]{:S(2)}, u32[]{:S(2)}) collective-permute-start(bf16[4,48,896]{2,1,0:T(8,128)(2,1)S(1)} %get-tuple-element.205), channel_id=1, source_target_pairs={{0,3},{1,2},{2,1},{3,0},{4,7},{5,6},{6,5},{7,4},{8,11},{9,10},{10,... | collective-permute-start | bytes 1032200 | tf_op jit(solution)/shard_map/ppermute | solution.py:28
  530.5 38.7 %collective-permute-start.46 = (bf16[192,768]{1,0:T(8,128)(2,1)S(1)}, bf16[192,768]{1,0:T(8,128)(2,1)S(1)}, u32[]{:S(2)}, u32[]{:S(2)}) collective-permute-start(bf16[192,768]{1,0:T(8,128)(2,1)S(1)} %get-tuple-element.199), channel_id=1, source_target_pairs={{0,8},{4,12},{8,0},{12,4},{1,9},{5,13},{9,1},{13,5},{2,10},{6,14},... | collective-permute-start | bytes 884744 | tf_op jit(solution)/shard_map/ppermute | solution.py:28
  540.0 16.6 %collective-permute-start.47 = (bf16[192,768]{1,0:T(8,128)(2,1)S(1)}, bf16[192,768]{1,0:T(8,128)(2,1)S(1)}, u32[]{:S(2)}, u32[]{:S(2)}) collective-permute-start(bf16[192,768]{1,0:T(8,128)(2,1)S(1)} %get-tuple-element.201), channel_id=1, source_target_pairs={{0,8},{4,12},{8,0},{12,4},{1,9},{5,13},{9,1},{13,5},{2,10},{6,14},... | collective-permute-start | bytes 884744 | tf_op jit(solution)/shard_map/ppermute | solution.py:28
  552.8 11.4 %collective-permute-start.64 = (bf16[48,896]{1,0:T(8,128)(2,1)S(1)}, bf16[48,896]{1,0:T(8,128)(2,1)S(1)}, u32[]{:S(2)}, u32[]{:S(2)}) collective-permute-start(bf16[48,896]{1,0:T(8,128)(2,1)S(1)} %fusion.27), channel_id=1, source_target_pairs={{0,4},{4,0},{8,12},{12,8},{1,5},{5,1},{9,13},{13,9},{2,6},{6,2},{1... | collective-permute-start | bytes 258056 | tf_op jit(solution)/shard_map/ppermute | solution.py:28
  556.7 12.5 %collective-permute-start.48 = (bf16[192,768]{1,0:T(8,128)(2,1)S(1)}, bf16[192,768]{1,0:T(8,128)(2,1)S(1)}, u32[]{:S(2)}, u32[]{:S(2)}) collective-permute-start(bf16[192,768]{1,0:T(8,128)(2,1)S(1)} %add_convert_fusion.4), channel_id=1, source_target_pairs={{0,4},{4,0},{8,12},{12,8},{1,5},{5,1},{9,13},{13,9},{2,6},{6,2},{1... | collective-permute-start | bytes 884744 | tf_op jit(solution)/shard_map/ppermute | solution.py:28
  578.9 13.6 %collective-permute-start.65 = (bf16[192,3072]{1,0:T(8,128)(2,1)S(1)}, bf16[192,3072]{1,0:T(8,128)(2,1)S(1)}, u32[]{:S(2)}, u32[]{:S(2)}) collective-permute-start(bf16[192,3072]{1,0:T(8,128)(2,1)S(1)} %get-tuple-element.216), channel_id=1, source_target_pairs={{0,16},{16,0},{1,17},{17,1},{2,18},{18,2},{3,19},{19,3},{4,20},{20... | collective-permute-start | bytes 3538952 | tf_op jit(solution)/shard_map/ppermute | solution.py:18
  578.9 14.5 %collective-permute-start.66 = (bf16[768,768]{1,0:T(8,128)(2,1)S(1)}, bf16[768,768]{1,0:T(8,128)(2,1)S(1)}, u32[]{:S(2)}, u32[]{:S(2)}) collective-permute-start(bf16[768,768]{1,0:T(8,128)(2,1)S(1)} %get-tuple-element.217), channel_id=1, source_target_pairs={{0,16},{16,0},{1,17},{17,1},{2,18},{18,2},{3,19},{19,3},{4,20},{20... | collective-permute-start | bytes 3538952 | tf_op jit(solution)/shard_map/ppermute | solution.py:18
  (229 other events, 1507.8 us)
Sparse Core Ops, SparseCore 0:
  20.4 79.8 all-gather.4
  102.2 60.7 all-gather.6
  164.8 61.2 all-gather.10
  228.4 58.1 all-gather.8
  305.9 60.2 reduce-scatter.4
  369.6 56.8 reduce-scatter.6
  429.5 63.0 reduce-scatter.8
  495.6 68.9 reduce-scatter.10
